TPU v7x, 32 devices: a whole 2x2x4 slice. The times are simulated.
32 devices in a mesh: groups: 2 (over y), lon: 4 (over z), lat: 2 (over x), head: 2 (over core).
Axes of the slice: x: 2, y: 2, z: 4, core: 2. Of those that a mesh axis runs over, the one named last changes fastest.
Arguments:
- queries: bfloat16 [4, 4, 128, 1536], P(('groups', 'lat'), 'lon', None, 'head'), parts along dimension 0, may hold values from -12 to 12
- key_tokens: bfloat16 [4, 4, 128, 1536], P(('groups', 'lat'), 'lon', None, 'head'), parts along dimension 0, may hold values from -4 to 4
- value_tokens: bfloat16 [4, 4, 128, 1536], P(('groups', 'lat'), 'lon', None, 'head'), parts along dimension 0, may hold values from -6 to 6
- out_grad: bfloat16 [4, 4, 128, 1536], P(('groups', 'lat'), 'lon', None, 'head'), parts along dimension 0, may hold values from -6 to 6
- counts: int32 [4, 4], P('groups'), parts along dimension 0, may hold values from 16 to 128, as said below
Outputs:
- attended: bfloat16 [4, 4, 128, 1536], P(('groups', 'lat'), 'lon', None, 'head'), parts along dimension 0
- query_grad: bfloat16 [4, 4, 128, 1536], P(('groups', 'lat'), 'lon', None, 'head'), parts along dimension 0
- key_grad: bfloat16 [4, 4, 128, 1536], P(('groups', 'lat'), 'lon', None, 'head'), parts along dimension 0
- value_grad: bfloat16 [4, 4, 128, 1536], P(('groups', 'lat'), 'lon', None, 'head'), parts along dimension 0
There are 2 independent parts, one for each index of `groups`. A program takes and returns all parts, laid end to end along the dimension named above; each array names one. Nothing has to cross between parts.
Inputs may be any that keep to these rules, and one draw needn't show every extreme that they name: `counts`: every row of tiles holds a tile of 128 valid tokens; tiles of the first and last rows hold at least 16 valid tokens, the others at least 64.
All inputs are finite; a program needn't handle non-finite values.
Results may differ from a plain program's by a relative error of at most 0.012.
The roundings to bfloat16 on the way count: a program that leaves them out, or rounds other values in their place, can miss the bound.
Values may be sent and summed in bfloat16 or wider, within the bound.
No kernel may reach another device: no remote copies, remote signals or barrier semaphores. Data moves between devices by JAX's collectives and lax.ppermute only.
A program may use at most 64 MiB of HBM per device.

v0:
```python
import math

import jax
import jax.numpy as jnp
from jax import lax
from jax.sharding import PartitionSpec as P

HD = 128


def with_halo(cells, sides, width, closed):
    for axis, dim in sides:
        count = lax.axis_size(axis)
        ends = count if closed else count - 1
        head = lax.slice_in_dim(cells, 0, width, axis=dim)
        tail = lax.slice_in_dim(cells, cells.shape[dim] - width, cells.shape[dim], axis=dim)
        cells = jnp.concatenate(
            [
                lax.ppermute(tail, axis, [(i, (i + 1) % count) for i in range(ends)]),
                cells,
                lax.ppermute(head, axis, [((i + 1) % count, i) for i in range(ends)]),
            ],
            axis=dim,
        )
    return cells


def passed_along(block, axis, distance):
    devices = range(lax.axis_size(axis))
    route = [((i - distance) % len(devices), i) for i in devices]
    return lax.ppermute(block, axis, route)


def neighbour_tiles(row_at, col_at, lat_tiles, lon_tiles):
    row_step = jnp.array([-1, -1, -1, 0, 0, 0, 1, 1, 1], dtype=jnp.int32)
    col_step = jnp.array([-1, 0, 1, -1, 0, 1, -1, 0, 1], dtype=jnp.int32)
    row_next = row_at + row_step
    across = (row_next < 0) | (row_next > lat_tiles - 1)
    col_next = (col_at + col_step + jnp.where(across, lon_tiles // 2, 0)) % lon_tiles
    row_next = jnp.clip(row_next, 0, lat_tiles - 1)
    return row_next * lon_tiles + col_next


def close_poles(rim_block, mirror):
    lat_index = lax.axis_index("lat")
    last_index = lax.axis_size("lat") - 1
    north_rim = jnp.where(lat_index == 0, mirror, rim_block[:1])
    south_rim = jnp.where(lat_index == last_index, mirror, rim_block[-1:])
    return jnp.concatenate([north_rim, rim_block[1:-1], south_rim], 0)


def around_pair(first_block, second_block):
    row_faces = (
        with_halo(first_block, (("lat", 0),), 1, False),
        with_halo(second_block, (("lat", 0),), 1, False),
    )
    mirror = passed_along((first_block, second_block), "lon", lax.axis_size("lon") // 2)
    column_a = close_poles(row_faces[0], mirror[0])
    column_b = close_poles(row_faces[1], mirror[1])
    return (
        with_halo(column_a, (("lon", 1),), 1, True),
        with_halo(column_b, (("lon", 1),), 1, True),
    )


def around_stats(log_total, out_dot):
    near_stats = (
        with_halo(log_total, (("lon", 1), ("lat", 0)), 1, True),
        with_halo(out_dot, (("lon", 1), ("lat", 0)), 1, True),
    )
    own_rows = log_total.shape[0]
    own_total = near_stats[0][1 : own_rows + 1]
    own_dot = near_stats[1][1 : own_rows + 1]
    mirror = passed_along((own_total, own_dot), "lon", lax.axis_size("lon") // 2)
    return (close_poles(near_stats[0], mirror[0]), close_poles(near_stats[1], mirror[1]))


def on_device(queries, key_tokens, value_tokens, out_grad, counts):
    own_rows = queries.shape[0]
    tile_len = queries.shape[2]
    feat_width = queries.shape[3]
    head_count = feat_width // HD
    lat_tiles = counts.shape[0]
    lon_tiles = counts.shape[1]
    row_base = lax.axis_index("lat") * own_rows
    col_at = lax.axis_index("lon")
    score_scale = 1.0 / math.sqrt(HD)
    positions = jnp.arange(tile_len, dtype=jnp.int32)
    flat_counts = counts.reshape(-1)
    near_k, near_v = around_pair(key_tokens, value_tokens)
    attended_rows, query_rows, total_rows, dot_rows = ([], [], [], [])
    row_local = 0
    slot_ids = neighbour_tiles(row_base + row_local, col_at, lat_tiles, lon_tiles)
    key_valid = (positions[None, :] < flat_counts[slot_ids][:, None]).reshape(-1)
    near_keys = near_k.reshape(9 * tile_len, feat_width)
    near_values = near_v.reshape(9 * tile_len, feat_width)
    head_outs = []
    query_parts = []
    head_totals = []
    head_dots = []
    for head_index in range(head_count):
        columns = slice(head_index * HD, (head_index + 1) * HD)
        query_here = queries[row_local, 0, :, columns]
        grad_here = out_grad[row_local, 0, :, columns]
        keys_head = near_keys[:, columns]
        values_head = near_values[:, columns]
        scores = (
            jnp.einsum("qd,kd->qk", query_here, keys_head, preferred_element_type=jnp.float32)
            * score_scale
        )
        row_max = jnp.max(jnp.where(key_valid[None, :], scores, -1e30), axis=-1, keepdims=True)
        row_total = jnp.sum(
            jnp.where(key_valid[None, :], jnp.exp(scores - row_max), 0.0), axis=-1, keepdims=True
        )
        log_total = row_max + jnp.log(row_total)
        weights = jnp.where(key_valid[None, :], jnp.exp(scores - log_total), 0.0)
        weights_low = weights.astype(jnp.bfloat16)
        head_out = jnp.dot(weights_low, values_head, preferred_element_type=jnp.float32).astype(
            jnp.bfloat16
        )
        out_dot = jnp.sum(grad_here.astype(jnp.float32) * head_out.astype(jnp.float32), axis=-1)
        grad_weights = jnp.einsum(
            "qd,kd->qk", grad_here, values_head, preferred_element_type=jnp.float32
        )
        grad_scores = (weights * (grad_weights - out_dot[:, None])).astype(jnp.bfloat16)
        query_part = (
            jnp.dot(grad_scores, keys_head, preferred_element_type=jnp.float32) * score_scale
        )
        head_outs.append(head_out)
        query_parts.append(query_part.astype(jnp.bfloat16))
        head_totals.append(log_total[:, 0])
        head_dots.append(out_dot)
    attended_rows.append(jnp.concatenate(head_outs, -1))
    query_rows.append(jnp.concatenate(query_parts, -1))
    total_rows.append(jnp.stack(head_totals))
    dot_rows.append(jnp.stack(head_dots))
    attended = jnp.stack(attended_rows)[:, None]
    query_grad = jnp.stack(query_rows)[:, None]
    own_totals = jnp.stack(total_rows)[:, None]
    own_dots = jnp.stack(dot_rows)[:, None]
    near_q, near_g = around_pair(queries, out_grad)
    near_total, near_dot = around_stats(own_totals, own_dots)
    key_rows, value_rows = ([], [])
    row_local = 0
    own_valid = positions < counts[row_base + row_local, col_at]
    near_queries = near_q.reshape(9 * tile_len, feat_width)
    near_grads = near_g.reshape(9 * tile_len, feat_width)
    key_parts = []
    value_parts = []
    for head_index in range(head_count):
        columns = slice(head_index * HD, (head_index + 1) * HD)
        queries_head = near_queries[:, columns]
        grads_head = near_grads[:, columns]
        keys_here = key_tokens[row_local, 0, :, columns]
        values_here = value_tokens[row_local, 0, :, columns]
        totals_head = near_total[:, :, head_index, :].reshape(9 * tile_len)
        dots_head = near_dot[:, :, head_index, :].reshape(9 * tile_len)
        scores = (
            jnp.einsum("qd,kd->qk", queries_head, keys_here, preferred_element_type=jnp.float32)
            * score_scale
        )
        weights = jnp.where(own_valid[None, :], jnp.exp(scores - totals_head[:, None]), 0.0)
        weights_low = weights.astype(jnp.bfloat16)
        value_part = jnp.einsum(
            "qk,qd->kd", weights_low, grads_head, preferred_element_type=jnp.float32
        )
        grad_weights = jnp.einsum(
            "qd,kd->qk", grads_head, values_here, preferred_element_type=jnp.float32
        )
        grad_scores = (weights * (grad_weights - dots_head[:, None])).astype(jnp.bfloat16)
        key_part = (
            jnp.einsum("qk,qd->kd", grad_scores, queries_head, preferred_element_type=jnp.float32)
            * score_scale
        )
        key_parts.append(key_part.astype(jnp.bfloat16))
        value_parts.append(value_part.astype(jnp.bfloat16))
    key_rows.append(jnp.concatenate(key_parts, -1))
    value_rows.append(jnp.concatenate(value_parts, -1))
    key_grad = jnp.stack(key_rows)[:, None]
    value_grad = jnp.stack(value_rows)[:, None]
    return (attended, query_grad, key_grad, value_grad)


def solution(mesh):
    placed = (
        P(("groups", "lat"), "lon", None, "head"),
        P(("groups", "lat"), "lon", None, "head"),
        P(("groups", "lat"), "lon", None, "head"),
        P(("groups", "lat"), "lon", None, "head"),
        P("groups", None),
    )
    return jax.shard_map(
        on_device,
        mesh=mesh,
        in_specs=placed,
        out_specs=(
            P(("groups", "lat"), "lon", None, "head"),
            P(("groups", "lat"), "lon", None, "head"),
            P(("groups", "lat"), "lon", None, "head"),
            P(("groups", "lat"), "lon", None, "head"),
        ),
        check_vma=False,
    )
```

profile of v0, /device:TPU:0, one launch (start us, length us, event | category | flops | bytes accessed | tf_op | source)
XLA Modules:
  0.0 219.1 jit_solution(3975038279234772611)
XLA Ops:
  0.7 4.1 %collective-permute-start.5 = (bf16[1,1,128,768]{3,2,1,0:T(8,128)(2,1)}, bf16[1,1,128,768]{3,2,1,0:T(8,128)(2,1)S(1)}, u32[]{:S(2)}, u32[]{:S(2)}) collective-permute-start(bf16[1,1,128,768]{3,2,1,0:T(8,128)(2,1)} %param.9), channel_id=1, source_target_pairs={{8,0},{12,4},{0,8},{4,12},{9,1},{13,5},{1,9},{5,13},{10,2},{14,6},... | collective-permute-start | bytes 589832 | tf_op jit(solution)/shard_map/ppermute | solution.py:31
  4.8 3.4 %collective-permute-start.6 = (bf16[1,1,128,768]{3,2,1,0:T(8,128)(2,1)}, bf16[1,1,128,768]{3,2,1,0:T(8,128)(2,1)S(1)}, u32[]{:S(2)}, u32[]{:S(2)}) collective-permute-start(bf16[1,1,128,768]{3,2,1,0:T(8,128)(2,1)} %param.9), channel_id=1, source_target_pairs={{0,2},{1,3},{4,6},{5,7},{8,10},{9,11},{12,14},{13,15},{16,18},{17,... | collective-permute-start | bytes 589832 | tf_op jit(solution)/shard_map/ppermute | solution.py:19
  8.2 1.3 collective-permute-start.7
  20.9 4.6 %collective-permute-start.1 = (bf16[1,1,128,768]{3,2,1,0:T(8,128)(2,1)}, bf16[1,1,128,768]{3,2,1,0:T(8,128)(2,1)S(1)}, u32[]{:S(2)}, u32[]{:S(2)}) collective-permute-start(bf16[1,1,128,768]{3,2,1,0:T(8,128)(2,1)} %param.8), channel_id=1, source_target_pairs={{0,2},{1,3},{4,6},{5,7},{8,10},{9,11},{12,14},{13,15},{16,18},{17,... | collective-permute-start | bytes 589832 | tf_op jit(solution)/shard_map/ppermute | solution.py:19
  25.6 2.7 %collective-permute-start.20 = (bf16[1,1,128,768]{3,2,1,0:T(8,128)(2,1)}, bf16[1,1,128,768]{3,2,1,0:T(8,128)(2,1)S(1)}, u32[]{:S(2)}, u32[]{:S(2)}) collective-permute-start(bf16[1,1,128,768]{3,2,1,0:T(8,128)(2,1)} %param.10), channel_id=1, source_target_pairs={{8,0},{12,4},{0,8},{4,12},{9,1},{13,5},{1,9},{5,13},{10,2},{14,6},... | collective-permute-start | bytes 589832 | tf_op jit(solution)/shard_map/ppermute | solution.py:31
  28.2 1.3 collective-permute-start.21
  29.5 1.3 collective-permute-start.22
  32.6 9.1 %collective-permute-done.20 = bf16[1,1,128,768]{3,2,1,0:T(8,128)(2,1)S(1)} collective-permute-done((bf16[1,1,128,768]{3,2,1,0:T(8,128)(2,1)}, bf16[1,1,128,768]{3,2,1,0:T(8,128)(2,1)S(1)}, u32[]{:S(2)}, u32[]{:S(2)}) %collective-permute-start.20) | collective-permute-done | bytes 196640 | tf_op jit(solution)/shard_map/ppermute | solution.py:31
  41.7 1.3 collective-permute-start.11
  43.1 2.7 %collective-permute-start.4 = (bf16[3,1,128,768]{3,2,1,0:T(8,128)(2,1)S(1)}, bf16[3,1,128,768]{3,2,1,0:T(8,128)(2,1)S(1)}, u32[]{:S(2)}, u32[]{:S(2)}) collective-permute-start(bf16[3,1,128,768]{3,2,1,0:T(8,128)(2,1)S(1)} %pad_maximum_fusion.4), channel_id=1, source_target_pairs={{4,0},{8,4},{12,8},{0,12},{5,1},{9,5},{13,9},{1,13},{6,2},{10,6},{... | collective-permute-start | bytes 1769480 | tf_op jit(solution)/shard_map/ppermute | solution.py:21
  46.0 3.9 %collective-permute-start.9 = (bf16[3,1,128,768]{3,2,1,0:T(8,128)(2,1)S(1)}, bf16[3,1,128,768]{3,2,1,0:T(8,128)(2,1)S(1)}, u32[]{:S(2)}, u32[]{:S(2)}) collective-permute-start(bf16[3,1,128,768]{3,2,1,0:T(8,128)(2,1)S(1)} %pad_maximum_fusion.5), channel_id=1, source_target_pairs={{4,0},{8,4},{12,8},{0,12},{5,1},{9,5},{13,9},{1,13},{6,2},{10,6},{... | collective-permute-start | bytes 1769480 | tf_op jit(solution)/shard_map/ppermute | solution.py:21
  51.0 3.8 %collective-permute-start.14 = (bf16[3,1,128,768]{3,2,1,0:T(8,128)(2,1)}, bf16[3,1,128,768]{3,2,1,0:T(8,128)(2,1)}, u32[]{:S(2)}, u32[]{:S(2)}) collective-permute-start(bf16[3,1,128,768]{3,2,1,0:T(8,128)(2,1)} %pad_maximum_fusion.6), channel_id=1, source_target_pairs={{4,0},{8,4},{12,8},{0,12},{5,1},{9,5},{13,9},{1,13},{6,2},{10,6},{... | collective-permute-start | bytes 1769480 | tf_op jit(solution)/shard_map/ppermute | solution.py:21
  55.7 15.7 %collective-permute-done.4 = bf16[3,1,128,768]{3,2,1,0:T(8,128)(2,1)S(1)} collective-permute-done((bf16[3,1,128,768]{3,2,1,0:T(8,128)(2,1)S(1)}, bf16[3,1,128,768]{3,2,1,0:T(8,128)(2,1)S(1)}, u32[]{:S(2)}, u32[]{:S(2)}) %collective-permute-start.4) | collective-permute-done | bytes 589856 | tf_op jit(solution)/shard_map/ppermute | solution.py:21
  71.4 1.3 collective-permute-done.3
  72.8 3.5 %collective-permute-start.24 = (bf16[3,1,128,768]{3,2,1,0:T(8,128)(2,1)}, bf16[3,1,128,768]{3,2,1,0:T(8,128)(2,1)}, u32[]{:S(2)}, u32[]{:S(2)}) collective-permute-start(bf16[3,1,128,768]{3,2,1,0:T(8,128)(2,1)} %pad_maximum_fusion.7), channel_id=1, source_target_pairs={{4,0},{8,4},{12,8},{0,12},{5,1},{9,5},{13,9},{1,13},{6,2},{10,6},{... | collective-permute-start | bytes 1769480 | tf_op jit(solution)/shard_map/ppermute | solution.py:21
  81.5 15.2 %collective-permute-done.9 = bf16[3,1,128,768]{3,2,1,0:T(8,128)(2,1)S(1)} collective-permute-done((bf16[3,1,128,768]{3,2,1,0:T(8,128)(2,1)S(1)}, bf16[3,1,128,768]{3,2,1,0:T(8,128)(2,1)S(1)}, u32[]{:S(2)}, u32[]{:S(2)}) %collective-permute-start.9) | collective-permute-done | bytes 589856 | tf_op jit(solution)/shard_map/ppermute | solution.py:21
  96.7 1.4 collective-permute-done.8
  100.7 2.1 fusion.89
  102.7 2.4 %constant_dynamic-update-slice_fusion.4 = (bf16[128,768]{0,1:T(8,128)(2,1)}, bf16[128,128]{0,1:T(8,128)(2,1)}) fusion(bf16[128,768]{0,1:T(8,128)(2,1)} %get-tuple-element.56, bf16[1152,768]{1,0:T(8,128)(2,1)} %bitcast.163, f32[1152,128]{1,0:T(8,128)} %copy-done.5, f32[128]{0:T(128)} %log_add_fusion.4, pred[1152]{0:T(1024)(128)(4,1)S(1)} %fusion.282), kind=kOutput, calls=%fused_computation.285 | convolution fusion | flops 38207488 | bytes 951936 | tf_op jit(solution)/shard_map/dot_general | solution.py:118
  105.1 2.3 %constant_dynamic-update-slice_fusion.3 = (bf16[128,768]{0,1:T(8,128)(2,1)}, bf16[128,128]{0,1:T(8,128)(2,1)}) fusion(bf16[128,768]{0,1:T(8,128)(2,1)} %get-tuple-element.58, bf16[1152,768]{1,0:T(8,128)(2,1)} %bitcast.164, f32[1152,128]{1,0:T(8,128)} %copy-done, f32[128]{0:T(128)} %log_add_fusion.3, pred[1152]{0:T(1024)(128)(4,1)S(1)} %fusion.282), kind=kOutput, calls=%fused_computation.284 | convolution fusion | flops 38207488 | bytes 951936 | tf_op jit(solution)/shard_map/dot_general | solution.py:118
  111.4 3.4 %collective-permute-start.16 = (f32[1,1,6,128]{3,2,1,0:T(8,128)S(1)}, f32[1,1,6,128]{3,2,1,0:T(8,128)S(1)}, u32[]{:S(2)}, u32[]{:S(2)}) collective-permute-start(f32[1,1,6,128]{3,2,1,0:T(8,128)S(1)} %bitcast.177), channel_id=1, source_target_pairs={{4,0},{8,4},{12,8},{0,12},{5,1},{9,5},{13,9},{1,13},{6,2},{10,6},{... | collective-permute-start | bytes 9224 | tf_op jit(solution)/shard_map/ppermute | solution.py:21
  115.6 2.3 %fusion.87 = bf16[128,768]{0,1:T(8,128)(2,1)} fusion(bf16[128,768]{0,1:T(8,128)(2,1)} %fusion.89, f32[1152,128]{1,0:T(8,128)} %copy-done.5, f32[128]{0:T(128)S(1)} %multiply_reduce_fusion.4, f32[128]{0:T(128)} %log_add_fusion.4, pred[1152]{0:T(1024)(128)(4,1)S(1)} %fusion.282, bf16[1152,768]{1,0:T(8,128)(2,1)} %bitcast.165, ...), kind=kOutput, calls=%fused_computation.116 | convolution fusion | flops 76267520 | bytes 1248256 | tf_op jit(solution)/shard_map/dot_general | solution.py:127
  117.9 1.3 multiply_reduce_fusion.3
  119.2 1.4 multiply_reduce_fusion.2
  120.6 1.3 multiply_reduce_fusion.1
  121.9 1.4 multiply_reduce_fusion
  124.0 2.1 fusion.85
  126.1 2.1 fusion.83
  128.3 3.8 %collective-permute-start.26 = (f32[1,1,6,128]{3,2,1,0:T(8,128)S(1)}, f32[1,1,6,128]{3,2,1,0:T(8,128)S(1)}, u32[]{:S(2)}, u32[]{:S(2)}) collective-permute-start(f32[1,1,6,128]{3,2,1,0:T(8,128)S(1)} %bitcast.182), channel_id=1, source_target_pairs={{4,0},{8,4},{12,8},{0,12},{5,1},{9,5},{13,9},{1,13},{6,2},{10,6},{... | collective-permute-start | bytes 9224 | tf_op jit(solution)/shard_map/ppermute | solution.py:21
  132.1 2.7 %pad_maximum_fusion.2 = bf16[3,3,128,768]{3,2,1,0:T(8,128)(2,1)} fusion(bf16[3,1,128,768]{3,2,1,0:T(8,128)(2,1)} %collective-permute-done.14, bf16[1,1,128,768]{3,2,1,0:T(8,128)(2,1)S(1)} %copy-done.16, bf16[1,1,128,768]{3,2,1,0:T(8,128)(2,1)S(1)} %copy-done.8, bf16[1,1,128,768]{3,2,1,0:T(8,128)(2,1)} %copy-done.17, ...), kind=kLoop, calls=%fused_computation.69 | loop fusion | flops 3538944 | bytes 3538944 | tf_op jit(solution)/shard_map/concatenate | solution.py:17
  134.8 2.2 fusion.81
  137.0 2.1 fusion.79
  139.1 8.6 %collective-permute-done.23 = bf16[3,1,128,768]{3,2,1,0:T(8,128)(2,1)} collective-permute-done((bf16[3,1,128,768]{3,2,1,0:T(8,128)(2,1)}, bf16[3,1,128,768]{3,2,1,0:T(8,128)(2,1)}, u32[]{:S(2)}, u32[]{:S(2)}) %collective-permute-start.23) | collective-permute-done | bytes 589856 | tf_op jit(solution)/shard_map/ppermute | solution.py:19
  147.7 1.4 pad_maximum_fusion.3
  149.2 1.9 copy.27
  151.0 1.7 copy.28
  154.3 2.0 collective-permute-start.19
  157.6 2.1 collective-permute-start.27
  159.8 2.0 collective-permute-start.29
  162.4 1.5 maximum_reduce_fusion.5
  163.9 1.3 sub.336
  166.5 1.5 maximum_reduce_fusion.4
  172.3 2.2 fusion.77
  175.8 1.9 fusion.21
  178.9 1.3 sub.348
  180.2 1.9 fusion.23
  182.1 1.3 sub.351
  183.4 1.5 fusion.284
  185.6 1.9 fusion.25
  187.5 1.5 fusion.283
  189.0 1.3 sub.357
  190.3 1.3 sub.360
  191.6 1.9 fusion.27
  193.5 1.3 sub.363
  195.4 1.9 fusion.29
  197.9 2.2 fusion.75
  200.0 2.2 fusion.73
  202.2 2.2 fusion.71
  204.4 2.2 fusion.69
  206.6 2.2 fusion.67
  208.7 1.8 copy.29
  210.6 2.0 fusion.94
  212.6 2.0 fusion.93
  217.4 1.7 copy.30
  (189 shorter events, 45.0 us)
Async XLA Ops:
  0.6 42.4 %copy-start.21 = (bf16[1,1,128,768]{3,2,1,0:T(8,128)(2,1)S(1)}, bf16[1,1,128,768]{3,2,1,0:T(8,128)(2,1)}, u32[]{:S(2)}) copy-start(bf16[1,1,128,768]{3,2,1,0:T(8,128)(2,1)} %param.8) | copy-start | bytes 589828
  0.6 41.1 %copy-start.6 = (bf16[1,1,128,768]{3,2,1,0:T(8,128)(2,1)S(1)}, bf16[1,1,128,768]{3,2,1,0:T(8,128)(2,1)}, u32[]{:S(2)}) copy-start(bf16[1,1,128,768]{3,2,1,0:T(8,128)(2,1)} %param.7) | copy-start | bytes 589828
  0.7 20.3 %collective-permute-start.5 = (bf16[1,1,128,768]{3,2,1,0:T(8,128)(2,1)}, bf16[1,1,128,768]{3,2,1,0:T(8,128)(2,1)S(1)}, u32[]{:S(2)}, u32[]{:S(2)}) collective-permute-start(bf16[1,1,128,768]{3,2,1,0:T(8,128)(2,1)} %param.9), channel_id=1, source_target_pairs={{8,0},{12,4},{0,8},{4,12},{9,1},{13,5},{1,9},{5,13},{10,2},{14,6},... | collective-permute-start | bytes 589832 | tf_op jit(solution)/shard_map/ppermute | solution.py:31
  4.8 20.8 %collective-permute-start.6 = (bf16[1,1,128,768]{3,2,1,0:T(8,128)(2,1)}, bf16[1,1,128,768]{3,2,1,0:T(8,128)(2,1)S(1)}, u32[]{:S(2)}, u32[]{:S(2)}) collective-permute-start(bf16[1,1,128,768]{3,2,1,0:T(8,128)(2,1)} %param.9), channel_id=1, source_target_pairs={{0,2},{1,3},{4,6},{5,7},{8,10},{9,11},{12,14},{13,15},{16,18},{17,... | collective-permute-start | bytes 589832 | tf_op jit(solution)/shard_map/ppermute | solution.py:19
  8.2 20.1 %collective-permute-start.7 = (bf16[1,1,128,768]{3,2,1,0:T(8,128)(2,1)}, bf16[1,1,128,768]{3,2,1,0:T(8,128)(2,1)S(1)}, u32[]{:S(2)}, u32[]{:S(2)}) collective-permute-start(bf16[1,1,128,768]{3,2,1,0:T(8,128)(2,1)} %param.9), channel_id=1, source_target_pairs={{2,0},{3,1},{6,4},{7,5},{10,8},{11,9},{14,12},{15,13},{18,16},{19,... | collective-permute-start | bytes 589832 | tf_op jit(solution)/shard_map/ppermute | solution.py:21
  9.5 20.1 %collective-permute-start = (bf16[1,1,128,768]{3,2,1,0:T(8,128)(2,1)}, bf16[1,1,128,768]{3,2,1,0:T(8,128)(2,1)S(1)}, u32[]{:S(2)}, u32[]{:S(2)}) collective-permute-start(bf16[1,1,128,768]{3,2,1,0:T(8,128)(2,1)} %param.8), channel_id=1, source_target_pairs={{8,0},{12,4},{0,8},{4,12},{9,1},{13,5},{1,9},{5,13},{10,2},{14,6},... | collective-permute-start | bytes 589832 | tf_op jit(solution)/shard_map/ppermute | solution.py:31
  9.9 21.0 %collective-permute-start.2 = (bf16[1,1,128,768]{3,2,1,0:T(8,128)(2,1)}, bf16[1,1,128,768]{3,2,1,0:T(8,128)(2,1)S(1)}, u32[]{:S(2)}, u32[]{:S(2)}) collective-permute-start(bf16[1,1,128,768]{3,2,1,0:T(8,128)(2,1)} %param.8), channel_id=1, source_target_pairs={{2,0},{3,1},{6,4},{7,5},{10,8},{11,9},{14,12},{15,13},{18,16},{19,... | collective-permute-start | bytes 589832 | tf_op jit(solution)/shard_map/ppermute | solution.py:21
  17.7 28.1 %copy-start.22 = (bf16[1,1,128,768]{3,2,1,0:T(8,128)(2,1)S(1)}, bf16[1,1,128,768]{3,2,1,0:T(8,128)(2,1)}, u32[]{:S(2)}) copy-start(bf16[1,1,128,768]{3,2,1,0:T(8,128)(2,1)} %param.9) | copy-start | bytes 589828
  20.9 10.3 %collective-permute-start.1 = (bf16[1,1,128,768]{3,2,1,0:T(8,128)(2,1)}, bf16[1,1,128,768]{3,2,1,0:T(8,128)(2,1)S(1)}, u32[]{:S(2)}, u32[]{:S(2)}) collective-permute-start(bf16[1,1,128,768]{3,2,1,0:T(8,128)(2,1)} %param.8), channel_id=1, source_target_pairs={{0,2},{1,3},{4,6},{5,7},{8,10},{9,11},{12,14},{13,15},{16,18},{17,... | collective-permute-start | bytes 589832 | tf_op jit(solution)/shard_map/ppermute | solution.py:19
  25.6 100.6 %copy-start.35 = (pred[1152]{0:T(1024)(128)(4,1)}, pred[1152]{0:T(1024)(128)(4,1)S(1)}, u32[]{:S(2)}) copy-start(pred[1152]{0:T(1024)(128)(4,1)S(1)} %fusion.282) | copy-start | bytes 3460
  25.6 16.1 %collective-permute-start.20 = (bf16[1,1,128,768]{3,2,1,0:T(8,128)(2,1)}, bf16[1,1,128,768]{3,2,1,0:T(8,128)(2,1)S(1)}, u32[]{:S(2)}, u32[]{:S(2)}) collective-permute-start(bf16[1,1,128,768]{3,2,1,0:T(8,128)(2,1)} %param.10), channel_id=1, source_target_pairs={{8,0},{12,4},{0,8},{4,12},{9,1},{13,5},{1,9},{5,13},{10,2},{14,6},... | collective-permute-start | bytes 589832 | tf_op jit(solution)/shard_map/ppermute | solution.py:31
  28.2 14.9 %collective-permute-start.21 = (bf16[1,1,128,768]{3,2,1,0:T(8,128)(2,1)}, bf16[1,1,128,768]{3,2,1,0:T(8,128)(2,1)S(1)}, u32[]{:S(2)}, u32[]{:S(2)}) collective-permute-start(bf16[1,1,128,768]{3,2,1,0:T(8,128)(2,1)} %param.10), channel_id=1, source_target_pairs={{0,2},{1,3},{4,6},{5,7},{8,10},{9,11},{12,14},{13,15},{16,18},{17,... | collective-permute-start | bytes 589832 | tf_op jit(solution)/shard_map/ppermute | solution.py:19
  29.5 16.3 %collective-permute-start.22 = (bf16[1,1,128,768]{3,2,1,0:T(8,128)(2,1)}, bf16[1,1,128,768]{3,2,1,0:T(8,128)(2,1)S(1)}, u32[]{:S(2)}, u32[]{:S(2)}) collective-permute-start(bf16[1,1,128,768]{3,2,1,0:T(8,128)(2,1)} %param.10), channel_id=1, source_target_pairs={{2,0},{3,1},{6,4},{7,5},{10,8},{11,9},{14,12},{15,13},{18,16},{19,... | collective-permute-start | bytes 589832 | tf_op jit(solution)/shard_map/ppermute | solution.py:21
  30.9 15.1 %collective-permute-start.10 = (bf16[1,1,128,768]{3,2,1,0:T(8,128)(2,1)}, bf16[1,1,128,768]{3,2,1,0:T(8,128)(2,1)S(1)}, u32[]{:S(2)}, u32[]{:S(2)}) collective-permute-start(bf16[1,1,128,768]{3,2,1,0:T(8,128)(2,1)} %param.7), channel_id=1, source_target_pairs={{8,0},{12,4},{0,8},{4,12},{9,1},{13,5},{1,9},{5,13},{10,2},{14,6},... | collective-permute-start | bytes 589832 | tf_op jit(solution)/shard_map/ppermute | solution.py:31
  31.3 18.6 %collective-permute-start.12 = (bf16[1,1,128,768]{3,2,1,0:T(8,128)(2,1)}, bf16[1,1,128,768]{3,2,1,0:T(8,128)(2,1)S(1)}, u32[]{:S(2)}, u32[]{:S(2)}) collective-permute-start(bf16[1,1,128,768]{3,2,1,0:T(8,128)(2,1)} %param.7), channel_id=1, source_target_pairs={{2,0},{3,1},{6,4},{7,5},{10,8},{11,9},{14,12},{15,13},{18,16},{19,... | collective-permute-start | bytes 589832 | tf_op jit(solution)/shard_map/ppermute | solution.py:21
  41.7 8.1 %collective-permute-start.11 = (bf16[1,1,128,768]{3,2,1,0:T(8,128)(2,1)S(1)}, bf16[1,1,128,768]{3,2,1,0:T(8,128)(2,1)S(1)}, u32[]{:S(2)}, u32[]{:S(2)}) collective-permute-start(bf16[1,1,128,768]{3,2,1,0:T(8,128)(2,1)S(1)} %copy-done.6), channel_id=1, source_target_pairs={{0,2},{1,3},{4,6},{5,7},{8,10},{9,11},{12,14},{13,15},{16,18},{17,... | collective-permute-start | bytes 589832 | tf_op jit(solution)/shard_map/ppermute | solution.py:19
  43.1 28.3 %collective-permute-start.4 = (bf16[3,1,128,768]{3,2,1,0:T(8,128)(2,1)S(1)}, bf16[3,1,128,768]{3,2,1,0:T(8,128)(2,1)S(1)}, u32[]{:S(2)}, u32[]{:S(2)}) collective-permute-start(bf16[3,1,128,768]{3,2,1,0:T(8,128)(2,1)S(1)} %pad_maximum_fusion.4), channel_id=1, source_target_pairs={{4,0},{8,4},{12,8},{0,12},{5,1},{9,5},{13,9},{1,13},{6,2},{10,6},{... | collective-permute-start | bytes 1769480 | tf_op jit(solution)/shard_map/ppermute | solution.py:21
  45.9 26.9 %collective-permute-start.3 = (bf16[3,1,128,768]{3,2,1,0:T(8,128)(2,1)S(1)}, bf16[3,1,128,768]{3,2,1,0:T(8,128)(2,1)S(1)}, u32[]{:S(2)}, u32[]{:S(2)}) collective-permute-start(bf16[3,1,128,768]{3,2,1,0:T(8,128)(2,1)S(1)} %pad_maximum_fusion.4), channel_id=1, source_target_pairs={{0,4},{4,8},{8,12},{12,0},{1,5},{5,9},{9,13},{13,1},{2,6},{6,10},{... | collective-permute-start | bytes 1769480 | tf_op jit(solution)/shard_map/ppermute | solution.py:19
  45.9 8.8 %copy-start.9 = (bf16[1,1,128,768]{3,2,1,0:T(8,128)(2,1)S(1)}, bf16[1,1,128,768]{3,2,1,0:T(8,128)(2,1)}, u32[]{:S(2)}) copy-start(bf16[1,1,128,768]{3,2,1,0:T(8,128)(2,1)} %param.10) | copy-start | bytes 589828
  46.0 50.7 %collective-permute-start.9 = (bf16[3,1,128,768]{3,2,1,0:T(8,128)(2,1)S(1)}, bf16[3,1,128,768]{3,2,1,0:T(8,128)(2,1)S(1)}, u32[]{:S(2)}, u32[]{:S(2)}) collective-permute-start(bf16[3,1,128,768]{3,2,1,0:T(8,128)(2,1)S(1)} %pad_maximum_fusion.5), channel_id=1, source_target_pairs={{4,0},{8,4},{12,8},{0,12},{5,1},{9,5},{13,9},{1,13},{6,2},{10,6},{... | collective-permute-start | bytes 1769480 | tf_op jit(solution)/shard_map/ppermute | solution.py:21
  49.8 48.2 %collective-permute-start.8 = (bf16[3,1,128,768]{3,2,1,0:T(8,128)(2,1)S(1)}, bf16[3,1,128,768]{3,2,1,0:T(8,128)(2,1)S(1)}, u32[]{:S(2)}, u32[]{:S(2)}) collective-permute-start(bf16[3,1,128,768]{3,2,1,0:T(8,128)(2,1)S(1)} %pad_maximum_fusion.5), channel_id=1, source_target_pairs={{0,4},{4,8},{8,12},{12,0},{1,5},{5,9},{9,13},{13,1},{2,6},{6,10},{... | collective-permute-start | bytes 1769480 | tf_op jit(solution)/shard_map/ppermute | solution.py:19
  49.9 22.8 %copy-start.11 = (bf16[1,1,128,768]{3,2,1,0:T(8,128)(2,1)}, bf16[1,1,128,768]{3,2,1,0:T(8,128)(2,1)S(1)}, u32[]{:S(2)}) copy-start(bf16[1,1,128,768]{3,2,1,0:T(8,128)(2,1)S(1)} %get-tuple-element.36) | copy-start | bytes 589828
  49.9 22.8 %copy-start.13 = (bf16[1,1,128,768]{3,2,1,0:T(8,128)(2,1)}, bf16[1,1,128,768]{3,2,1,0:T(8,128)(2,1)S(1)}, u32[]{:S(2)}) copy-start(bf16[1,1,128,768]{3,2,1,0:T(8,128)(2,1)S(1)} %get-tuple-element.37) | copy-start | bytes 589828
  49.9 22.8 %copy-start.15 = (bf16[1,1,128,768]{3,2,1,0:T(8,128)(2,1)}, bf16[1,1,128,768]{3,2,1,0:T(8,128)(2,1)S(1)}, u32[]{:S(2)}) copy-start(bf16[1,1,128,768]{3,2,1,0:T(8,128)(2,1)S(1)} %get-tuple-element.68) | copy-start | bytes 589828
  50.0 22.8 %copy-start.17 = (bf16[1,1,128,768]{3,2,1,0:T(8,128)(2,1)}, bf16[1,1,128,768]{3,2,1,0:T(8,128)(2,1)S(1)}, u32[]{:S(2)}) copy-start(bf16[1,1,128,768]{3,2,1,0:T(8,128)(2,1)S(1)} %get-tuple-element.69) | copy-start | bytes 589828
  51.0 77.3 %collective-permute-start.14 = (bf16[3,1,128,768]{3,2,1,0:T(8,128)(2,1)}, bf16[3,1,128,768]{3,2,1,0:T(8,128)(2,1)}, u32[]{:S(2)}, u32[]{:S(2)}) collective-permute-start(bf16[3,1,128,768]{3,2,1,0:T(8,128)(2,1)} %pad_maximum_fusion.6), channel_id=1, source_target_pairs={{4,0},{8,4},{12,8},{0,12},{5,1},{9,5},{13,9},{1,13},{6,2},{10,6},{... | collective-permute-start | bytes 1769480 | tf_op jit(solution)/shard_map/ppermute | solution.py:21
  71.4 56.9 %collective-permute-start.13 = (bf16[3,1,128,768]{3,2,1,0:T(8,128)(2,1)}, bf16[3,1,128,768]{3,2,1,0:T(8,128)(2,1)}, u32[]{:S(2)}, u32[]{:S(2)}) collective-permute-start(bf16[3,1,128,768]{3,2,1,0:T(8,128)(2,1)} %pad_maximum_fusion.6), channel_id=1, source_target_pairs={{0,4},{4,8},{8,12},{12,0},{1,5},{5,9},{9,13},{13,1},{2,6},{6,10},{... | collective-permute-start | bytes 1769480 | tf_op jit(solution)/shard_map/ppermute | solution.py:19
  72.8 66.3 %collective-permute-start.24 = (bf16[3,1,128,768]{3,2,1,0:T(8,128)(2,1)}, bf16[3,1,128,768]{3,2,1,0:T(8,128)(2,1)}, u32[]{:S(2)}, u32[]{:S(2)}) collective-permute-start(bf16[3,1,128,768]{3,2,1,0:T(8,128)(2,1)} %pad_maximum_fusion.7), channel_id=1, source_target_pairs={{4,0},{8,4},{12,8},{0,12},{5,1},{9,5},{13,9},{1,13},{6,2},{10,6},{... | collective-permute-start | bytes 1769480 | tf_op jit(solution)/shard_map/ppermute | solution.py:21
  78.8 19.3 %copy-start.23 = (bf16[1,1,128,768]{3,2,1,0:T(8,128)(2,1)S(1)}, bf16[1,1,128,768]{3,2,1,0:T(8,128)(2,1)}, u32[]{:S(2)}) copy-start(bf16[1,1,128,768]{3,2,1,0:T(8,128)(2,1)} %param.9) | copy-start | bytes 589828
  78.8 19.5 %copy-start.46 = (f32[128]{0:T(128)}, f32[128]{0:T(128)S(1)}, u32[]{:S(2)}) copy-start(f32[128]{0:T(128)S(1)} %log_add_fusion.5) | copy-start | bytes 1540
  81.4 27.1 %copy-start.43 = (f32[128]{0:T(128)}, f32[128]{0:T(128)S(1)}, u32[]{:S(2)}) copy-start(f32[128]{0:T(128)S(1)} %log_add_fusion.1) | copy-start | bytes 1540
  81.4 29.3 %copy-start.42 = (f32[128]{0:T(128)}, f32[128]{0:T(128)S(1)}, u32[]{:S(2)}) copy-start(f32[128]{0:T(128)S(1)} %log_add_fusion) | copy-start | bytes 1540
  81.4 19.2 %copy-start.28 = (bf16[1,1,128,128]{2,3,1,0:T(8,128)(2,1)S(1)}, bf16[1,1,128,128]{2,3,1,0:T(8,128)(2,1)}, u32[]{:S(2)}) copy-start(bf16[1,1,128,128]{2,3,1,0:T(8,128)(2,1)} %copy.31) | copy-start | bytes 98308
  96.7 51.0 %collective-permute-start.23 = (bf16[3,1,128,768]{3,2,1,0:T(8,128)(2,1)}, bf16[3,1,128,768]{3,2,1,0:T(8,128)(2,1)}, u32[]{:S(2)}, u32[]{:S(2)}) collective-permute-start(bf16[3,1,128,768]{3,2,1,0:T(8,128)(2,1)} %pad_maximum_fusion.7), channel_id=1, source_target_pairs={{0,4},{4,8},{8,12},{12,0},{1,5},{5,9},{9,13},{13,1},{2,6},{6,10},{... | collective-permute-start | bytes 1769480 | tf_op jit(solution)/shard_map/ppermute | solution.py:19
  100.7 6.8 %copy-start.40 = (f32[128]{0:T(128)}, f32[128]{0:T(128)S(1)}, u32[]{:S(2)}) copy-start(f32[128]{0:T(128)S(1)} %multiply_reduce_fusion.5) | copy-start | bytes 1540
  102.7 4.7 %copy-start.20 = (bf16[3,3,128,768]{3,2,1,0:T(8,128)(2,1)S(1)}, bf16[3,3,128,768]{3,2,1,0:T(8,128)(2,1)}, u32[]{:S(2)}) copy-start(bf16[3,3,128,768]{3,2,1,0:T(8,128)(2,1)} %copy-done.19) | copy-start | bytes 5308420
  102.7 4.7 %copy-start.44 = (f32[128]{0:T(128)S(1)}, f32[128]{0:T(128)}, u32[]{:S(2)}) copy-start(f32[128]{0:T(128)} %log_add_fusion.2) | copy-start | bytes 1540
  105.1 4.5 %copy-start.3 = (f32[1152,128]{1,0:T(8,128)S(1)}, f32[1152,128]{1,0:T(8,128)}, u32[]{:S(2)}) copy-start(f32[1152,128]{1,0:T(8,128)} %copy-done.2) | copy-start | bytes 1769476
  109.6 14.4 %copy-start.1 = (f32[1152,128]{1,0:T(8,128)S(1)}, f32[1152,128]{1,0:T(8,128)}, u32[]{:S(2)}) copy-start(f32[1152,128]{1,0:T(8,128)} %copy-done) | copy-start | bytes 1769476
  111.4 41.4 %collective-permute-start.16 = (f32[1,1,6,128]{3,2,1,0:T(8,128)S(1)}, f32[1,1,6,128]{3,2,1,0:T(8,128)S(1)}, u32[]{:S(2)}, u32[]{:S(2)}) collective-permute-start(f32[1,1,6,128]{3,2,1,0:T(8,128)S(1)} %bitcast.177), channel_id=1, source_target_pairs={{4,0},{8,4},{12,8},{0,12},{5,1},{9,5},{13,9},{1,13},{6,2},{10,6},{... | collective-permute-start | bytes 9224 | tf_op jit(solution)/shard_map/ppermute | solution.py:21
  115.6 7.7 %copy-start.41 = (f32[128]{0:T(128)}, f32[128]{0:T(128)S(1)}, u32[]{:S(2)}) copy-start(f32[128]{0:T(128)S(1)} %multiply_reduce_fusion.4) | copy-start | bytes 1540
  124.0 32.3 %copy-start.32 = (f32[6,128]{1,0:T(8,128)}, f32[6,128]{1,0:T(8,128)S(1)}, u32[]{:S(2)}) copy-start(f32[6,128]{1,0:T(8,128)S(1)} %stack.31) | copy-start | bytes 9220
  126.1 6.0 %copy-start.8 = (bf16[1,1,128,768]{3,2,1,0:T(8,128)(2,1)S(1)}, bf16[1,1,128,768]{3,2,1,0:T(8,128)(2,1)}, u32[]{:S(2)}) copy-start(bf16[1,1,128,768]{3,2,1,0:T(8,128)(2,1)} %param.7) | copy-start | bytes 589828
  126.1 6.0 %copy-start.16 = (bf16[1,1,128,768]{3,2,1,0:T(8,128)(2,1)S(1)}, bf16[1,1,128,768]{3,2,1,0:T(8,128)(2,1)}, u32[]{:S(2)}) copy-start(bf16[1,1,128,768]{3,2,1,0:T(8,128)(2,1)} %copy-done.15) | copy-start | bytes 589828
  128.3 24.5 %collective-permute-start.15 = (f32[1,1,6,128]{3,2,1,0:T(8,128)S(1)}, f32[1,1,6,128]{3,2,1,0:T(8,128)}, u32[]{:S(2)}, u32[]{:S(2)}) collective-permute-start(f32[1,1,6,128]{3,2,1,0:T(8,128)S(1)} %bitcast.178), channel_id=1, source_target_pairs={{0,4},{4,8},{8,12},{12,0},{1,5},{5,9},{9,13},{13,1},{2,6},{6,10},{... | collective-permute-start | bytes 9224 | tf_op jit(solution)/shard_map/ppermute | solution.py:19
  128.3 6.5 %copy-start.10 = (bf16[1,1,128,768]{3,2,1,0:T(8,128)(2,1)S(1)}, bf16[1,1,128,768]{3,2,1,0:T(8,128)(2,1)}, u32[]{:S(2)}) copy-start(bf16[1,1,128,768]{3,2,1,0:T(8,128)(2,1)} %param.10) | copy-start | bytes 589828
  128.3 28.0 %collective-permute-start.26 = (f32[1,1,6,128]{3,2,1,0:T(8,128)S(1)}, f32[1,1,6,128]{3,2,1,0:T(8,128)S(1)}, u32[]{:S(2)}, u32[]{:S(2)}) collective-permute-start(f32[1,1,6,128]{3,2,1,0:T(8,128)S(1)} %bitcast.182), channel_id=1, source_target_pairs={{4,0},{8,4},{12,8},{0,12},{5,1},{9,5},{13,9},{1,13},{6,2},{10,6},{... | collective-permute-start | bytes 9224 | tf_op jit(solution)/shard_map/ppermute | solution.py:21
  134.8 12.9 %copy-start.12 = (bf16[1,1,128,768]{3,2,1,0:T(8,128)(2,1)S(1)}, bf16[1,1,128,768]{3,2,1,0:T(8,128)(2,1)}, u32[]{:S(2)}) copy-start(bf16[1,1,128,768]{3,2,1,0:T(8,128)(2,1)} %copy-done.11) | copy-start | bytes 589828
  134.8 12.9 %copy-start.14 = (bf16[1,1,128,768]{3,2,1,0:T(8,128)(2,1)S(1)}, bf16[1,1,128,768]{3,2,1,0:T(8,128)(2,1)}, u32[]{:S(2)}) copy-start(bf16[1,1,128,768]{3,2,1,0:T(8,128)(2,1)} %copy-done.13) | copy-start | bytes 589828
  139.1 17.3 %collective-permute-start.25 = (f32[1,1,6,128]{3,2,1,0:T(8,128)S(1)}, f32[1,1,6,128]{3,2,1,0:T(8,128)}, u32[]{:S(2)}, u32[]{:S(2)}) collective-permute-start(f32[1,1,6,128]{3,2,1,0:T(8,128)S(1)} %bitcast.183), channel_id=1, source_target_pairs={{0,4},{4,8},{8,12},{12,0},{1,5},{5,9},{9,13},{13,1},{2,6},{6,10},{... | collective-permute-start | bytes 9224 | tf_op jit(solution)/shard_map/ppermute | solution.py:19
  149.2 23.2 %copy-start.18 = (bf16[3,3,128,768]{3,2,1,0:T(8,128)(2,1)S(1)}, bf16[3,3,128,768]{3,2,1,0:T(8,128)(2,1)}, u32[]{:S(2)}) copy-start(bf16[3,3,128,768]{3,2,1,0:T(8,128)(2,1)} %pad_maximum_fusion.2) | copy-start | bytes 5308420
  152.8 9.0 %copy-start.33 = (f32[1,1,6,128]{3,2,1,0:T(8,128)}, f32[1,1,6,128]{3,2,1,0:T(8,128)S(1)}, u32[]{:S(2)}) copy-start(f32[1,1,6,128]{3,2,1,0:T(8,128)S(1)} %collective-permute-done.16) | copy-start | bytes 9220
  153.5 6.3 %collective-permute-start.17 = (f32[1,3,6,128]{3,2,1,0:T(8,128)S(1)}, f32[1,3,6,128]{3,2,1,0:T(8,128)S(1)}, u32[]{:S(2)}, u32[]{:S(2)}) collective-permute-start(f32[1,3,6,128]{3,2,1,0:T(8,128)S(1)} %pad_maximum_fusion.8), channel_id=1, source_target_pairs={{8,0},{12,4},{0,8},{4,12},{9,1},{13,5},{1,9},{5,13},{10,2},{14,6},... | collective-permute-start | bytes 27656 | tf_op jit(solution)/shard_map/ppermute | solution.py:31
  154.3 7.5 %collective-permute-start.18 = (f32[1,3,6,128]{3,2,1,0:T(8,128)S(1)}, f32[1,3,6,128]{3,2,1,0:T(8,128)S(1)}, u32[]{:S(2)}, u32[]{:S(2)}) collective-permute-start(f32[1,3,6,128]{3,2,1,0:T(8,128)S(1)} %pad_maximum_fusion.8), channel_id=1, source_target_pairs={{0,2},{2,0},{1,3},{3,1},{4,6},{6,4},{5,7},{7,5},{8,10},{10,8},{9,1... | collective-permute-start | bytes 27656 | tf_op jit(solution)/shard_map/ppermute | solution.py:19
  154.3 7.5 %collective-permute-start.19 = (f32[1,3,6,128]{3,2,1,0:T(8,128)S(1)}, f32[1,3,6,128]{3,2,1,0:T(8,128)S(1)}, u32[]{:S(2)}, u32[]{:S(2)}) collective-permute-start(f32[1,3,6,128]{3,2,1,0:T(8,128)S(1)} %pad_maximum_fusion.8), channel_id=1, source_target_pairs={{2,0},{0,2},{3,1},{1,3},{6,4},{4,6},{7,5},{5,7},{10,8},{8,10},{11,... | collective-permute-start | bytes 27656 | tf_op jit(solution)/shard_map/ppermute | solution.py:21
  156.3 5.4 %copy-start.34 = (f32[1,1,6,128]{3,2,1,0:T(8,128)}, f32[1,1,6,128]{3,2,1,0:T(8,128)S(1)}, u32[]{:S(2)}) copy-start(f32[1,1,6,128]{3,2,1,0:T(8,128)S(1)} %collective-permute-done.26) | copy-start | bytes 9220
  157.6 7.5 %collective-permute-start.27 = (f32[1,3,6,128]{3,2,1,0:T(8,128)}, f32[1,3,6,128]{3,2,1,0:T(8,128)}, u32[]{:S(2)}, u32[]{:S(2)}) collective-permute-start(f32[1,3,6,128]{3,2,1,0:T(8,128)} %pad_maximum_fusion.9), channel_id=1, source_target_pairs={{8,0},{12,4},{0,8},{4,12},{9,1},{13,5},{1,9},{5,13},{10,2},{14,6},... | collective-permute-start | bytes 27656 | tf_op jit(solution)/shard_map/ppermute | solution.py:31
  159.7 5.4 %collective-permute-start.28 = (f32[1,3,6,128]{3,2,1,0:T(8,128)}, f32[1,3,6,128]{3,2,1,0:T(8,128)}, u32[]{:S(2)}, u32[]{:S(2)}) collective-permute-start(f32[1,3,6,128]{3,2,1,0:T(8,128)} %pad_maximum_fusion.9), channel_id=1, source_target_pairs={{0,2},{2,0},{1,3},{3,1},{4,6},{6,4},{5,7},{7,5},{8,10},{10,8},{9,1... | collective-permute-start | bytes 27656 | tf_op jit(solution)/shard_map/ppermute | solution.py:19
  159.8 5.4 %collective-permute-start.29 = (f32[1,3,6,128]{3,2,1,0:T(8,128)}, f32[1,3,6,128]{3,2,1,0:T(8,128)}, u32[]{:S(2)}, u32[]{:S(2)}) collective-permute-start(f32[1,3,6,128]{3,2,1,0:T(8,128)} %pad_maximum_fusion.9), channel_id=1, source_target_pairs={{2,0},{0,2},{3,1},{1,3},{6,4},{4,6},{7,5},{5,7},{10,8},{8,10},{11,... | collective-permute-start | bytes 27656 | tf_op jit(solution)/shard_map/ppermute | solution.py:21
  184.9 9.9 %copy-start.36 = (f32[3,3,128]{2,1,0:T(4,128)S(1)}, f32[3,3,128]{2,1,0:T(4,128)}, u32[]{:S(2)}) copy-start(f32[3,3,128]{2,1,0:T(4,128)} %get-tuple-element.15) | copy-start | bytes 13828
  195.4 4.7 %copy-start.37 = (f32[1152]{0:T(1024)S(1)}, f32[1152]{0:T(1024)}, u32[]{:S(2)}) copy-start(f32[1152]{0:T(1024)} %sub.351) | copy-start | bytes 13828
  208.7 5.9 %copy-start.24 = (f32[1152,128]{1,0:T(8,128)S(1)}, f32[1152,128]{1,0:T(8,128)}, u32[]{:S(2)}) copy-start(f32[1152,128]{1,0:T(8,128)} %fusion.25) | copy-start | bytes 1769476
  208.7 6.8 %copy-start.25 = (f32[1152,128]{1,0:T(8,128)S(1)}, f32[1152,128]{1,0:T(8,128)}, u32[]{:S(2)}) copy-start(f32[1152,128]{1,0:T(8,128)} %fusion.27) | copy-start | bytes 1769476
  210.6 5.9 %copy-start.26 = (f32[1152,128]{1,0:T(8,128)S(1)}, f32[1152,128]{1,0:T(8,128)}, u32[]{:S(2)}) copy-start(f32[1152,128]{1,0:T(8,128)} %fusion.29) | copy-start | bytes 1769476
  (13 other events, 24.0 us)
where the time goes:
time: 221 us; the launch traced here: 219 us
  matrix products  55 us (25%)
  waiting for transfers between devices  51.5 us (23%)
  starting transfers between devices  51.3 us (23%)
  local copies, waits for them, and re-layouts  34.2 us (15%)
  other arithmetic  25.9 us (12%)
    ppermute x12, waiting for transfers between devices, with_halo(): lax.ppermute(head, axis, [((i + 1) % count, i) for i in range(ends)])  31 us
    ppermute x12, starting transfers between devices, with_halo(): lax.ppermute(head, axis, [((i + 1) % count, i) for i in range(ends)])  30.2 us
    unnamed x104, local copies, waits for them, and re-layouts  15.7 us
    dot_general x6, matrix products, on_device(): jnp.einsum('qk,qd->kd', grad_scores, queries_head, preferred_element_type...  13 us
    dot_general x6, matrix products, on_device(): jnp.dot(grad_scores, keys_head, preferred_element_type=jnp.float32)  12.8 us
    ppermute x12, waiting for transfers between devices, with_halo(): lax.ppermute(tail, axis, [(i, (i + 1) % count) for i in range(ends)])  11.4 us
    dot_general x6, matrix products, on_device(): jnp.einsum('qd,kd->qk', queries_head, keys_here, preferred_element_type=j...  10.7 us
    ppermute x12, starting transfers between devices, with_halo(): lax.ppermute(tail, axis, [(i, (i + 1) % count) for i in range(ends)])  10.6 us
  transfers between devices with their start and end apart: 30, of which 6 were waited for; matrix products, arithmetic and copies ran while one was open for 27% of the time, Pallas kernels for 0%

commit v1 on v0

--- a/solution.py
+++ b/solution.py
@@ -1,8 +1,11 @@
+import functools
 import math
 
 import jax
 import jax.numpy as jnp
 from jax import lax
+from jax.experimental import pallas as pl
+from jax.experimental.pallas import tpu as pltpu
 from jax.sharding import PartitionSpec as P
 
 HD = 128
@@ -75,7 +78,7 @@
     return (close_poles(near_stats[0], mirror[0]), close_poles(near_stats[1], mirror[1]))
 
 
-def on_device(queries, key_tokens, value_tokens, out_grad, counts):
+def by_tiles(queries, key_tokens, value_tokens, out_grad, counts):
     own_rows = queries.shape[0]
     tile_len = queries.shape[2]
     feat_width = queries.shape[3]
@@ -88,9 +91,7 @@
     positions = jnp.arange(tile_len, dtype=jnp.int32)
     flat_counts = counts.reshape(-1)
     near_k, near_v = around_pair(key_tokens, value_tokens)
-    attended_rows, query_rows, total_rows, dot_rows = ([], [], [], [])
-    row_local = 0
-    slot_ids = neighbour_tiles(row_base + row_local, col_at, lat_tiles, lon_tiles)
+    slot_ids = neighbour_tiles(row_base, col_at, lat_tiles, lon_tiles)
     key_valid = (positions[None, :] < flat_counts[slot_ids][:, None]).reshape(-1)
     near_keys = near_k.reshape(9 * tile_len, feat_width)
     near_values = near_v.reshape(9 * tile_len, feat_width)
@@ -100,8 +101,8 @@
     head_dots = []
     for head_index in range(head_count):
         columns = slice(head_index * HD, (head_index + 1) * HD)
-        query_here = queries[row_local, 0, :, columns]
-        grad_here = out_grad[row_local, 0, :, columns]
+        query_here = queries[0, 0, :, columns]
+        grad_here = out_grad[0, 0, :, columns]
         keys_head = near_keys[:, columns]
         values_head = near_values[:, columns]
         scores = (
@@ -130,19 +131,13 @@
         query_parts.append(query_part.astype(jnp.bfloat16))
         head_totals.append(log_total[:, 0])
         head_dots.append(out_dot)
-    attended_rows.append(jnp.concatenate(head_outs, -1))
-    query_rows.append(jnp.concatenate(query_parts, -1))
-    total_rows.append(jnp.stack(head_totals))
-    dot_rows.append(jnp.stack(head_dots))
-    attended = jnp.stack(attended_rows)[:, None]
-    query_grad = jnp.stack(query_rows)[:, None]
-    own_totals = jnp.stack(total_rows)[:, None]
-    own_dots = jnp.stack(dot_rows)[:, None]
+    attended = jnp.concatenate(head_outs, -1)[None, None]
+    query_grad = jnp.concatenate(query_parts, -1)[None, None]
+    own_totals = jnp.stack(head_totals)[None, None]
+    own_dots = jnp.stack(head_dots)[None, None]
     near_q, near_g = around_pair(queries, out_grad)
     near_total, near_dot = around_stats(own_totals, own_dots)
-    key_rows, value_rows = ([], [])
-    row_local = 0
-    own_valid = positions < counts[row_base + row_local, col_at]
+    own_valid = positions < counts[row_base, col_at]
     near_queries = near_q.reshape(9 * tile_len, feat_width)
     near_grads = near_g.reshape(9 * tile_len, feat_width)
     key_parts = []
@@ -151,8 +146,8 @@
         columns = slice(head_index * HD, (head_index + 1) * HD)
         queries_head = near_queries[:, columns]
         grads_head = near_grads[:, columns]
-        keys_here = key_tokens[row_local, 0, :, columns]
-        values_here = value_tokens[row_local, 0, :, columns]
+        keys_here = key_tokens[0, 0, :, columns]
+        values_here = value_tokens[0, 0, :, columns]
         totals_head = near_total[:, :, head_index, :].reshape(9 * tile_len)
         dots_head = near_dot[:, :, head_index, :].reshape(9 * tile_len)
         scores = (
@@ -174,30 +169,535 @@
         )
         key_parts.append(key_part.astype(jnp.bfloat16))
         value_parts.append(value_part.astype(jnp.bfloat16))
-    key_rows.append(jnp.concatenate(key_parts, -1))
-    value_rows.append(jnp.concatenate(value_parts, -1))
-    key_grad = jnp.stack(key_rows)[:, None]
-    value_grad = jnp.stack(value_rows)[:, None]
+    key_grad = jnp.concatenate(key_parts, -1)[None, None]
+    value_grad = jnp.concatenate(value_parts, -1)[None, None]
     return (attended, query_grad, key_grad, value_grad)
 
 
+def heads_fit(lat, lon, heads):
+    fits = (
+        heads % lat == 0
+        and heads // lat <= lon <= 2 * (heads // lat)
+        and lon % 2 == 0
+        and 4 <= lat * lon <= 16
+    )
+    if not fits:
+        return False
+    first = relative_counts(lat, lon)
+    return all(
+        relative_counts(lat, lon, row, col, core) == first
+        for row in range(lat)
+        for col in range(lon)
+        for core in range(2)
+    )
+
+
+def relative_counts(lat, lon, row=0, col=0, core=0):
+    times = slot_counts(lat, lon)
+    tile = []
+    for step in steps_of(lat, lon, core):
+        from_col = [c for c in range(lon) if column_after(c, step, lon) == col][0]
+        tile.append((row - step[1]) % lat * lon + from_col)
+    tile = in_slots(tile)
+    return [[times[i][j] for j in tile] for i in tile]
+
+
+def in_slots(found):
+    return [*found[:-3], found[-1], *found[-3:-1]]
+
+
+def in_steps(found):
+    return [*found[:-3], *found[-2:], found[-3]]
+
+
+def head_of(row, col, core, lat, lon, heads):
+    per_row = heads // lat
+    place = col - (1 - core % 2) * (lon - per_row)
+    return row * per_row + place, (place >= 0) & (place < per_row)
+
+
+def steps_of(lat, lon, core):
+    half = lon // 2
+    found = [(True, row_step, 0) for row_step in range(lat - 1, -1, -1)]
+    for row_step in range(lat - 1, -1, -1):
+        for col_step in range(1, half):
+            turns = (True, row_step, col_step), (False, row_step, col_step)
+            found.extend(turns[::-1] if core % 2 else turns)
+    found.extend((False, row_step, 0) for row_step in range(1, lat))
+    return found + [(False, 0, 0)]
+
+
+def column_after(col, step, lon):
+    half = lon // 2
+    other = col // half ^ int(step[0])
+    return other * half + (col + step[2]) % half
+
+
+def partner(row, col, core, n, lat, lon, back=False):
+    places = []
+    for which in (0, 1):
+        step = steps_of(lat, lon, which)[n]
+        to_row = lax.rem(row + (lat - step[1] if back else step[1]), lat)
+        to_col = jnp.int32(0)
+        for here in range(lon):
+            there = column_after(here, step, lon)
+            if back:
+                to_col = jnp.where(col == there, here, to_col)
+            else:
+                to_col = jnp.where(col == here, there, to_col)
+        places.append((to_row, to_col))
+    return [jnp.where(core % 2 == 0, a, b) for a, b in zip(*places)]
+
+
+def routes(n, lat, lon, cores, heads, back):
+    pairs = []
+    for row in range(lat):
+        for col in range(lon):
+            for core in range(cores):
+                step = steps_of(lat, lon, core)[n]
+                to_row, to_col = (row + step[1]) % lat, column_after(col, step, lon)
+                if head_of(to_row, to_col, core, lat, lon, heads)[1]:
+                    here = (col * lat + row) * cores + core
+                    there = (to_col * lat + to_row) * cores + core
+                    pairs.append((there, here) if back else (here, there))
+    return pairs
+
+
+def slot_counts(lat, lon):
+    times = [[0] * (lat * lon) for _ in range(lat * lon)]
+    for row in range(lat):
+        for col in range(lon):
+            for a in (-1, 0, 1):
+                for b in (-1, 0, 1):
+                    near_row, near_col = row + a, col + b
+                    if near_row < 0 or near_row > lat - 1:
+                        near_col += lon // 2
+                        near_row = min(max(near_row, 0), lat - 1)
+                    times[row * lon + col][near_row * lon + near_col % lon] += 1
+    return times
+
+
+def pack_kernel(lat, lon, heads, *refs):
+    tensors, blocks, whole, sems = refs[:4], refs[4:-2], refs[-2], refs[-1]
+    row, col, core = (lax.axis_index(a) for a in ("lat", "lon", "head"))
+    parts = sems.shape[1]
+    size = whole.shape[1] // parts
+    copies = []
+    for n in range(parts):
+        rows = pl.ds(n * size, size)
+        for t, tensor in enumerate(tensors):
+            copies.append(
+                pltpu.make_async_copy(
+                    tensor.at[0, 0, rows, :], whole.at[t, rows, :], sems.at[t, n]
+                )
+            )
+    for copy in copies:
+        copy.start()
+    for n in range(parts):
+        rows = slice(n * size, (n + 1) * size)
+        for copy in copies[4 * n : 4 * n + 4]:
+            copy.wait()
+        for m, block in enumerate(blocks):
+            head, used = head_of(*partner(row, col, core, m, lat, lon), core, lat, lon, heads)
+
+            @pl.when(used)
+            def _():
+                features = pl.ds(pl.multiple_of(head * HD, HD), HD)
+                for t in range(4):
+                    block[t, rows, :] = whole[t, rows, features]
+
+
+def unpack_kernel(lat, lon, heads, *refs):
+    blocks, tensors, whole, sems = refs[:-6], refs[-6:-2], refs[-2], refs[-1]
+    row, col, core = (lax.axis_index(a) for a in ("lat", "lon", "head"))
+    parts = sems.shape[1]
+    size = whole.shape[1] // parts
+    copies = []
+    for n in range(parts):
+        rows = slice(n * size, (n + 1) * size)
+        for m, block in enumerate(blocks):
+            head, used = head_of(*partner(row, col, core, m, lat, lon), core, lat, lon, heads)
+
+            @pl.when(used)
+            def _():
+                features = pl.ds(pl.multiple_of(head * HD, HD), HD)
+                for t in range(4):
+                    whole[t, rows, features] = block[t, rows, :]
+
+        rows = pl.ds(n * size, size)
+        for t, tensor in enumerate(tensors):
+            copies.append(
+                pltpu.make_async_copy(
+                    whole.at[t, rows, :], tensor.at[0, 0, rows, :], sems.at[t, n]
+                )
+            )
+            copies[-1].start()
+    for copy in copies:
+        copy.wait()
+
+
+class Sphere:
+    def __init__(self, lat, lon, times, key_marks, query_marks):
+        self.tiles = lat * lon
+        self.times = times
+        self.key_marks, self.query_marks = key_marks, query_marks
+        self.size = key_marks.shape[1]
+        self.wide = 2 * self.size
+        self.rounds = self.tiles // 2
+        self.scale = 1.0 / math.sqrt(HD)
+        self.of_tile = lax.broadcasted_iota(jnp.int32, (1, self.wide), 1) // self.size
+        self.held = [None] * self.tiles
+
+    def mark(self, limits):
+        shape = (self.size, HD)
+        key_row = lax.broadcasted_iota(jnp.int32, shape, 0)
+        lane = lax.broadcasted_iota(jnp.int32, shape, 1)
+        for j in range(self.tiles):
+            unseen = (lane == 0) & (key_row >= limits[j])
+            key_mark = jnp.where(unseen, -1e30, jnp.where(lane == j + 1, 1.0, 0.0))
+            self.key_marks[j] = key_mark.astype(self.key_marks.dtype)
+            apart = jnp.zeros(shape, jnp.bool_)
+            for k in range(self.tiles):
+                if self.times[j][k] == 0:
+                    apart = apart | (lane == k + 1)
+            query_mark = jnp.where(apart, -1e30, jnp.where(lane == 0, 1.0, 0.0))
+            self.query_marks[j] = query_mark.astype(self.query_marks.dtype)
+
+    def rows(self, j):
+        return slice(j * self.size, (j + 1) * self.size)
+
+    def lanes(self, t):
+        return slice(t * self.wide, (t + 1) * self.wide)
+
+    def stacked(self, t, n):
+        return jnp.concatenate([self.held[2 * t + k][n] for k in range(2)], 0)
+
+    def marked(self, t, n, marks):
+        parts = [(self.held[i][n], marks[i]) for i in (2 * t, 2 * t + 1)]
+        return jnp.concatenate([jnp.concatenate(part, 1) for part in parts], 0)
+
+    def score(self, t, u):
+        return contract_last(
+            self.marked(u, 1, self.key_marks), self.marked(t, 0, self.query_marks)
+        )
+
+    def grad_weight(self, t, u):
+        return contract_last(self.stacked(u, 2), self.stacked(t, 3))
+
+    def exponential(self, scores, top):
+        return jnp.exp2((scores - top) * (self.scale * math.log2(math.e)))
+
+    def named(self, t, j):
+        line = jnp.ones((1, self.wide), jnp.float32)
+        for k in range(2):
+            if self.times[2 * t + k][j] > 1:
+                line = jnp.where(self.of_tile == k, float(self.times[2 * t + k][j]), line)
+        return line
+
+    def folded(self, part, op):
+        return op(part.reshape(part.shape[0] // 8, 8, self.wide), axis=0)
+
+    def added(self, total, t, u, parts):
+        for k in range(2):
+            part = self.folded(parts[self.rows(k), :], jnp.sum) * self.named(t, 2 * u + k)
+            total = part if total is None else total + part
+        return total
+
+
+def contract_last(a, b):
+    return lax.dot_general(a, b, (((1,), (1,)), ((), ())), preferred_element_type=jnp.float32)
+
+
+def greater(a, b):
+    return b if a is None else jnp.maximum(a, b)
+
+
+def begin_kernel(lat, lon, times, *refs):
+    tiles = lat * lon
+    all_counts, blocks, outs = refs[0], refs[1 : tiles - 1], refs[tiles - 1 :]
+    key_marks, query_marks, keys_t, values_t, grads_t, scores, grad_weights, stats = outs[:8]
+    counts, sem = outs[8:]
+    sphere = Sphere(lat, lon, times, key_marks, query_marks)
+    sphere.held[: tiles - 2] = blocks
+    rounds = sphere.rounds - 1
+    copy = pltpu.make_async_copy(all_counts, counts, sem)
+    copy.start()
+    for t in range(rounds):
+        for u in range(rounds):
+            grad_weights[t, sphere.lanes(u), :] = sphere.grad_weight(t, u)
+        for i in (2 * t, 2 * t + 1):
+            keys_t[:, sphere.rows(i)] = blocks[i][1].T
+            values_t[:, sphere.rows(i)] = blocks[i][2].T
+            grads_t[:, sphere.rows(i)] = blocks[i][3].T
+    copy.wait()
+    row, col, core = (lax.axis_index(a) for a in ("lat", "lon", "head"))
+    limits = [
+        counts[tuple(partner(row, col, core, n, lat, lon, True))] for n in range(tiles)
+    ]
+    sphere.mark(in_slots(limits))
+    best, total = [None] * rounds, [None] * rounds
+
+    def score(t, u):
+        part = sphere.score(t, u)
+        scores[t, sphere.lanes(u), :] = part
+        best[t] = greater(best[t], sphere.folded(part, jnp.max))
+
+    for u in range(rounds):
+        score(0, u)
+    for t in range(rounds):
+        best[t] = jnp.max(best[t], axis=0, keepdims=True)
+        for u in range(rounds):
+            part = sphere.exponential(scores[t, sphere.lanes(u), :], best[t])
+            scores[t, sphere.lanes(u), :] = part
+            total[t] = sphere.added(total[t], t, u, part)
+            if t + 1 < rounds:
+                score(t + 1, u)
+        stats[t, :8, :] = jnp.broadcast_to(best[t], (8, sphere.wide))
+        stats[t, 8:, :] = total[t]
+
+
+def finish_kernel(lat, lon, times, *refs):
+    tiles = lat * lon
+    blocks, refs = refs[:tiles], refs[tiles:]
+    key_marks, query_marks, keys_t, values_t, grads_t, scores, grad_weights, stats = refs[:8]
+    made, refs = refs[8 : 8 + tiles], refs[8 + tiles :]
+    last_keys_t, last_values_t, last_grads_t, more_scores, weights_low, grads_low = refs
+    sphere = Sphere(lat, lon, times, key_marks, query_marks)
+    sphere.held[:] = blocks
+    f32, low = jnp.float32, weights_low.dtype
+    rounds, last = sphere.rounds, sphere.rounds - 1
+    best, total, old, share, out_dot = ([None] * rounds for _ in range(5))
+    early = slice(0, last * sphere.wide)
+    late = sphere.lanes(last)
+
+    def held_scores(t, j):
+        if t < last and j // 2 < last:
+            return scores.at[t, sphere.rows(j), :]
+        if t < last:
+            return more_scores.at[t, sphere.rows(j - 2 * last), :]
+        return more_scores.at[last + j // 2, sphere.rows(j % 2), :]
+
+    def score(t, u):
+        part = sphere.score(t, u)
+        for k in range(2):
+            held_scores(t, 2 * u + k)[...] = part[sphere.rows(k), :]
+        best[t] = greater(best[t], sphere.folded(part, jnp.max))
+
+    def exponential(t, u):
+        parts = []
+        for j in (2 * u, 2 * u + 1):
+            parts.append(sphere.exponential(held_scores(t, j)[...], best[t]))
+            held_scores(t, j)[...] = parts[-1]
+        total[t] = sphere.added(total[t], t, u, jnp.concatenate(parts, 0))
+
+    def settle(t):
+        before = stats[t, :1, :]
+        best[t] = jnp.maximum(before, jnp.max(best[t], axis=0, keepdims=True))
+        old[t] = sphere.exponential(before, best[t])
+        total[t] = stats[t, 8:, :] * old[t]
+        exponential(t, last)
+        share[t] = 1.0 / jnp.sum(total[t], axis=0, keepdims=True)
+
+    def factor(t, j):
+        line = share[t] * sphere.named(t, j)
+        return line * old[t] if t < last and j // 2 < last else line
+
+    def weight(t, u):
+        for j in (2 * u, 2 * u + 1):
+            part = held_scores(t, j)[...] * factor(t, j)
+            weights_low[sphere.rows(j), sphere.lanes(t)] = part.astype(low)
+
+    def from_keys(first_t, last_t, low_scores, t):
+        lanes = sphere.lanes(t)
+        return jnp.dot(
+            first_t[...], low_scores[early, lanes], preferred_element_type=f32
+        ) + jnp.dot(last_t[...], low_scores[late, lanes], preferred_element_type=f32)
+
+    def attend(t):
+        out_t = from_keys(values_t, last_values_t, weights_low, t).astype(low)
+        grad_t = grads_t[:, sphere.lanes(t)] if t < last else last_grads_t[...]
+        out_dot[t] = jnp.sum(grad_t.astype(f32) * out_t.astype(f32), axis=0, keepdims=True)
+        for k in range(2):
+            made[2 * t + k][0] = out_t[:, sphere.rows(k)].T
+
+    def grad_score(t, u):
+        if t < last and u < last:
+            part = grad_weights[t, sphere.lanes(u), :]
+        else:
+            part = sphere.grad_weight(t, u)
+        for k in range(2):
+            j = 2 * u + k
+            weights = held_scores(t, j)[...] * factor(t, j)
+            grad = weights * (part[sphere.rows(k), :] - out_dot[t])
+            grads_low[sphere.rows(j), sphere.lanes(t)] = grad.astype(low)
+
+    def query_grad(t):
+        query_t = (from_keys(keys_t, last_keys_t, grads_low, t) * sphere.scale).astype(low)
+        for k in range(2):
+            made[2 * t + k][1] = query_t[:, sphere.rows(k)].T
+
+    def key_side(n, low_scores, to, factor):
+        part = jnp.dot(
+            low_scores[...],
+            jnp.concatenate([block[n] for block in blocks], 0),
+            preferred_element_type=f32,
+        )
+        for j in range(tiles):
+            made[j][to] = (part[sphere.rows(j), :] * factor).astype(low)
+
+    for t in range(last):
+        score(t, last)
+    for k in range(2):
+        block = blocks[2 * last + k]
+        last_keys_t[:, sphere.rows(k)] = block[1].T
+        last_values_t[:, sphere.rows(k)] = block[2].T
+        last_grads_t[:, sphere.rows(k)] = block[3].T
+    for t in range(last):
+        settle(t)
+        if t > 0:
+            attend(t - 1)
+        if t > 1:
+            query_grad(t - 2)
+        for u in range(rounds):
+            weight(t, u)
+            if t == 0:
+                score(last, u)
+            if t == 1 or last == 1:
+                if u == 0:
+                    best[last] = jnp.max(best[last], axis=0, keepdims=True)
+                exponential(last, u)
+            if t > 0:
+                grad_score(t - 1, u)
+    share[last] = 1.0 / jnp.sum(total[last], axis=0, keepdims=True)
+    attend(last - 1)
+    if last > 1:
+        query_grad(last - 2)
+    for u in range(rounds):
+        weight(last, u)
+        grad_score(last - 1, u)
+    attend(last)
+    key_side(3, weights_low, 3, 1.0)
+    query_grad(last - 1)
+    for u in range(rounds):
+        grad_score(last, u)
+    query_grad(last)
+    key_side(0, grads_low, 2, sphere.scale)
+
+
+def by_heads(queries, key_tokens, value_tokens, out_grad, counts):
+    lat, lon, cores = (lax.axis_size(a) for a in ("lat", "lon", "head"))
+    tiles = lat * lon
+    tile_len, width = queries.shape[2], queries.shape[3]
+    heads = width // HD
+    low, f32 = queries.dtype, jnp.float32
+    in_vmem = pl.BlockSpec(memory_space=pltpu.VMEM)
+    in_hbm = pl.BlockSpec(memory_space=pltpu.HBM)
+    whole = jax.ShapeDtypeStruct(queries.shape, low)
+    block = pltpu.VMEM((4, tile_len, HD), low)
+    small = pltpu.CompilerParams(vmem_limit_bytes=6 * 1024 * 1024)
+
+    def sent(blocks, back):
+        axes = ("lon", "lat", "head")
+        return [
+            lax.ppermute(b, axes, routes(n, lat, lon, cores, heads, back))
+            for n, b in enumerate(blocks[:-1])
+        ] + [blocks[-1]]
+
+    def from_hbm(*arrays):
+        return [pltpu.with_memory_space_constraint(x, pltpu.HBM) for x in arrays]
+
+    packed = pl.pallas_call(
+        functools.partial(pack_kernel, lat, lon, heads),
+        out_shape=[block] * tiles,
+        in_specs=[in_hbm] * 4,
+        out_specs=[in_vmem] * tiles,
+        scratch_shapes=[
+            pltpu.VMEM((4, tile_len, width), low),
+            pltpu.SemaphoreType.DMA((4, 4)),
+        ],
+        compiler_params=small,
+        name="pack",
+    )(*from_hbm(queries, key_tokens, value_tokens, out_grad))
+    there = in_slots(sent(packed, False))
+    key_len, wide, begun = tiles * tile_len, 2 * tile_len, (tiles - 2) * tile_len
+    times = relative_counts(lat, lon)
+    large = pltpu.CompilerParams(vmem_limit_bytes=24 * 1024 * 1024)
+    shared = [
+        pltpu.VMEM((tiles, tile_len, HD), low),
+        pltpu.VMEM((tiles, tile_len, HD), low),
+        pltpu.VMEM((HD, begun), low),
+        pltpu.VMEM((HD, begun), low),
+        pltpu.VMEM((HD, begun), low),
+        pltpu.VMEM((tiles // 2 - 1, begun, wide), f32),
+        pltpu.VMEM((tiles // 2 - 1, begun, wide), f32),
+        pltpu.VMEM((tiles // 2 - 1, 16, wide), f32),
+    ]
+    done = pl.pallas_call(
+        functools.partial(begin_kernel, lat, lon, times),
+        out_shape=shared,
+        in_specs=[in_hbm] + [in_vmem] * (tiles - 2),
+        out_specs=[in_vmem] * len(shared),
+        scratch_shapes=[pltpu.SMEM(counts.shape, counts.dtype), pltpu.SemaphoreType.DMA],
+        compiler_params=large,
+        cost_estimate=pl.CostEstimate(
+            flops=6 * begun * begun * HD,
+            bytes_accessed=8 * begun * HD,
+            transcendentals=begun * begun,
+        ),
+        name="begin",
+    )(*from_hbm(counts), *there[: tiles - 2])
+    made = pl.pallas_call(
+        functools.partial(finish_kernel, lat, lon, times),
+        out_shape=[block] * tiles,
+        in_specs=[in_vmem] * (tiles + len(shared)),
+        out_specs=[in_vmem] * tiles,
+        scratch_shapes=[
+            pltpu.VMEM((HD, wide), low),
+            pltpu.VMEM((HD, wide), low),
+            pltpu.VMEM((HD, wide), low),
+            pltpu.VMEM((tiles - 1, wide, wide), f32),
+            pltpu.VMEM((key_len, key_len), low),
+            pltpu.VMEM((key_len, key_len), low),
+        ],
+        compiler_params=large,
+        cost_estimate=pl.CostEstimate(
+            flops=14 * key_len * key_len * HD - 6 * begun * begun * HD,
+            bytes_accessed=16 * key_len * HD,
+            transcendentals=key_len * key_len - begun * begun,
+        ),
+        name="finish",
+    )(*there, *done)
+    home = sent(in_steps(made), True)
+    return tuple(
+        pl.pallas_call(
+            functools.partial(unpack_kernel, lat, lon, heads),
+            out_shape=[whole] * 4,
+            in_specs=[in_vmem] * tiles,
+            out_specs=[in_hbm] * 4,
+            scratch_shapes=[
+                pltpu.VMEM((4, tile_len, width), low),
+                pltpu.SemaphoreType.DMA((4, 4)),
+            ],
+            compiler_params=small,
+            name="unpack",
+        )(*home)
+    )
+
+
 def solution(mesh):
-    placed = (
-        P(("groups", "lat"), "lon", None, "head"),
-        P(("groups", "lat"), "lon", None, "head"),
-        P(("groups", "lat"), "lon", None, "head"),
-        P(("groups", "lat"), "lon", None, "head"),
-        P("groups", None),
-    )
+    tokens = P(("groups", "lat"), "lon", None, "head")
+
+    def on_device(queries, *rest):
+        lat, lon = mesh.shape["lat"], mesh.shape["lon"]
+        one_tile = queries.shape[:2] == (1, 1)
+        if one_tile and heads_fit(lat, lon, queries.shape[3] // HD):
+            return by_heads(queries, *rest)
+        return by_tiles(queries, *rest)
+
     return jax.shard_map(
         on_device,
         mesh=mesh,
-        in_specs=placed,
-        out_specs=(
-            P(("groups", "lat"), "lon", None, "head"),
-            P(("groups", "lat"), "lon", None, "head"),
-            P(("groups", "lat"), "lon", None, "head"),
-            P(("groups", "lat"), "lon", None, "head"),
-        ),
+        in_specs=(tokens,) * 4 + (P("groups", None),),
+        out_specs=(tokens,) * 4,
         check_vma=False,
     )

time: 221 us -> 55.7 us (0.25)
  the two profiles are of different devices: /device:TPU:0 before, /device:TPU:20 now
where the time goes in v1:
time: 55.7 us; the launch traced here: 55.2 us
  starting transfers between devices  40.2 us (72%)
  waiting for transfers between devices  7.23 us (13%)
  Pallas kernels  6.96 us (12%)
  between operations  0.84 us (2%)
    ppermute x14, starting transfers between devices, sent(): lax.ppermute(b, axes, routes(n, lat, lon, cores, heads, back))  40.2 us
    ppermute x14, waiting for transfers between devices, sent(): lax.ppermute(b, axes, routes(n, lat, lon, cores, heads, back))  7.23 us
    pallas_call x1, Pallas kernels, by_heads(): pl.pallas_call(functools.partial(finish_kernel, lat, lon, times), out_sha...  3.08 us
    pallas_call x1, Pallas kernels, by_heads(): pl.pallas_call(functools.partial(begin_kernel, lat, lon, times), out_shap...  1.54 us
    pallas_call x1, Pallas kernels, by_heads(): pl.pallas_call(functools.partial(pack_kernel, lat, lon, heads), out_shape...  1.3 us
  transfers between devices with their start and end apart: 14, of which 4 were waited for; matrix products, arithmetic and copies ran while one was open for 0% of the time, Pallas kernels for 3%

profile of v1, /device:TPU:20, one launch (start us, length us, event | category | flops | bytes accessed | tf_op | source)
XLA Modules:
  0.0 55.2 jit_solution(16232695728467991902)
XLA Ops:
  0.6 1.3 %pack.1 = (bf16[4,128,128]{2,1,0:T(8,128)(2,1)S(1)}, bf16[4,128,128]{2,1,0:T(8,128)(2,1)S(1)}, bf16[4,128,128]{2,1,0:T(8,128)(2,1)S(1)}, bf16[4,128,128]{2,1,0:T...) custom-call(bf16[1,1,128,768]{3,2,1,0:T(8,128)(2,1)} %refs_0_.2, ...), custom_call_target="tpu_custom_call" | custom-call | tf_op jit(solution)/shard_map/pack/pallas_call | solution.py:609
  1.9 1.3 %collective-permute-start = (bf16[4,128,128]{2,1,0:T(8,128)(2,1)S(1)}, bf16[4,128,128]{2,1,0:T(8,128)(2,1)S(1)}, u32[]{:S(2)}, u32[]{:S(2)}) collective-permute-start(bf16[4,128,128]{2,1,0:T(8,128)(2,1)S(1)} %get-tuple-element.28), channel_id=1, source_target_pairs={{0,10},{1,11},{4,14},{9,3},{12,6},{13,7},{2,8},{3,9},{6,12},{11,1}... | collective-permute-start | bytes 393224 | tf_op jit(solution)/shard_map/ppermute | solution.py:602
  3.2 1.3 %collective-permute-start.1 = (bf16[4,128,128]{2,1,0:T(8,128)(2,1)S(1)}, bf16[4,128,128]{2,1,0:T(8,128)(2,1)S(1)}, u32[]{:S(2)}, u32[]{:S(2)}) collective-permute-start(bf16[4,128,128]{2,1,0:T(8,128)(2,1)S(1)} %get-tuple-element.29), channel_id=1, source_target_pairs={{0,8},{1,9},{4,12},{9,1},{12,4},{13,5},{2,10},{3,11},{6,14},{11,3}... | collective-permute-start | bytes 393224 | tf_op jit(solution)/shard_map/ppermute | solution.py:602
  4.5 7.4 %collective-permute-start.2 = (bf16[4,128,128]{2,1,0:T(8,128)(2,1)S(1)}, bf16[4,128,128]{2,1,0:T(8,128)(2,1)S(1)}, u32[]{:S(2)}, u32[]{:S(2)}) collective-permute-start(bf16[4,128,128]{2,1,0:T(8,128)(2,1)S(1)} %get-tuple-element.30), channel_id=1, source_target_pairs={{0,14},{1,7},{4,10},{5,3},{8,6},{13,11},{2,12},{3,5},{6,8},{7,1},{... | collective-permute-start | bytes 393224 | tf_op jit(solution)/shard_map/ppermute | solution.py:602
  12.0 2.4 %collective-permute-start.3 = (bf16[4,128,128]{2,1,0:T(8,128)(2,1)S(1)}, bf16[4,128,128]{2,1,0:T(8,128)(2,1)S(1)}, u32[]{:S(2)}, u32[]{:S(2)}) collective-permute-start(bf16[4,128,128]{2,1,0:T(8,128)(2,1)S(1)} %get-tuple-element.31), channel_id=1, source_target_pairs={{0,6},{5,11},{8,14},{9,7},{12,10},{13,3},{2,4},{7,9},{10,12},{11,5... | collective-permute-start | bytes 393224 | tf_op jit(solution)/shard_map/ppermute | solution.py:602
  14.4 1.9 %collective-permute-start.4 = (bf16[4,128,128]{2,1,0:T(8,128)(2,1)S(1)}, bf16[4,128,128]{2,1,0:T(8,128)(2,1)S(1)}, u32[]{:S(2)}, u32[]{:S(2)}) collective-permute-start(bf16[4,128,128]{2,1,0:T(8,128)(2,1)S(1)} %get-tuple-element.32), channel_id=1, source_target_pairs={{0,12},{1,5},{4,8},{5,1},{8,4},{13,9},{2,14},{3,7},{6,10},{7,3},{1... | collective-permute-start | bytes 393224 | tf_op jit(solution)/shard_map/ppermute | solution.py:602
  16.3 0.0 collective-permute-done.refs_1_.refs_0_
  16.3 3.7 %collective-permute-start.5 = (bf16[4,128,128]{2,1,0:T(8,128)(2,1)S(1)}, bf16[4,128,128]{2,1,0:T(8,128)(2,1)S(1)}, u32[]{:S(2)}, u32[]{:S(2)}) collective-permute-start(bf16[4,128,128]{2,1,0:T(8,128)(2,1)S(1)} %get-tuple-element.34), channel_id=1, source_target_pairs={{0,4},{5,9},{8,12},{9,5},{12,8},{13,1},{2,6},{7,11},{10,14},{11,7}... | collective-permute-start | bytes 393224 | tf_op jit(solution)/shard_map/ppermute | solution.py:602
  20.1 0.0 collective-permute-done.1.refs_2_.refs_1_
  20.1 2.4 %collective-permute-start.6 = (bf16[4,128,128]{2,1,0:T(8,128)(2,1)S(1)}, bf16[4,128,128]{2,1,0:T(8,128)(2,1)S(1)}, u32[]{:S(2)}, u32[]{:S(2)}) collective-permute-start(bf16[4,128,128]{2,1,0:T(8,128)(2,1)S(1)} %get-tuple-element.35), channel_id=1, source_target_pairs={{1,3},{4,6},{5,7},{8,10},{9,11},{12,14},{3,1},{6,4},{7,5},{10,8},{... | collective-permute-start | bytes 393224 | tf_op jit(solution)/shard_map/ppermute | solution.py:602
  22.5 0.0 collective-permute-done.2.refs_3_.refs_2_
  22.5 0.0 collective-permute-done.3.refs_4_.refs_3_
  22.6 2.4 %collective-permute-done.4.refs_5_.refs_4_ = bf16[4,128,128]{2,1,0:T(8,128)(2,1)S(1)} collective-permute-done((bf16[4,128,128]{2,1,0:T(8,128)(2,1)S(1)}, bf16[4,128,128]{2,1,0:T(8,128)(2,1)S(1)}, u32[]{:S(2)}, u32[]{:S(2)}) %collective-permute-start.4) | collective-permute-done | bytes 131104 | tf_op jit(solution)/shard_map/ppermute | solution.py:602
  25.0 1.5 %begin.1 = (bf16[8,128,128]{2,1,0:T(8,128)(2,1)S(1)}, bf16[8,128,128]{2,1,0:T(8,128)(2,1)S(1)}, bf16[128,768]{1,0:T(8,128)(2,1)S(1)}, bf16[128,768]{1,0:T(8,128)...) custom-call(s32[2,4]{1,0:T(2,128)} %refs_0_.3, ...), custom_call_target="tpu_custom_call" | custom-call | flops 452984832 | bytes 786432 | tf_op jit(solution)/shard_map/begin/pallas_call | solution.py:635
  26.5 0.0 collective-permute-done.5.refs_6_
  26.5 0.4 collective-permute-done.6.refs_7_
  26.9 3.1 %finish.1 = (bf16[4,128,128]{2,1,0:T(8,128)(2,1)S(1)}, bf16[4,128,128]{2,1,0:T(8,128)(2,1)S(1)}, bf16[4,128,128]{2,1,0:T(8,128)(2,1)S(1)}, bf16[4,128,128]{2,1,0...) custom-call(bf16[4,128,128]{2,1,0:T(8,128)(2,1)S(1)} %collective-per, ...), custom_call_target="tpu_custom_call" | custom-call | flops 1426063360 | bytes 2097152 | tf_op jit(solution)/shard_map/finish/pallas_call | solution.py:649
  30.0 1.3 %collective-permute-start.7 = (bf16[4,128,128]{2,1,0:T(8,128)(2,1)S(1)}, bf16[4,128,128]{2,1,0:T(8,128)(2,1)S(1)}, u32[]{:S(2)}, u32[]{:S(2)}) collective-permute-start(bf16[4,128,128]{2,1,0:T(8,128)(2,1)S(1)} %get-tuple-element.44), channel_id=1, source_target_pairs={{10,0},{11,1},{14,4},{3,9},{6,12},{7,13},{8,2},{9,3},{12,6},{1,11}... | collective-permute-start | bytes 393224 | tf_op jit(solution)/shard_map/ppermute | solution.py:602
  31.3 1.3 %collective-permute-start.8 = (bf16[4,128,128]{2,1,0:T(8,128)(2,1)S(1)}, bf16[4,128,128]{2,1,0:T(8,128)(2,1)S(1)}, u32[]{:S(2)}, u32[]{:S(2)}) collective-permute-start(bf16[4,128,128]{2,1,0:T(8,128)(2,1)S(1)} %get-tuple-element.45), channel_id=1, source_target_pairs={{8,0},{9,1},{12,4},{1,9},{4,12},{5,13},{10,2},{11,3},{14,6},{3,11}... | collective-permute-start | bytes 393224 | tf_op jit(solution)/shard_map/ppermute | solution.py:602
  32.6 6.5 %collective-permute-start.9 = (bf16[4,128,128]{2,1,0:T(8,128)(2,1)S(1)}, bf16[4,128,128]{2,1,0:T(8,128)(2,1)S(1)}, u32[]{:S(2)}, u32[]{:S(2)}) collective-permute-start(bf16[4,128,128]{2,1,0:T(8,128)(2,1)S(1)} %get-tuple-element.46), channel_id=1, source_target_pairs={{14,0},{7,1},{10,4},{3,5},{6,8},{11,13},{12,2},{5,3},{8,6},{1,7},{... | collective-permute-start | bytes 393224 | tf_op jit(solution)/shard_map/ppermute | solution.py:602
  39.2 2.4 %collective-permute-start.10 = (bf16[4,128,128]{2,1,0:T(8,128)(2,1)S(1)}, bf16[4,128,128]{2,1,0:T(8,128)(2,1)S(1)}, u32[]{:S(2)}, u32[]{:S(2)}) collective-permute-start(bf16[4,128,128]{2,1,0:T(8,128)(2,1)S(1)} %get-tuple-element.47), channel_id=1, source_target_pairs={{6,0},{11,5},{14,8},{7,9},{10,12},{3,13},{4,2},{9,7},{12,10},{5,11... | collective-permute-start | bytes 393224 | tf_op jit(solution)/shard_map/ppermute | solution.py:602
  41.6 1.9 %collective-permute-start.11 = (bf16[4,128,128]{2,1,0:T(8,128)(2,1)S(1)}, bf16[4,128,128]{2,1,0:T(8,128)(2,1)S(1)}, u32[]{:S(2)}, u32[]{:S(2)}) collective-permute-start(bf16[4,128,128]{2,1,0:T(8,128)(2,1)S(1)} %get-tuple-element.48), channel_id=1, source_target_pairs={{12,0},{5,1},{8,4},{1,5},{4,8},{9,13},{14,2},{7,3},{10,6},{3,7},{6... | collective-permute-start | bytes 393224 | tf_op jit(solution)/shard_map/ppermute | solution.py:602
  43.5 0.0 collective-permute-done.7.refs_0_
  43.5 3.7 %collective-permute-start.12 = (bf16[4,128,128]{2,1,0:T(8,128)(2,1)S(1)}, bf16[4,128,128]{2,1,0:T(8,128)(2,1)S(1)}, u32[]{:S(2)}, u32[]{:S(2)}) collective-permute-start(bf16[4,128,128]{2,1,0:T(8,128)(2,1)S(1)} %get-tuple-element.49), channel_id=1, source_target_pairs={{4,0},{9,5},{12,8},{5,9},{8,12},{1,13},{6,2},{11,7},{14,10},{7,11}... | collective-permute-start | bytes 393224 | tf_op jit(solution)/shard_map/ppermute | solution.py:602
  47.3 0.0 collective-permute-done.8.refs_1_
  47.3 2.4 %collective-permute-start.13 = (bf16[4,128,128]{2,1,0:T(8,128)(2,1)S(1)}, bf16[4,128,128]{2,1,0:T(8,128)(2,1)S(1)}, u32[]{:S(2)}, u32[]{:S(2)}) collective-permute-start(bf16[4,128,128]{2,1,0:T(8,128)(2,1)S(1)} %get-tuple-element.50), channel_id=1, source_target_pairs={{3,1},{6,4},{7,5},{10,8},{11,9},{14,12},{1,3},{4,6},{5,7},{8,10},{... | collective-permute-start | bytes 393224 | tf_op jit(solution)/shard_map/ppermute | solution.py:602
  49.7 0.0 collective-permute-done.9.refs_2_
  49.8 0.0 collective-permute-done.10.refs_3_
  49.8 0.0 collective-permute-done.11.refs_4_
  49.8 0.6 %collective-permute-done.12.refs_5_ = bf16[4,128,128]{2,1,0:T(8,128)(2,1)S(1)} collective-permute-done((bf16[4,128,128]{2,1,0:T(8,128)(2,1)S(1)}, bf16[4,128,128]{2,1,0:T(8,128)(2,1)S(1)}, u32[]{:S(2)}, u32[]{:S(2)}) %collective-permute-start.12) | collective-permute-done | bytes 131104 | tf_op jit(solution)/shard_map/ppermute | solution.py:602
  50.4 3.7 %collective-permute-done.13.refs_6_ = bf16[4,128,128]{2,1,0:T(8,128)(2,1)S(1)} collective-permute-done((bf16[4,128,128]{2,1,0:T(8,128)(2,1)S(1)}, bf16[4,128,128]{2,1,0:T(8,128)(2,1)S(1)}, u32[]{:S(2)}, u32[]{:S(2)}) %collective-permute-start.13) | collective-permute-done | bytes 131104 | tf_op jit(solution)/shard_map/ppermute | solution.py:602
  54.2 1.0 %unpack.1 = (bf16[1,1,128,768]{3,2,1,0:T(8,128)(2,1)}, bf16[1,1,128,768]{3,2,1,0:T(8,128)(2,1)}, bf16[1,1,128,768]{3,2,1,0:T(8,128)(2,1)}, bf16[1,1,128,768]{3,2,1,0:T(8,128)(2,1)}) custom-call(bf16[4,128,128]{2,1,0:T(8,128)(2,1)S(1)} %collective-permute-done.7.refs_0_, bf16[4,128,128]{2,1,0:T(8,128)(2,1)S(1)} %collective-permute-done.8.refs_1_, ...), custom_call_target="tpu_custom_call" | custom-call | tf_op jit(solution)/shard_map/unpack/pallas_call | solution.py:672
Async XLA Ops:
  1.9 14.4 %collective-permute-start = (bf16[4,128,128]{2,1,0:T(8,128)(2,1)S(1)}, bf16[4,128,128]{2,1,0:T(8,128)(2,1)S(1)}, u32[]{:S(2)}, u32[]{:S(2)}) collective-permute-start(bf16[4,128,128]{2,1,0:T(8,128)(2,1)S(1)} %get-tuple-element.28), channel_id=1, source_target_pairs={{0,10},{1,11},{4,14},{9,3},{12,6},{13,7},{2,8},{3,9},{6,12},{11,1}... | collective-permute-start | bytes 393224 | tf_op jit(solution)/shard_map/ppermute | solution.py:602
  3.2 16.8 %collective-permute-start.1 = (bf16[4,128,128]{2,1,0:T(8,128)(2,1)S(1)}, bf16[4,128,128]{2,1,0:T(8,128)(2,1)S(1)}, u32[]{:S(2)}, u32[]{:S(2)}) collective-permute-start(bf16[4,128,128]{2,1,0:T(8,128)(2,1)S(1)} %get-tuple-element.29), channel_id=1, source_target_pairs={{0,8},{1,9},{4,12},{9,1},{12,4},{13,5},{2,10},{3,11},{6,14},{11,3}... | collective-permute-start | bytes 393224 | tf_op jit(solution)/shard_map/ppermute | solution.py:602
  4.5 18.0 %collective-permute-start.2 = (bf16[4,128,128]{2,1,0:T(8,128)(2,1)S(1)}, bf16[4,128,128]{2,1,0:T(8,128)(2,1)S(1)}, u32[]{:S(2)}, u32[]{:S(2)}) collective-permute-start(bf16[4,128,128]{2,1,0:T(8,128)(2,1)S(1)} %get-tuple-element.30), channel_id=1, source_target_pairs={{0,14},{1,7},{4,10},{5,3},{8,6},{13,11},{2,12},{3,5},{6,8},{7,1},{... | collective-permute-start | bytes 393224 | tf_op jit(solution)/shard_map/ppermute | solution.py:602
  12.0 10.6 %collective-permute-start.3 = (bf16[4,128,128]{2,1,0:T(8,128)(2,1)S(1)}, bf16[4,128,128]{2,1,0:T(8,128)(2,1)S(1)}, u32[]{:S(2)}, u32[]{:S(2)}) collective-permute-start(bf16[4,128,128]{2,1,0:T(8,128)(2,1)S(1)} %get-tuple-element.31), channel_id=1, source_target_pairs={{0,6},{5,11},{8,14},{9,7},{12,10},{13,3},{2,4},{7,9},{10,12},{11,5... | collective-permute-start | bytes 393224 | tf_op jit(solution)/shard_map/ppermute | solution.py:602
  14.4 10.6 %collective-permute-start.4 = (bf16[4,128,128]{2,1,0:T(8,128)(2,1)S(1)}, bf16[4,128,128]{2,1,0:T(8,128)(2,1)S(1)}, u32[]{:S(2)}, u32[]{:S(2)}) collective-permute-start(bf16[4,128,128]{2,1,0:T(8,128)(2,1)S(1)} %get-tuple-element.32), channel_id=1, source_target_pairs={{0,12},{1,5},{4,8},{5,1},{8,4},{13,9},{2,14},{3,7},{6,10},{7,3},{1... | collective-permute-start | bytes 393224 | tf_op jit(solution)/shard_map/ppermute | solution.py:602
  16.3 10.2 %collective-permute-start.5 = (bf16[4,128,128]{2,1,0:T(8,128)(2,1)S(1)}, bf16[4,128,128]{2,1,0:T(8,128)(2,1)S(1)}, u32[]{:S(2)}, u32[]{:S(2)}) collective-permute-start(bf16[4,128,128]{2,1,0:T(8,128)(2,1)S(1)} %get-tuple-element.34), channel_id=1, source_target_pairs={{0,4},{5,9},{8,12},{9,5},{12,8},{13,1},{2,6},{7,11},{10,14},{11,7}... | collective-permute-start | bytes 393224 | tf_op jit(solution)/shard_map/ppermute | solution.py:602
  20.1 6.9 %collective-permute-start.6 = (bf16[4,128,128]{2,1,0:T(8,128)(2,1)S(1)}, bf16[4,128,128]{2,1,0:T(8,128)(2,1)S(1)}, u32[]{:S(2)}, u32[]{:S(2)}) collective-permute-start(bf16[4,128,128]{2,1,0:T(8,128)(2,1)S(1)} %get-tuple-element.35), channel_id=1, source_target_pairs={{1,3},{4,6},{5,7},{8,10},{9,11},{12,14},{3,1},{6,4},{7,5},{10,8},{... | collective-permute-start | bytes 393224 | tf_op jit(solution)/shard_map/ppermute | solution.py:602
  30.0 13.5 %collective-permute-start.7 = (bf16[4,128,128]{2,1,0:T(8,128)(2,1)S(1)}, bf16[4,128,128]{2,1,0:T(8,128)(2,1)S(1)}, u32[]{:S(2)}, u32[]{:S(2)}) collective-permute-start(bf16[4,128,128]{2,1,0:T(8,128)(2,1)S(1)} %get-tuple-element.44), channel_id=1, source_target_pairs={{10,0},{11,1},{14,4},{3,9},{6,12},{7,13},{8,2},{9,3},{12,6},{1,11}... | collective-permute-start | bytes 393224 | tf_op jit(solution)/shard_map/ppermute | solution.py:602
  31.3 16.0 %collective-permute-start.8 = (bf16[4,128,128]{2,1,0:T(8,128)(2,1)S(1)}, bf16[4,128,128]{2,1,0:T(8,128)(2,1)S(1)}, u32[]{:S(2)}, u32[]{:S(2)}) collective-permute-start(bf16[4,128,128]{2,1,0:T(8,128)(2,1)S(1)} %get-tuple-element.45), channel_id=1, source_target_pairs={{8,0},{9,1},{12,4},{1,9},{4,12},{5,13},{10,2},{11,3},{14,6},{3,11}... | collective-permute-start | bytes 393224 | tf_op jit(solution)/shard_map/ppermute | solution.py:602
  32.6 17.1 %collective-permute-start.9 = (bf16[4,128,128]{2,1,0:T(8,128)(2,1)S(1)}, bf16[4,128,128]{2,1,0:T(8,128)(2,1)S(1)}, u32[]{:S(2)}, u32[]{:S(2)}) collective-permute-start(bf16[4,128,128]{2,1,0:T(8,128)(2,1)S(1)} %get-tuple-element.46), channel_id=1, source_target_pairs={{14,0},{7,1},{10,4},{3,5},{6,8},{11,13},{12,2},{5,3},{8,6},{1,7},{... | collective-permute-start | bytes 393224 | tf_op jit(solution)/shard_map/ppermute | solution.py:602
  39.2 10.6 %collective-permute-start.10 = (bf16[4,128,128]{2,1,0:T(8,128)(2,1)S(1)}, bf16[4,128,128]{2,1,0:T(8,128)(2,1)S(1)}, u32[]{:S(2)}, u32[]{:S(2)}) collective-permute-start(bf16[4,128,128]{2,1,0:T(8,128)(2,1)S(1)} %get-tuple-element.47), channel_id=1, source_target_pairs={{6,0},{11,5},{14,8},{7,9},{10,12},{3,13},{4,2},{9,7},{12,10},{5,11... | collective-permute-start | bytes 393224 | tf_op jit(solution)/shard_map/ppermute | solution.py:602
  41.6 8.2 %collective-permute-start.11 = (bf16[4,128,128]{2,1,0:T(8,128)(2,1)S(1)}, bf16[4,128,128]{2,1,0:T(8,128)(2,1)S(1)}, u32[]{:S(2)}, u32[]{:S(2)}) collective-permute-start(bf16[4,128,128]{2,1,0:T(8,128)(2,1)S(1)} %get-tuple-element.48), channel_id=1, source_target_pairs={{12,0},{5,1},{8,4},{1,5},{4,8},{9,13},{14,2},{7,3},{10,6},{3,7},{6... | collective-permute-start | bytes 393224 | tf_op jit(solution)/shard_map/ppermute | solution.py:602
  43.5 6.9 %collective-permute-start.12 = (bf16[4,128,128]{2,1,0:T(8,128)(2,1)S(1)}, bf16[4,128,128]{2,1,0:T(8,128)(2,1)S(1)}, u32[]{:S(2)}, u32[]{:S(2)}) collective-permute-start(bf16[4,128,128]{2,1,0:T(8,128)(2,1)S(1)} %get-tuple-element.49), channel_id=1, source_target_pairs={{4,0},{9,5},{12,8},{5,9},{8,12},{1,13},{6,2},{11,7},{14,10},{7,11}... | collective-permute-start | bytes 393224 | tf_op jit(solution)/shard_map/ppermute | solution.py:602
  47.3 6.9 %collective-permute-start.13 = (bf16[4,128,128]{2,1,0:T(8,128)(2,1)S(1)}, bf16[4,128,128]{2,1,0:T(8,128)(2,1)S(1)}, u32[]{:S(2)}, u32[]{:S(2)}) collective-permute-start(bf16[4,128,128]{2,1,0:T(8,128)(2,1)S(1)} %get-tuple-element.50), channel_id=1, source_target_pairs={{3,1},{6,4},{7,5},{10,8},{11,9},{14,12},{1,3},{4,6},{5,7},{8,10},{... | collective-permute-start | bytes 393224 | tf_op jit(solution)/shard_map/ppermute | solution.py:602

commit v2 on v1

--- a/solution.py
+++ b/solution.py
@@ -222,7 +222,7 @@
     for row_step in range(lat - 1, -1, -1):
         for col_step in range(1, half):
             turns = (True, row_step, col_step), (False, row_step, col_step)
-            found.extend(turns[::-1] if core % 2 else turns)
+            found.extend(turns if core % 2 else turns[::-1])
     found.extend((False, row_step, 0) for row_step in range(1, lat))
     return found + [(False, 0, 0)]
 

time: 55.7 us -> 56.8 us (1.020)
  starting transfers between devices: 40.2 us -> 41.3 us
    ppermute x14, starting transfers between devices: 40.2 us -> 41.3 us  [sent(): lax.ppermute(b, axes, routes(n, lat, lon, cores, heads, back))]
  transfers between devices with their start and end apart: 14 -> 14, of which waited for: 4 -> 3; matrix products, arithmetic and copies ran while one was open for 0% -> 0% of each run, Pallas kernels for 3% -> 3%
where the time goes in v2:
time: 56.8 us; the launch traced here: 56.3 us
  starting transfers between devices  41.3 us (73%)
  waiting for transfers between devices  7.22 us (13%)
  Pallas kernels  6.97 us (12%)
  between operations  0.85 us (1%)
    ppermute x14, starting transfers between devices, sent(): lax.ppermute(b, axes, routes(n, lat, lon, cores, heads, back))  41.3 us
    ppermute x14, waiting for transfers between devices, sent(): lax.ppermute(b, axes, routes(n, lat, lon, cores, heads, back))  7.22 us
    pallas_call x1, Pallas kernels, by_heads(): pl.pallas_call(functools.partial(finish_kernel, lat, lon, times), out_sha...  3.08 us
    pallas_call x1, Pallas kernels, by_heads(): pl.pallas_call(functools.partial(begin_kernel, lat, lon, times), out_shap...  1.55 us
    pallas_call x1, Pallas kernels, by_heads(): pl.pallas_call(functools.partial(pack_kernel, lat, lon, heads), out_shape...  1.3 us
  transfers between devices with their start and end apart: 14, of which 3 were waited for; matrix products, arithmetic and copies ran while one was open for 0% of the time, Pallas kernels for 3%

profile of v2, /device:TPU:20, one launch (start us, length us, event | category | flops | bytes accessed | tf_op | source)
XLA Modules:
  0.0 56.3 jit_solution(13387213335233967670)
XLA Ops:
  0.6 1.3 %pack.1 = (bf16[4,128,128]{2,1,0:T(8,128)(2,1)S(1)}, bf16[4,128,128]{2,1,0:T(8,128)(2,1)S(1)}, bf16[4,128,128]{2,1,0:T(8,128)(2,1)S(1)}, bf16[4,128,128]{2,1,0:T...) custom-call(bf16[1,1,128,768]{3,2,1,0:T(8,128)(2,1)} %refs_0_.2, ...), custom_call_target="tpu_custom_call" | custom-call | tf_op jit(solution)/shard_map/pack/pallas_call | solution.py:609
  1.9 1.3 %collective-permute-start = (bf16[4,128,128]{2,1,0:T(8,128)(2,1)S(1)}, bf16[4,128,128]{2,1,0:T(8,128)(2,1)S(1)}, u32[]{:S(2)}, u32[]{:S(2)}) collective-permute-start(bf16[4,128,128]{2,1,0:T(8,128)(2,1)S(1)} %get-tuple-element.28), channel_id=1, source_target_pairs={{0,10},{1,11},{4,14},{9,3},{12,6},{13,7},{2,8},{3,9},{6,12},{11,1}... | collective-permute-start | bytes 393224 | tf_op jit(solution)/shard_map/ppermute | solution.py:602
  3.2 1.3 %collective-permute-start.1 = (bf16[4,128,128]{2,1,0:T(8,128)(2,1)S(1)}, bf16[4,128,128]{2,1,0:T(8,128)(2,1)S(1)}, u32[]{:S(2)}, u32[]{:S(2)}) collective-permute-start(bf16[4,128,128]{2,1,0:T(8,128)(2,1)S(1)} %get-tuple-element.29), channel_id=1, source_target_pairs={{0,8},{1,9},{4,12},{9,1},{12,4},{13,5},{2,10},{3,11},{6,14},{11,3}... | collective-permute-start | bytes 393224 | tf_op jit(solution)/shard_map/ppermute | solution.py:602
  4.5 8.6 %collective-permute-start.2 = (bf16[4,128,128]{2,1,0:T(8,128)(2,1)S(1)}, bf16[4,128,128]{2,1,0:T(8,128)(2,1)S(1)}, u32[]{:S(2)}, u32[]{:S(2)}) collective-permute-start(bf16[4,128,128]{2,1,0:T(8,128)(2,1)S(1)} %get-tuple-element.30), channel_id=1, source_target_pairs={{0,6},{5,11},{8,14},{9,7},{12,10},{13,3},{2,4},{7,9},{10,12},{11,5... | collective-permute-start | bytes 393224 | tf_op jit(solution)/shard_map/ppermute | solution.py:602
  13.1 1.9 %collective-permute-start.3 = (bf16[4,128,128]{2,1,0:T(8,128)(2,1)S(1)}, bf16[4,128,128]{2,1,0:T(8,128)(2,1)S(1)}, u32[]{:S(2)}, u32[]{:S(2)}) collective-permute-start(bf16[4,128,128]{2,1,0:T(8,128)(2,1)S(1)} %get-tuple-element.31), channel_id=1, source_target_pairs={{0,14},{1,7},{4,10},{5,3},{8,6},{13,11},{2,12},{3,5},{6,8},{7,1},{... | collective-permute-start | bytes 393224 | tf_op jit(solution)/shard_map/ppermute | solution.py:602
  15.0 1.9 %collective-permute-start.4 = (bf16[4,128,128]{2,1,0:T(8,128)(2,1)S(1)}, bf16[4,128,128]{2,1,0:T(8,128)(2,1)S(1)}, u32[]{:S(2)}, u32[]{:S(2)}) collective-permute-start(bf16[4,128,128]{2,1,0:T(8,128)(2,1)S(1)} %get-tuple-element.32), channel_id=1, source_target_pairs={{0,4},{5,9},{8,12},{9,5},{12,8},{13,1},{2,6},{7,11},{10,14},{11,7}... | collective-permute-start | bytes 393224 | tf_op jit(solution)/shard_map/ppermute | solution.py:602
  17.0 0.0 collective-permute-done.refs_1_.refs_0_
  17.0 4.2 %collective-permute-start.5 = (bf16[4,128,128]{2,1,0:T(8,128)(2,1)S(1)}, bf16[4,128,128]{2,1,0:T(8,128)(2,1)S(1)}, u32[]{:S(2)}, u32[]{:S(2)}) collective-permute-start(bf16[4,128,128]{2,1,0:T(8,128)(2,1)S(1)} %get-tuple-element.34), channel_id=1, source_target_pairs={{0,12},{1,5},{4,8},{5,1},{8,4},{13,9},{2,14},{3,7},{6,10},{7,3},{1... | collective-permute-start | bytes 393224 | tf_op jit(solution)/shard_map/ppermute | solution.py:602
  21.2 0.0 collective-permute-done.1.refs_2_.refs_1_
  21.2 2.4 %collective-permute-start.6 = (bf16[4,128,128]{2,1,0:T(8,128)(2,1)S(1)}, bf16[4,128,128]{2,1,0:T(8,128)(2,1)S(1)}, u32[]{:S(2)}, u32[]{:S(2)}) collective-permute-start(bf16[4,128,128]{2,1,0:T(8,128)(2,1)S(1)} %get-tuple-element.35), channel_id=1, source_target_pairs={{1,3},{4,6},{5,7},{8,10},{9,11},{12,14},{3,1},{6,4},{7,5},{10,8},{... | collective-permute-start | bytes 393224 | tf_op jit(solution)/shard_map/ppermute | solution.py:602
  23.7 0.0 collective-permute-done.2.refs_3_.refs_2_
  23.7 0.0 collective-permute-done.3.refs_4_.refs_3_
  23.7 0.0 collective-permute-done.4.refs_5_.refs_4_
  23.7 1.5 %begin.1 = (bf16[8,128,128]{2,1,0:T(8,128)(2,1)S(1)}, bf16[8,128,128]{2,1,0:T(8,128)(2,1)S(1)}, bf16[128,768]{1,0:T(8,128)(2,1)S(1)}, bf16[128,768]{1,0:T(8,128)...) custom-call(s32[2,4]{1,0:T(2,128)} %refs_0_.3, ...), custom_call_target="tpu_custom_call" | custom-call | flops 452984832 | bytes 786432 | tf_op jit(solution)/shard_map/begin/pallas_call | solution.py:635
  25.2 0.0 collective-permute-done.5.refs_6_
  25.3 2.8 %collective-permute-done.6.refs_7_ = bf16[4,128,128]{2,1,0:T(8,128)(2,1)S(1)} collective-permute-done((bf16[4,128,128]{2,1,0:T(8,128)(2,1)S(1)}, bf16[4,128,128]{2,1,0:T(8,128)(2,1)S(1)}, u32[]{:S(2)}, u32[]{:S(2)}) %collective-permute-start.6) | collective-permute-done | bytes 131104 | tf_op jit(solution)/shard_map/ppermute | solution.py:602
  28.1 3.1 %finish.1 = (bf16[4,128,128]{2,1,0:T(8,128)(2,1)S(1)}, bf16[4,128,128]{2,1,0:T(8,128)(2,1)S(1)}, bf16[4,128,128]{2,1,0:T(8,128)(2,1)S(1)}, bf16[4,128,128]{2,1,0...) custom-call(bf16[4,128,128]{2,1,0:T(8,128)(2,1)S(1)} %collective-per, ...), custom_call_target="tpu_custom_call" | custom-call | flops 1426063360 | bytes 2097152 | tf_op jit(solution)/shard_map/finish/pallas_call | solution.py:649
  31.2 1.3 %collective-permute-start.7 = (bf16[4,128,128]{2,1,0:T(8,128)(2,1)S(1)}, bf16[4,128,128]{2,1,0:T(8,128)(2,1)S(1)}, u32[]{:S(2)}, u32[]{:S(2)}) collective-permute-start(bf16[4,128,128]{2,1,0:T(8,128)(2,1)S(1)} %get-tuple-element.44), channel_id=1, source_target_pairs={{10,0},{11,1},{14,4},{3,9},{6,12},{7,13},{8,2},{9,3},{12,6},{1,11}... | collective-permute-start | bytes 393224 | tf_op jit(solution)/shard_map/ppermute | solution.py:602
  32.5 1.3 %collective-permute-start.8 = (bf16[4,128,128]{2,1,0:T(8,128)(2,1)S(1)}, bf16[4,128,128]{2,1,0:T(8,128)(2,1)S(1)}, u32[]{:S(2)}, u32[]{:S(2)}) collective-permute-start(bf16[4,128,128]{2,1,0:T(8,128)(2,1)S(1)} %get-tuple-element.45), channel_id=1, source_target_pairs={{8,0},{9,1},{12,4},{1,9},{4,12},{5,13},{10,2},{11,3},{14,6},{3,11}... | collective-permute-start | bytes 393224 | tf_op jit(solution)/shard_map/ppermute | solution.py:602
  33.8 6.5 %collective-permute-start.9 = (bf16[4,128,128]{2,1,0:T(8,128)(2,1)S(1)}, bf16[4,128,128]{2,1,0:T(8,128)(2,1)S(1)}, u32[]{:S(2)}, u32[]{:S(2)}) collective-permute-start(bf16[4,128,128]{2,1,0:T(8,128)(2,1)S(1)} %get-tuple-element.46), channel_id=1, source_target_pairs={{6,0},{11,5},{14,8},{7,9},{10,12},{3,13},{4,2},{9,7},{12,10},{5,11... | collective-permute-start | bytes 393224 | tf_op jit(solution)/shard_map/ppermute | solution.py:602
  40.3 1.9 %collective-permute-start.10 = (bf16[4,128,128]{2,1,0:T(8,128)(2,1)S(1)}, bf16[4,128,128]{2,1,0:T(8,128)(2,1)S(1)}, u32[]{:S(2)}, u32[]{:S(2)}) collective-permute-start(bf16[4,128,128]{2,1,0:T(8,128)(2,1)S(1)} %get-tuple-element.47), channel_id=1, source_target_pairs={{14,0},{7,1},{10,4},{3,5},{6,8},{11,13},{12,2},{5,3},{8,6},{1,7},{... | collective-permute-start | bytes 393224 | tf_op jit(solution)/shard_map/ppermute | solution.py:602
  42.2 1.9 %collective-permute-start.11 = (bf16[4,128,128]{2,1,0:T(8,128)(2,1)S(1)}, bf16[4,128,128]{2,1,0:T(8,128)(2,1)S(1)}, u32[]{:S(2)}, u32[]{:S(2)}) collective-permute-start(bf16[4,128,128]{2,1,0:T(8,128)(2,1)S(1)} %get-tuple-element.48), channel_id=1, source_target_pairs={{4,0},{9,5},{12,8},{5,9},{8,12},{1,13},{6,2},{11,7},{14,10},{7,11}... | collective-permute-start | bytes 393224 | tf_op jit(solution)/shard_map/ppermute | solution.py:602
  44.2 0.0 collective-permute-done.7.refs_0_
  44.2 4.2 %collective-permute-start.12 = (bf16[4,128,128]{2,1,0:T(8,128)(2,1)S(1)}, bf16[4,128,128]{2,1,0:T(8,128)(2,1)S(1)}, u32[]{:S(2)}, u32[]{:S(2)}) collective-permute-start(bf16[4,128,128]{2,1,0:T(8,128)(2,1)S(1)} %get-tuple-element.49), channel_id=1, source_target_pairs={{12,0},{5,1},{8,4},{1,5},{4,8},{9,13},{14,2},{7,3},{10,6},{3,7},{6... | collective-permute-start | bytes 393224 | tf_op jit(solution)/shard_map/ppermute | solution.py:602
  48.4 0.0 collective-permute-done.8.refs_1_
  48.4 2.4 %collective-permute-start.13 = (bf16[4,128,128]{2,1,0:T(8,128)(2,1)S(1)}, bf16[4,128,128]{2,1,0:T(8,128)(2,1)S(1)}, u32[]{:S(2)}, u32[]{:S(2)}) collective-permute-start(bf16[4,128,128]{2,1,0:T(8,128)(2,1)S(1)} %get-tuple-element.50), channel_id=1, source_target_pairs={{3,1},{6,4},{7,5},{10,8},{11,9},{14,12},{1,3},{4,6},{5,7},{8,10},{... | collective-permute-start | bytes 393224 | tf_op jit(solution)/shard_map/ppermute | solution.py:602
  50.9 0.0 collective-permute-done.9.refs_2_
  50.9 0.0 collective-permute-done.10.refs_3_
  50.9 0.0 collective-permute-done.11.refs_4_
  50.9 0.4 collective-permute-done.12.refs_5_
  51.3 3.9 %collective-permute-done.13.refs_6_ = bf16[4,128,128]{2,1,0:T(8,128)(2,1)S(1)} collective-permute-done((bf16[4,128,128]{2,1,0:T(8,128)(2,1)S(1)}, bf16[4,128,128]{2,1,0:T(8,128)(2,1)S(1)}, u32[]{:S(2)}, u32[]{:S(2)}) %collective-permute-start.13) | collective-permute-done | bytes 131104 | tf_op jit(solution)/shard_map/ppermute | solution.py:602
  55.3 1.0 %unpack.1 = (bf16[1,1,128,768]{3,2,1,0:T(8,128)(2,1)}, bf16[1,1,128,768]{3,2,1,0:T(8,128)(2,1)}, bf16[1,1,128,768]{3,2,1,0:T(8,128)(2,1)}, bf16[1,1,128,768]{3,2,1,0:T(8,128)(2,1)}) custom-call(bf16[4,128,128]{2,1,0:T(8,128)(2,1)S(1)} %collective-permute-done.7.refs_0_, bf16[4,128,128]{2,1,0:T(8,128)(2,1)S(1)} %collective-permute-done.8.refs_1_, ...), custom_call_target="tpu_custom_call" | custom-call | tf_op jit(solution)/shard_map/unpack/pallas_call | solution.py:672
Async XLA Ops:
  1.9 15.0 %collective-permute-start = (bf16[4,128,128]{2,1,0:T(8,128)(2,1)S(1)}, bf16[4,128,128]{2,1,0:T(8,128)(2,1)S(1)}, u32[]{:S(2)}, u32[]{:S(2)}) collective-permute-start(bf16[4,128,128]{2,1,0:T(8,128)(2,1)S(1)} %get-tuple-element.28), channel_id=1, source_target_pairs={{0,10},{1,11},{4,14},{9,3},{12,6},{13,7},{2,8},{3,9},{6,12},{11,1}... | collective-permute-start | bytes 393224 | tf_op jit(solution)/shard_map/ppermute | solution.py:602
  3.2 18.0 %collective-permute-start.1 = (bf16[4,128,128]{2,1,0:T(8,128)(2,1)S(1)}, bf16[4,128,128]{2,1,0:T(8,128)(2,1)S(1)}, u32[]{:S(2)}, u32[]{:S(2)}) collective-permute-start(bf16[4,128,128]{2,1,0:T(8,128)(2,1)S(1)} %get-tuple-element.29), channel_id=1, source_target_pairs={{0,8},{1,9},{4,12},{9,1},{12,4},{13,5},{2,10},{3,11},{6,14},{11,3}... | collective-permute-start | bytes 393224 | tf_op jit(solution)/shard_map/ppermute | solution.py:602
  4.5 19.1 %collective-permute-start.2 = (bf16[4,128,128]{2,1,0:T(8,128)(2,1)S(1)}, bf16[4,128,128]{2,1,0:T(8,128)(2,1)S(1)}, u32[]{:S(2)}, u32[]{:S(2)}) collective-permute-start(bf16[4,128,128]{2,1,0:T(8,128)(2,1)S(1)} %get-tuple-element.30), channel_id=1, source_target_pairs={{0,6},{5,11},{8,14},{9,7},{12,10},{13,3},{2,4},{7,9},{10,12},{11,5... | collective-permute-start | bytes 393224 | tf_op jit(solution)/shard_map/ppermute | solution.py:602
  13.1 10.6 %collective-permute-start.3 = (bf16[4,128,128]{2,1,0:T(8,128)(2,1)S(1)}, bf16[4,128,128]{2,1,0:T(8,128)(2,1)S(1)}, u32[]{:S(2)}, u32[]{:S(2)}) collective-permute-start(bf16[4,128,128]{2,1,0:T(8,128)(2,1)S(1)} %get-tuple-element.31), channel_id=1, source_target_pairs={{0,14},{1,7},{4,10},{5,3},{8,6},{13,11},{2,12},{3,5},{6,8},{7,1},{... | collective-permute-start | bytes 393224 | tf_op jit(solution)/shard_map/ppermute | solution.py:602
  15.0 8.7 %collective-permute-start.4 = (bf16[4,128,128]{2,1,0:T(8,128)(2,1)S(1)}, bf16[4,128,128]{2,1,0:T(8,128)(2,1)S(1)}, u32[]{:S(2)}, u32[]{:S(2)}) collective-permute-start(bf16[4,128,128]{2,1,0:T(8,128)(2,1)S(1)} %get-tuple-element.32), channel_id=1, source_target_pairs={{0,4},{5,9},{8,12},{9,5},{12,8},{13,1},{2,6},{7,11},{10,14},{11,7}... | collective-permute-start | bytes 393224 | tf_op jit(solution)/shard_map/ppermute | solution.py:602
  17.0 8.3 %collective-permute-start.5 = (bf16[4,128,128]{2,1,0:T(8,128)(2,1)S(1)}, bf16[4,128,128]{2,1,0:T(8,128)(2,1)S(1)}, u32[]{:S(2)}, u32[]{:S(2)}) collective-permute-start(bf16[4,128,128]{2,1,0:T(8,128)(2,1)S(1)} %get-tuple-element.34), channel_id=1, source_target_pairs={{0,12},{1,5},{4,8},{5,1},{8,4},{13,9},{2,14},{3,7},{6,10},{7,3},{1... | collective-permute-start | bytes 393224 | tf_op jit(solution)/shard_map/ppermute | solution.py:602
  21.2 6.9 %collective-permute-start.6 = (bf16[4,128,128]{2,1,0:T(8,128)(2,1)S(1)}, bf16[4,128,128]{2,1,0:T(8,128)(2,1)S(1)}, u32[]{:S(2)}, u32[]{:S(2)}) collective-permute-start(bf16[4,128,128]{2,1,0:T(8,128)(2,1)S(1)} %get-tuple-element.35), channel_id=1, source_target_pairs={{1,3},{4,6},{5,7},{8,10},{9,11},{12,14},{3,1},{6,4},{7,5},{10,8},{... | collective-permute-start | bytes 393224 | tf_op jit(solution)/shard_map/ppermute | solution.py:602
  31.2 13.0 %collective-permute-start.7 = (bf16[4,128,128]{2,1,0:T(8,128)(2,1)S(1)}, bf16[4,128,128]{2,1,0:T(8,128)(2,1)S(1)}, u32[]{:S(2)}, u32[]{:S(2)}) collective-permute-start(bf16[4,128,128]{2,1,0:T(8,128)(2,1)S(1)} %get-tuple-element.44), channel_id=1, source_target_pairs={{10,0},{11,1},{14,4},{3,9},{6,12},{7,13},{8,2},{9,3},{12,6},{1,11}... | collective-permute-start | bytes 393224 | tf_op jit(solution)/shard_map/ppermute | solution.py:602
  32.5 15.9 %collective-permute-start.8 = (bf16[4,128,128]{2,1,0:T(8,128)(2,1)S(1)}, bf16[4,128,128]{2,1,0:T(8,128)(2,1)S(1)}, u32[]{:S(2)}, u32[]{:S(2)}) collective-permute-start(bf16[4,128,128]{2,1,0:T(8,128)(2,1)S(1)} %get-tuple-element.45), channel_id=1, source_target_pairs={{8,0},{9,1},{12,4},{1,9},{4,12},{5,13},{10,2},{11,3},{14,6},{3,11}... | collective-permute-start | bytes 393224 | tf_op jit(solution)/shard_map/ppermute | solution.py:602
  33.8 17.1 %collective-permute-start.9 = (bf16[4,128,128]{2,1,0:T(8,128)(2,1)S(1)}, bf16[4,128,128]{2,1,0:T(8,128)(2,1)S(1)}, u32[]{:S(2)}, u32[]{:S(2)}) collective-permute-start(bf16[4,128,128]{2,1,0:T(8,128)(2,1)S(1)} %get-tuple-element.46), channel_id=1, source_target_pairs={{6,0},{11,5},{14,8},{7,9},{10,12},{3,13},{4,2},{9,7},{12,10},{5,11... | collective-permute-start | bytes 393224 | tf_op jit(solution)/shard_map/ppermute | solution.py:602
  40.3 10.6 %collective-permute-start.10 = (bf16[4,128,128]{2,1,0:T(8,128)(2,1)S(1)}, bf16[4,128,128]{2,1,0:T(8,128)(2,1)S(1)}, u32[]{:S(2)}, u32[]{:S(2)}) collective-permute-start(bf16[4,128,128]{2,1,0:T(8,128)(2,1)S(1)} %get-tuple-element.47), channel_id=1, source_target_pairs={{14,0},{7,1},{10,4},{3,5},{6,8},{11,13},{12,2},{5,3},{8,6},{1,7},{... | collective-permute-start | bytes 393224 | tf_op jit(solution)/shard_map/ppermute | solution.py:602
  42.2 8.7 %collective-permute-start.11 = (bf16[4,128,128]{2,1,0:T(8,128)(2,1)S(1)}, bf16[4,128,128]{2,1,0:T(8,128)(2,1)S(1)}, u32[]{:S(2)}, u32[]{:S(2)}) collective-permute-start(bf16[4,128,128]{2,1,0:T(8,128)(2,1)S(1)} %get-tuple-element.48), channel_id=1, source_target_pairs={{4,0},{9,5},{12,8},{5,9},{8,12},{1,13},{6,2},{11,7},{14,10},{7,11}... | collective-permute-start | bytes 393224 | tf_op jit(solution)/shard_map/ppermute | solution.py:602
  44.2 7.2 %collective-permute-start.12 = (bf16[4,128,128]{2,1,0:T(8,128)(2,1)S(1)}, bf16[4,128,128]{2,1,0:T(8,128)(2,1)S(1)}, u32[]{:S(2)}, u32[]{:S(2)}) collective-permute-start(bf16[4,128,128]{2,1,0:T(8,128)(2,1)S(1)} %get-tuple-element.49), channel_id=1, source_target_pairs={{12,0},{5,1},{8,4},{1,5},{4,8},{9,13},{14,2},{7,3},{10,6},{3,7},{6... | collective-permute-start | bytes 393224 | tf_op jit(solution)/shard_map/ppermute | solution.py:602
  48.4 6.9 %collective-permute-start.13 = (bf16[4,128,128]{2,1,0:T(8,128)(2,1)S(1)}, bf16[4,128,128]{2,1,0:T(8,128)(2,1)S(1)}, u32[]{:S(2)}, u32[]{:S(2)}) collective-permute-start(bf16[4,128,128]{2,1,0:T(8,128)(2,1)S(1)} %get-tuple-element.50), channel_id=1, source_target_pairs={{3,1},{6,4},{7,5},{10,8},{11,9},{14,12},{1,3},{4,6},{5,7},{8,10},{... | collective-permute-start | bytes 393224 | tf_op jit(solution)/shard_map/ppermute | solution.py:602

commit v3 on v1

--- a/solution.py
+++ b/solution.py
@@ -598,10 +598,14 @@
 
     def sent(blocks, back):
         axes = ("lon", "lat", "head")
-        return [
-            lax.ppermute(b, axes, routes(n, lat, lon, cores, heads, back))
-            for n, b in enumerate(blocks[:-1])
-        ] + [blocks[-1]]
+        moves = list(range(tiles - 1))
+        if back:
+            full, mixed, along = moves[:lat], moves[lat : 1 - lat], moves[1 - lat :]
+            moves = full + mixed[::2] + mixed[1::2] + along
+        found = list(blocks)
+        for n in moves:
+            found[n] = lax.ppermute(found[n], axes, routes(n, lat, lon, cores, heads, back))
+        return found
 
     def from_hbm(*arrays):
         return [pltpu.with_memory_space_constraint(x, pltpu.HBM) for x in arrays]

time: 55.7 us -> 55.7 us (level)
  no operation moved by 1% of the time
where the time goes in v3:
time: 55.7 us; the launch traced here: 55.2 us
  starting transfers between devices  40.2 us (72%)
  waiting for transfers between devices  7.23 us (13%)
  Pallas kernels  6.96 us (12%)
  between operations  0.84 us (2%)
    ppermute x14, starting transfers between devices, sent(): lax.ppermute(found[n], axes, routes(n, lat, lon, cores, heads, back))  40.2 us
    ppermute x14, waiting for transfers between devices, sent(): lax.ppermute(found[n], axes, routes(n, lat, lon, cores, heads, back))  7.23 us
    pallas_call x1, Pallas kernels, by_heads(): pl.pallas_call(functools.partial(finish_kernel, lat, lon, times), out_sha...  3.08 us
    pallas_call x1, Pallas kernels, by_heads(): pl.pallas_call(functools.partial(begin_kernel, lat, lon, times), out_shap...  1.54 us
    pallas_call x1, Pallas kernels, by_heads(): pl.pallas_call(functools.partial(pack_kernel, lat, lon, heads), out_shape...  1.3 us
  transfers between devices with their start and end apart: 14, of which 4 were waited for; matrix products, arithmetic and copies ran while one was open for 0% of the time, Pallas kernels for 3%

profile of v3, /device:TPU:20, one launch (start us, length us, event | category | flops | bytes accessed | tf_op | source)
XLA Modules:
  0.0 55.2 jit_solution(16232695728467991902)
XLA Ops:
  0.6 1.3 %pack.1 = (bf16[4,128,128]{2,1,0:T(8,128)(2,1)S(1)}, bf16[4,128,128]{2,1,0:T(8,128)(2,1)S(1)}, bf16[4,128,128]{2,1,0:T(8,128)(2,1)S(1)}, bf16[4,128,128]{2,1,0:T...) custom-call(bf16[1,1,128,768]{3,2,1,0:T(8,128)(2,1)} %refs_0_.2, ...), custom_call_target="tpu_custom_call" | custom-call | tf_op jit(solution)/shard_map/pack/pallas_call | solution.py:613
  1.9 1.3 %collective-permute-start = (bf16[4,128,128]{2,1,0:T(8,128)(2,1)S(1)}, bf16[4,128,128]{2,1,0:T(8,128)(2,1)S(1)}, u32[]{:S(2)}, u32[]{:S(2)}) collective-permute-start(bf16[4,128,128]{2,1,0:T(8,128)(2,1)S(1)} %get-tuple-element.28), channel_id=1, source_target_pairs={{0,10},{1,11},{4,14},{9,3},{12,6},{13,7},{2,8},{3,9},{6,12},{11,1}... | collective-permute-start | bytes 393224 | tf_op jit(solution)/shard_map/ppermute | solution.py:607
  3.2 1.3 %collective-permute-start.1 = (bf16[4,128,128]{2,1,0:T(8,128)(2,1)S(1)}, bf16[4,128,128]{2,1,0:T(8,128)(2,1)S(1)}, u32[]{:S(2)}, u32[]{:S(2)}) collective-permute-start(bf16[4,128,128]{2,1,0:T(8,128)(2,1)S(1)} %get-tuple-element.29), channel_id=1, source_target_pairs={{0,8},{1,9},{4,12},{9,1},{12,4},{13,5},{2,10},{3,11},{6,14},{11,3}... | collective-permute-start | bytes 393224 | tf_op jit(solution)/shard_map/ppermute | solution.py:607
  4.5 7.4 %collective-permute-start.2 = (bf16[4,128,128]{2,1,0:T(8,128)(2,1)S(1)}, bf16[4,128,128]{2,1,0:T(8,128)(2,1)S(1)}, u32[]{:S(2)}, u32[]{:S(2)}) collective-permute-start(bf16[4,128,128]{2,1,0:T(8,128)(2,1)S(1)} %get-tuple-element.30), channel_id=1, source_target_pairs={{0,14},{1,7},{4,10},{5,3},{8,6},{13,11},{2,12},{3,5},{6,8},{7,1},{... | collective-permute-start | bytes 393224 | tf_op jit(solution)/shard_map/ppermute | solution.py:607
  12.0 2.4 %collective-permute-start.3 = (bf16[4,128,128]{2,1,0:T(8,128)(2,1)S(1)}, bf16[4,128,128]{2,1,0:T(8,128)(2,1)S(1)}, u32[]{:S(2)}, u32[]{:S(2)}) collective-permute-start(bf16[4,128,128]{2,1,0:T(8,128)(2,1)S(1)} %get-tuple-element.31), channel_id=1, source_target_pairs={{0,6},{5,11},{8,14},{9,7},{12,10},{13,3},{2,4},{7,9},{10,12},{11,5... | collective-permute-start | bytes 393224 | tf_op jit(solution)/shard_map/ppermute | solution.py:607
  14.4 1.9 %collective-permute-start.4 = (bf16[4,128,128]{2,1,0:T(8,128)(2,1)S(1)}, bf16[4,128,128]{2,1,0:T(8,128)(2,1)S(1)}, u32[]{:S(2)}, u32[]{:S(2)}) collective-permute-start(bf16[4,128,128]{2,1,0:T(8,128)(2,1)S(1)} %get-tuple-element.32), channel_id=1, source_target_pairs={{0,12},{1,5},{4,8},{5,1},{8,4},{13,9},{2,14},{3,7},{6,10},{7,3},{1... | collective-permute-start | bytes 393224 | tf_op jit(solution)/shard_map/ppermute | solution.py:607
  16.3 0.0 collective-permute-done.refs_1_.refs_0_
  16.3 3.7 %collective-permute-start.5 = (bf16[4,128,128]{2,1,0:T(8,128)(2,1)S(1)}, bf16[4,128,128]{2,1,0:T(8,128)(2,1)S(1)}, u32[]{:S(2)}, u32[]{:S(2)}) collective-permute-start(bf16[4,128,128]{2,1,0:T(8,128)(2,1)S(1)} %get-tuple-element.34), channel_id=1, source_target_pairs={{0,4},{5,9},{8,12},{9,5},{12,8},{13,1},{2,6},{7,11},{10,14},{11,7}... | collective-permute-start | bytes 393224 | tf_op jit(solution)/shard_map/ppermute | solution.py:607
  20.1 0.0 collective-permute-done.1.refs_2_.refs_1_
  20.1 2.4 %collective-permute-start.6 = (bf16[4,128,128]{2,1,0:T(8,128)(2,1)S(1)}, bf16[4,128,128]{2,1,0:T(8,128)(2,1)S(1)}, u32[]{:S(2)}, u32[]{:S(2)}) collective-permute-start(bf16[4,128,128]{2,1,0:T(8,128)(2,1)S(1)} %get-tuple-element.35), channel_id=1, source_target_pairs={{1,3},{4,6},{5,7},{8,10},{9,11},{12,14},{3,1},{6,4},{7,5},{10,8},{... | collective-permute-start | bytes 393224 | tf_op jit(solution)/shard_map/ppermute | solution.py:607
  22.5 0.0 collective-permute-done.2.refs_3_.refs_2_
  22.5 0.0 collective-permute-done.3.refs_4_.refs_3_
  22.6 2.4 %collective-permute-done.4.refs_5_.refs_4_ = bf16[4,128,128]{2,1,0:T(8,128)(2,1)S(1)} collective-permute-done((bf16[4,128,128]{2,1,0:T(8,128)(2,1)S(1)}, bf16[4,128,128]{2,1,0:T(8,128)(2,1)S(1)}, u32[]{:S(2)}, u32[]{:S(2)}) %collective-permute-start.4) | collective-permute-done | bytes 131104 | tf_op jit(solution)/shard_map/ppermute | solution.py:607
  25.0 1.5 %begin.1 = (bf16[8,128,128]{2,1,0:T(8,128)(2,1)S(1)}, bf16[8,128,128]{2,1,0:T(8,128)(2,1)S(1)}, bf16[128,768]{1,0:T(8,128)(2,1)S(1)}, bf16[128,768]{1,0:T(8,128)...) custom-call(s32[2,4]{1,0:T(2,128)} %refs_0_.3, ...), custom_call_target="tpu_custom_call" | custom-call | flops 452984832 | bytes 786432 | tf_op jit(solution)/shard_map/begin/pallas_call | solution.py:639
  26.5 0.0 collective-permute-done.5.refs_6_
  26.5 0.4 collective-permute-done.6.refs_7_
  26.9 3.1 %finish.1 = (bf16[4,128,128]{2,1,0:T(8,128)(2,1)S(1)}, bf16[4,128,128]{2,1,0:T(8,128)(2,1)S(1)}, bf16[4,128,128]{2,1,0:T(8,128)(2,1)S(1)}, bf16[4,128,128]{2,1,0...) custom-call(bf16[4,128,128]{2,1,0:T(8,128)(2,1)S(1)} %collective-per, ...), custom_call_target="tpu_custom_call" | custom-call | flops 1426063360 | bytes 2097152 | tf_op jit(solution)/shard_map/finish/pallas_call | solution.py:653
  30.0 1.3 %collective-permute-start.7 = (bf16[4,128,128]{2,1,0:T(8,128)(2,1)S(1)}, bf16[4,128,128]{2,1,0:T(8,128)(2,1)S(1)}, u32[]{:S(2)}, u32[]{:S(2)}) collective-permute-start(bf16[4,128,128]{2,1,0:T(8,128)(2,1)S(1)} %get-tuple-element.44), channel_id=1, source_target_pairs={{10,0},{11,1},{14,4},{3,9},{6,12},{7,13},{8,2},{9,3},{12,6},{1,11}... | collective-permute-start | bytes 393224 | tf_op jit(solution)/shard_map/ppermute | solution.py:607
  31.3 1.3 %collective-permute-start.8 = (bf16[4,128,128]{2,1,0:T(8,128)(2,1)S(1)}, bf16[4,128,128]{2,1,0:T(8,128)(2,1)S(1)}, u32[]{:S(2)}, u32[]{:S(2)}) collective-permute-start(bf16[4,128,128]{2,1,0:T(8,128)(2,1)S(1)} %get-tuple-element.45), channel_id=1, source_target_pairs={{8,0},{9,1},{12,4},{1,9},{4,12},{5,13},{10,2},{11,3},{14,6},{3,11}... | collective-permute-start | bytes 393224 | tf_op jit(solution)/shard_map/ppermute | solution.py:607
  32.6 6.5 %collective-permute-start.9 = (bf16[4,128,128]{2,1,0:T(8,128)(2,1)S(1)}, bf16[4,128,128]{2,1,0:T(8,128)(2,1)S(1)}, u32[]{:S(2)}, u32[]{:S(2)}) collective-permute-start(bf16[4,128,128]{2,1,0:T(8,128)(2,1)S(1)} %get-tuple-element.46), channel_id=1, source_target_pairs={{14,0},{7,1},{10,4},{3,5},{6,8},{11,13},{12,2},{5,3},{8,6},{1,7},{... | collective-permute-start | bytes 393224 | tf_op jit(solution)/shard_map/ppermute | solution.py:607
  39.2 2.4 %collective-permute-start.10 = (bf16[4,128,128]{2,1,0:T(8,128)(2,1)S(1)}, bf16[4,128,128]{2,1,0:T(8,128)(2,1)S(1)}, u32[]{:S(2)}, u32[]{:S(2)}) collective-permute-start(bf16[4,128,128]{2,1,0:T(8,128)(2,1)S(1)} %get-tuple-element.47), channel_id=1, source_target_pairs={{6,0},{11,5},{14,8},{7,9},{10,12},{3,13},{4,2},{9,7},{12,10},{5,11... | collective-permute-start | bytes 393224 | tf_op jit(solution)/shard_map/ppermute | solution.py:607
  41.6 1.9 %collective-permute-start.11 = (bf16[4,128,128]{2,1,0:T(8,128)(2,1)S(1)}, bf16[4,128,128]{2,1,0:T(8,128)(2,1)S(1)}, u32[]{:S(2)}, u32[]{:S(2)}) collective-permute-start(bf16[4,128,128]{2,1,0:T(8,128)(2,1)S(1)} %get-tuple-element.48), channel_id=1, source_target_pairs={{12,0},{5,1},{8,4},{1,5},{4,8},{9,13},{14,2},{7,3},{10,6},{3,7},{6... | collective-permute-start | bytes 393224 | tf_op jit(solution)/shard_map/ppermute | solution.py:607
  43.5 0.0 collective-permute-done.7.refs_0_
  43.5 3.7 %collective-permute-start.12 = (bf16[4,128,128]{2,1,0:T(8,128)(2,1)S(1)}, bf16[4,128,128]{2,1,0:T(8,128)(2,1)S(1)}, u32[]{:S(2)}, u32[]{:S(2)}) collective-permute-start(bf16[4,128,128]{2,1,0:T(8,128)(2,1)S(1)} %get-tuple-element.49), channel_id=1, source_target_pairs={{4,0},{9,5},{12,8},{5,9},{8,12},{1,13},{6,2},{11,7},{14,10},{7,11}... | collective-permute-start | bytes 393224 | tf_op jit(solution)/shard_map/ppermute | solution.py:607
  47.3 0.0 collective-permute-done.8.refs_1_
  47.3 2.4 %collective-permute-start.13 = (bf16[4,128,128]{2,1,0:T(8,128)(2,1)S(1)}, bf16[4,128,128]{2,1,0:T(8,128)(2,1)S(1)}, u32[]{:S(2)}, u32[]{:S(2)}) collective-permute-start(bf16[4,128,128]{2,1,0:T(8,128)(2,1)S(1)} %get-tuple-element.50), channel_id=1, source_target_pairs={{3,1},{6,4},{7,5},{10,8},{11,9},{14,12},{1,3},{4,6},{5,7},{8,10},{... | collective-permute-start | bytes 393224 | tf_op jit(solution)/shard_map/ppermute | solution.py:607
  49.7 0.0 collective-permute-done.9.refs_2_
  49.8 0.0 collective-permute-done.10.refs_3_
  49.8 0.0 collective-permute-done.11.refs_4_
  49.8 0.6 %collective-permute-done.12.refs_5_ = bf16[4,128,128]{2,1,0:T(8,128)(2,1)S(1)} collective-permute-done((bf16[4,128,128]{2,1,0:T(8,128)(2,1)S(1)}, bf16[4,128,128]{2,1,0:T(8,128)(2,1)S(1)}, u32[]{:S(2)}, u32[]{:S(2)}) %collective-permute-start.12) | collective-permute-done | bytes 131104 | tf_op jit(solution)/shard_map/ppermute | solution.py:607
  50.4 3.7 %collective-permute-done.13.refs_6_ = bf16[4,128,128]{2,1,0:T(8,128)(2,1)S(1)} collective-permute-done((bf16[4,128,128]{2,1,0:T(8,128)(2,1)S(1)}, bf16[4,128,128]{2,1,0:T(8,128)(2,1)S(1)}, u32[]{:S(2)}, u32[]{:S(2)}) %collective-permute-start.13) | collective-permute-done | bytes 131104 | tf_op jit(solution)/shard_map/ppermute | solution.py:607
  54.2 1.0 %unpack.1 = (bf16[1,1,128,768]{3,2,1,0:T(8,128)(2,1)}, bf16[1,1,128,768]{3,2,1,0:T(8,128)(2,1)}, bf16[1,1,128,768]{3,2,1,0:T(8,128)(2,1)}, bf16[1,1,128,768]{3,2,1,0:T(8,128)(2,1)}) custom-call(bf16[4,128,128]{2,1,0:T(8,128)(2,1)S(1)} %collective-permute-done.7.refs_0_, bf16[4,128,128]{2,1,0:T(8,128)(2,1)S(1)} %collective-permute-done.8.refs_1_, ...), custom_call_target="tpu_custom_call" | custom-call | tf_op jit(solution)/shard_map/unpack/pallas_call | solution.py:676
Async XLA Ops:
  1.9 14.4 %collective-permute-start = (bf16[4,128,128]{2,1,0:T(8,128)(2,1)S(1)}, bf16[4,128,128]{2,1,0:T(8,128)(2,1)S(1)}, u32[]{:S(2)}, u32[]{:S(2)}) collective-permute-start(bf16[4,128,128]{2,1,0:T(8,128)(2,1)S(1)} %get-tuple-element.28), channel_id=1, source_target_pairs={{0,10},{1,11},{4,14},{9,3},{12,6},{13,7},{2,8},{3,9},{6,12},{11,1}... | collective-permute-start | bytes 393224 | tf_op jit(solution)/shard_map/ppermute | solution.py:607
  3.2 16.8 %collective-permute-start.1 = (bf16[4,128,128]{2,1,0:T(8,128)(2,1)S(1)}, bf16[4,128,128]{2,1,0:T(8,128)(2,1)S(1)}, u32[]{:S(2)}, u32[]{:S(2)}) collective-permute-start(bf16[4,128,128]{2,1,0:T(8,128)(2,1)S(1)} %get-tuple-element.29), channel_id=1, source_target_pairs={{0,8},{1,9},{4,12},{9,1},{12,4},{13,5},{2,10},{3,11},{6,14},{11,3}... | collective-permute-start | bytes 393224 | tf_op jit(solution)/shard_map/ppermute | solution.py:607
  4.5 18.0 %collective-permute-start.2 = (bf16[4,128,128]{2,1,0:T(8,128)(2,1)S(1)}, bf16[4,128,128]{2,1,0:T(8,128)(2,1)S(1)}, u32[]{:S(2)}, u32[]{:S(2)}) collective-permute-start(bf16[4,128,128]{2,1,0:T(8,128)(2,1)S(1)} %get-tuple-element.30), channel_id=1, source_target_pairs={{0,14},{1,7},{4,10},{5,3},{8,6},{13,11},{2,12},{3,5},{6,8},{7,1},{... | collective-permute-start | bytes 393224 | tf_op jit(solution)/shard_map/ppermute | solution.py:607
  12.0 10.6 %collective-permute-start.3 = (bf16[4,128,128]{2,1,0:T(8,128)(2,1)S(1)}, bf16[4,128,128]{2,1,0:T(8,128)(2,1)S(1)}, u32[]{:S(2)}, u32[]{:S(2)}) collective-permute-start(bf16[4,128,128]{2,1,0:T(8,128)(2,1)S(1)} %get-tuple-element.31), channel_id=1, source_target_pairs={{0,6},{5,11},{8,14},{9,7},{12,10},{13,3},{2,4},{7,9},{10,12},{11,5... | collective-permute-start | bytes 393224 | tf_op jit(solution)/shard_map/ppermute | solution.py:607
  14.4 10.6 %collective-permute-start.4 = (bf16[4,128,128]{2,1,0:T(8,128)(2,1)S(1)}, bf16[4,128,128]{2,1,0:T(8,128)(2,1)S(1)}, u32[]{:S(2)}, u32[]{:S(2)}) collective-permute-start(bf16[4,128,128]{2,1,0:T(8,128)(2,1)S(1)} %get-tuple-element.32), channel_id=1, source_target_pairs={{0,12},{1,5},{4,8},{5,1},{8,4},{13,9},{2,14},{3,7},{6,10},{7,3},{1... | collective-permute-start | bytes 393224 | tf_op jit(solution)/shard_map/ppermute | solution.py:607
  16.3 10.2 %collective-permute-start.5 = (bf16[4,128,128]{2,1,0:T(8,128)(2,1)S(1)}, bf16[4,128,128]{2,1,0:T(8,128)(2,1)S(1)}, u32[]{:S(2)}, u32[]{:S(2)}) collective-permute-start(bf16[4,128,128]{2,1,0:T(8,128)(2,1)S(1)} %get-tuple-element.34), channel_id=1, source_target_pairs={{0,4},{5,9},{8,12},{9,5},{12,8},{13,1},{2,6},{7,11},{10,14},{11,7}... | collective-permute-start | bytes 393224 | tf_op jit(solution)/shard_map/ppermute | solution.py:607
  20.1 6.9 %collective-permute-start.6 = (bf16[4,128,128]{2,1,0:T(8,128)(2,1)S(1)}, bf16[4,128,128]{2,1,0:T(8,128)(2,1)S(1)}, u32[]{:S(2)}, u32[]{:S(2)}) collective-permute-start(bf16[4,128,128]{2,1,0:T(8,128)(2,1)S(1)} %get-tuple-element.35), channel_id=1, source_target_pairs={{1,3},{4,6},{5,7},{8,10},{9,11},{12,14},{3,1},{6,4},{7,5},{10,8},{... | collective-permute-start | bytes 393224 | tf_op jit(solution)/shard_map/ppermute | solution.py:607
  30.0 13.5 %collective-permute-start.7 = (bf16[4,128,128]{2,1,0:T(8,128)(2,1)S(1)}, bf16[4,128,128]{2,1,0:T(8,128)(2,1)S(1)}, u32[]{:S(2)}, u32[]{:S(2)}) collective-permute-start(bf16[4,128,128]{2,1,0:T(8,128)(2,1)S(1)} %get-tuple-element.44), channel_id=1, source_target_pairs={{10,0},{11,1},{14,4},{3,9},{6,12},{7,13},{8,2},{9,3},{12,6},{1,11}... | collective-permute-start | bytes 393224 | tf_op jit(solution)/shard_map/ppermute | solution.py:607
  31.3 16.0 %collective-permute-start.8 = (bf16[4,128,128]{2,1,0:T(8,128)(2,1)S(1)}, bf16[4,128,128]{2,1,0:T(8,128)(2,1)S(1)}, u32[]{:S(2)}, u32[]{:S(2)}) collective-permute-start(bf16[4,128,128]{2,1,0:T(8,128)(2,1)S(1)} %get-tuple-element.45), channel_id=1, source_target_pairs={{8,0},{9,1},{12,4},{1,9},{4,12},{5,13},{10,2},{11,3},{14,6},{3,11}... | collective-permute-start | bytes 393224 | tf_op jit(solution)/shard_map/ppermute | solution.py:607
  32.6 17.1 %collective-permute-start.9 = (bf16[4,128,128]{2,1,0:T(8,128)(2,1)S(1)}, bf16[4,128,128]{2,1,0:T(8,128)(2,1)S(1)}, u32[]{:S(2)}, u32[]{:S(2)}) collective-permute-start(bf16[4,128,128]{2,1,0:T(8,128)(2,1)S(1)} %get-tuple-element.46), channel_id=1, source_target_pairs={{14,0},{7,1},{10,4},{3,5},{6,8},{11,13},{12,2},{5,3},{8,6},{1,7},{... | collective-permute-start | bytes 393224 | tf_op jit(solution)/shard_map/ppermute | solution.py:607
  39.2 10.6 %collective-permute-start.10 = (bf16[4,128,128]{2,1,0:T(8,128)(2,1)S(1)}, bf16[4,128,128]{2,1,0:T(8,128)(2,1)S(1)}, u32[]{:S(2)}, u32[]{:S(2)}) collective-permute-start(bf16[4,128,128]{2,1,0:T(8,128)(2,1)S(1)} %get-tuple-element.47), channel_id=1, source_target_pairs={{6,0},{11,5},{14,8},{7,9},{10,12},{3,13},{4,2},{9,7},{12,10},{5,11... | collective-permute-start | bytes 393224 | tf_op jit(solution)/shard_map/ppermute | solution.py:607
  41.6 8.2 %collective-permute-start.11 = (bf16[4,128,128]{2,1,0:T(8,128)(2,1)S(1)}, bf16[4,128,128]{2,1,0:T(8,128)(2,1)S(1)}, u32[]{:S(2)}, u32[]{:S(2)}) collective-permute-start(bf16[4,128,128]{2,1,0:T(8,128)(2,1)S(1)} %get-tuple-element.48), channel_id=1, source_target_pairs={{12,0},{5,1},{8,4},{1,5},{4,8},{9,13},{14,2},{7,3},{10,6},{3,7},{6... | collective-permute-start | bytes 393224 | tf_op jit(solution)/shard_map/ppermute | solution.py:607
  43.5 6.9 %collective-permute-start.12 = (bf16[4,128,128]{2,1,0:T(8,128)(2,1)S(1)}, bf16[4,128,128]{2,1,0:T(8,128)(2,1)S(1)}, u32[]{:S(2)}, u32[]{:S(2)}) collective-permute-start(bf16[4,128,128]{2,1,0:T(8,128)(2,1)S(1)} %get-tuple-element.49), channel_id=1, source_target_pairs={{4,0},{9,5},{12,8},{5,9},{8,12},{1,13},{6,2},{11,7},{14,10},{7,11}... | collective-permute-start | bytes 393224 | tf_op jit(solution)/shard_map/ppermute | solution.py:607
  47.3 6.9 %collective-permute-start.13 = (bf16[4,128,128]{2,1,0:T(8,128)(2,1)S(1)}, bf16[4,128,128]{2,1,0:T(8,128)(2,1)S(1)}, u32[]{:S(2)}, u32[]{:S(2)}) collective-permute-start(bf16[4,128,128]{2,1,0:T(8,128)(2,1)S(1)} %get-tuple-element.50), channel_id=1, source_target_pairs={{3,1},{6,4},{7,5},{10,8},{11,9},{14,12},{1,3},{4,6},{5,7},{8,10},{... | collective-permute-start | bytes 393224 | tf_op jit(solution)/shard_map/ppermute | solution.py:607

commit v4 on v3

--- a/solution.py
+++ b/solution.py
@@ -601,7 +601,7 @@
         moves = list(range(tiles - 1))
         if back:
             full, mixed, along = moves[:lat], moves[lat : 1 - lat], moves[1 - lat :]
-            moves = full + mixed[::2] + mixed[1::2] + along
+            moves = full + along + mixed[::2] + mixed[1::2]
         found = list(blocks)
         for n in moves:
             found[n] = lax.ppermute(found[n], axes, routes(n, lat, lon, cores, heads, back))

time: 55.7 us -> 55.7 us (level)
  no operation moved by 1% of the time
where the time goes in v4:
time: 55.7 us; the launch traced here: 55.2 us
  starting transfers between devices  40.2 us (72%)
  waiting for transfers between devices  7.23 us (13%)
  Pallas kernels  6.96 us (12%)
  between operations  0.84 us (2%)
    ppermute x14, starting transfers between devices, sent(): lax.ppermute(found[n], axes, routes(n, lat, lon, cores, heads, back))  40.2 us
    ppermute x14, waiting for transfers between devices, sent(): lax.ppermute(found[n], axes, routes(n, lat, lon, cores, heads, back))  7.23 us
    pallas_call x1, Pallas kernels, by_heads(): pl.pallas_call(functools.partial(finish_kernel, lat, lon, times), out_sha...  3.08 us
    pallas_call x1, Pallas kernels, by_heads(): pl.pallas_call(functools.partial(begin_kernel, lat, lon, times), out_shap...  1.54 us
    pallas_call x1, Pallas kernels, by_heads(): pl.pallas_call(functools.partial(pack_kernel, lat, lon, heads), out_shape...  1.3 us
  transfers between devices with their start and end apart: 14, of which 4 were waited for; matrix products, arithmetic and copies ran while one was open for 0% of the time, Pallas kernels for 3%

profile of v4, /device:TPU:20, one launch (start us, length us, event | category | flops | bytes accessed | tf_op | source)
XLA Modules:
  0.0 55.2 jit_solution(16232695728467991902)
XLA Ops:
  0.6 1.3 %pack.1 = (bf16[4,128,128]{2,1,0:T(8,128)(2,1)S(1)}, bf16[4,128,128]{2,1,0:T(8,128)(2,1)S(1)}, bf16[4,128,128]{2,1,0:T(8,128)(2,1)S(1)}, bf16[4,128,128]{2,1,0:T...) custom-call(bf16[1,1,128,768]{3,2,1,0:T(8,128)(2,1)} %refs_0_.2, ...), custom_call_target="tpu_custom_call" | custom-call | tf_op jit(solution)/shard_map/pack/pallas_call | solution.py:613
  1.9 1.3 %collective-permute-start = (bf16[4,128,128]{2,1,0:T(8,128)(2,1)S(1)}, bf16[4,128,128]{2,1,0:T(8,128)(2,1)S(1)}, u32[]{:S(2)}, u32[]{:S(2)}) collective-permute-start(bf16[4,128,128]{2,1,0:T(8,128)(2,1)S(1)} %get-tuple-element.28), channel_id=1, source_target_pairs={{0,10},{1,11},{4,14},{9,3},{12,6},{13,7},{2,8},{3,9},{6,12},{11,1}... | collective-permute-start | bytes 393224 | tf_op jit(solution)/shard_map/ppermute | solution.py:607
  3.2 1.3 %collective-permute-start.1 = (bf16[4,128,128]{2,1,0:T(8,128)(2,1)S(1)}, bf16[4,128,128]{2,1,0:T(8,128)(2,1)S(1)}, u32[]{:S(2)}, u32[]{:S(2)}) collective-permute-start(bf16[4,128,128]{2,1,0:T(8,128)(2,1)S(1)} %get-tuple-element.29), channel_id=1, source_target_pairs={{0,8},{1,9},{4,12},{9,1},{12,4},{13,5},{2,10},{3,11},{6,14},{11,3}... | collective-permute-start | bytes 393224 | tf_op jit(solution)/shard_map/ppermute | solution.py:607
  4.5 7.4 %collective-permute-start.2 = (bf16[4,128,128]{2,1,0:T(8,128)(2,1)S(1)}, bf16[4,128,128]{2,1,0:T(8,128)(2,1)S(1)}, u32[]{:S(2)}, u32[]{:S(2)}) collective-permute-start(bf16[4,128,128]{2,1,0:T(8,128)(2,1)S(1)} %get-tuple-element.30), channel_id=1, source_target_pairs={{0,14},{1,7},{4,10},{5,3},{8,6},{13,11},{2,12},{3,5},{6,8},{7,1},{... | collective-permute-start | bytes 393224 | tf_op jit(solution)/shard_map/ppermute | solution.py:607
  12.0 2.4 %collective-permute-start.3 = (bf16[4,128,128]{2,1,0:T(8,128)(2,1)S(1)}, bf16[4,128,128]{2,1,0:T(8,128)(2,1)S(1)}, u32[]{:S(2)}, u32[]{:S(2)}) collective-permute-start(bf16[4,128,128]{2,1,0:T(8,128)(2,1)S(1)} %get-tuple-element.31), channel_id=1, source_target_pairs={{0,6},{5,11},{8,14},{9,7},{12,10},{13,3},{2,4},{7,9},{10,12},{11,5... | collective-permute-start | bytes 393224 | tf_op jit(solution)/shard_map/ppermute | solution.py:607
  14.4 1.9 %collective-permute-start.4 = (bf16[4,128,128]{2,1,0:T(8,128)(2,1)S(1)}, bf16[4,128,128]{2,1,0:T(8,128)(2,1)S(1)}, u32[]{:S(2)}, u32[]{:S(2)}) collective-permute-start(bf16[4,128,128]{2,1,0:T(8,128)(2,1)S(1)} %get-tuple-element.32), channel_id=1, source_target_pairs={{0,12},{1,5},{4,8},{5,1},{8,4},{13,9},{2,14},{3,7},{6,10},{7,3},{1... | collective-permute-start | bytes 393224 | tf_op jit(solution)/shard_map/ppermute | solution.py:607
  16.3 0.0 collective-permute-done.refs_1_.refs_0_
  16.3 3.7 %collective-permute-start.5 = (bf16[4,128,128]{2,1,0:T(8,128)(2,1)S(1)}, bf16[4,128,128]{2,1,0:T(8,128)(2,1)S(1)}, u32[]{:S(2)}, u32[]{:S(2)}) collective-permute-start(bf16[4,128,128]{2,1,0:T(8,128)(2,1)S(1)} %get-tuple-element.34), channel_id=1, source_target_pairs={{0,4},{5,9},{8,12},{9,5},{12,8},{13,1},{2,6},{7,11},{10,14},{11,7}... | collective-permute-start | bytes 393224 | tf_op jit(solution)/shard_map/ppermute | solution.py:607
  20.1 0.0 collective-permute-done.1.refs_2_.refs_1_
  20.1 2.4 %collective-permute-start.6 = (bf16[4,128,128]{2,1,0:T(8,128)(2,1)S(1)}, bf16[4,128,128]{2,1,0:T(8,128)(2,1)S(1)}, u32[]{:S(2)}, u32[]{:S(2)}) collective-permute-start(bf16[4,128,128]{2,1,0:T(8,128)(2,1)S(1)} %get-tuple-element.35), channel_id=1, source_target_pairs={{1,3},{4,6},{5,7},{8,10},{9,11},{12,14},{3,1},{6,4},{7,5},{10,8},{... | collective-permute-start | bytes 393224 | tf_op jit(solution)/shard_map/ppermute | solution.py:607
  22.5 0.0 collective-permute-done.2.refs_3_.refs_2_
  22.5 0.0 collective-permute-done.3.refs_4_.refs_3_
  22.6 2.4 %collective-permute-done.4.refs_5_.refs_4_ = bf16[4,128,128]{2,1,0:T(8,128)(2,1)S(1)} collective-permute-done((bf16[4,128,128]{2,1,0:T(8,128)(2,1)S(1)}, bf16[4,128,128]{2,1,0:T(8,128)(2,1)S(1)}, u32[]{:S(2)}, u32[]{:S(2)}) %collective-permute-start.4) | collective-permute-done | bytes 131104 | tf_op jit(solution)/shard_map/ppermute | solution.py:607
  25.0 1.5 %begin.1 = (bf16[8,128,128]{2,1,0:T(8,128)(2,1)S(1)}, bf16[8,128,128]{2,1,0:T(8,128)(2,1)S(1)}, bf16[128,768]{1,0:T(8,128)(2,1)S(1)}, bf16[128,768]{1,0:T(8,128)...) custom-call(s32[2,4]{1,0:T(2,128)} %refs_0_.3, ...), custom_call_target="tpu_custom_call" | custom-call | flops 452984832 | bytes 786432 | tf_op jit(solution)/shard_map/begin/pallas_call | solution.py:639
  26.5 0.0 collective-permute-done.5.refs_6_
  26.5 0.4 collective-permute-done.6.refs_7_
  26.9 3.1 %finish.1 = (bf16[4,128,128]{2,1,0:T(8,128)(2,1)S(1)}, bf16[4,128,128]{2,1,0:T(8,128)(2,1)S(1)}, bf16[4,128,128]{2,1,0:T(8,128)(2,1)S(1)}, bf16[4,128,128]{2,1,0...) custom-call(bf16[4,128,128]{2,1,0:T(8,128)(2,1)S(1)} %collective-per, ...), custom_call_target="tpu_custom_call" | custom-call | flops 1426063360 | bytes 2097152 | tf_op jit(solution)/shard_map/finish/pallas_call | solution.py:653
  30.0 1.3 %collective-permute-start.7 = (bf16[4,128,128]{2,1,0:T(8,128)(2,1)S(1)}, bf16[4,128,128]{2,1,0:T(8,128)(2,1)S(1)}, u32[]{:S(2)}, u32[]{:S(2)}) collective-permute-start(bf16[4,128,128]{2,1,0:T(8,128)(2,1)S(1)} %get-tuple-element.44), channel_id=1, source_target_pairs={{10,0},{11,1},{14,4},{3,9},{6,12},{7,13},{8,2},{9,3},{12,6},{1,11}... | collective-permute-start | bytes 393224 | tf_op jit(solution)/shard_map/ppermute | solution.py:607
  31.3 1.3 %collective-permute-start.8 = (bf16[4,128,128]{2,1,0:T(8,128)(2,1)S(1)}, bf16[4,128,128]{2,1,0:T(8,128)(2,1)S(1)}, u32[]{:S(2)}, u32[]{:S(2)}) collective-permute-start(bf16[4,128,128]{2,1,0:T(8,128)(2,1)S(1)} %get-tuple-element.45), channel_id=1, source_target_pairs={{8,0},{9,1},{12,4},{1,9},{4,12},{5,13},{10,2},{11,3},{14,6},{3,11}... | collective-permute-start | bytes 393224 | tf_op jit(solution)/shard_map/ppermute | solution.py:607
  32.6 6.5 %collective-permute-start.9 = (bf16[4,128,128]{2,1,0:T(8,128)(2,1)S(1)}, bf16[4,128,128]{2,1,0:T(8,128)(2,1)S(1)}, u32[]{:S(2)}, u32[]{:S(2)}) collective-permute-start(bf16[4,128,128]{2,1,0:T(8,128)(2,1)S(1)} %get-tuple-element.46), channel_id=1, source_target_pairs={{14,0},{7,1},{10,4},{3,5},{6,8},{11,13},{12,2},{5,3},{8,6},{1,7},{... | collective-permute-start | bytes 393224 | tf_op jit(solution)/shard_map/ppermute | solution.py:607
  39.2 2.4 %collective-permute-start.10 = (bf16[4,128,128]{2,1,0:T(8,128)(2,1)S(1)}, bf16[4,128,128]{2,1,0:T(8,128)(2,1)S(1)}, u32[]{:S(2)}, u32[]{:S(2)}) collective-permute-start(bf16[4,128,128]{2,1,0:T(8,128)(2,1)S(1)} %get-tuple-element.47), channel_id=1, source_target_pairs={{6,0},{11,5},{14,8},{7,9},{10,12},{3,13},{4,2},{9,7},{12,10},{5,11... | collective-permute-start | bytes 393224 | tf_op jit(solution)/shard_map/ppermute | solution.py:607
  41.6 1.9 %collective-permute-start.11 = (bf16[4,128,128]{2,1,0:T(8,128)(2,1)S(1)}, bf16[4,128,128]{2,1,0:T(8,128)(2,1)S(1)}, u32[]{:S(2)}, u32[]{:S(2)}) collective-permute-start(bf16[4,128,128]{2,1,0:T(8,128)(2,1)S(1)} %get-tuple-element.48), channel_id=1, source_target_pairs={{12,0},{5,1},{8,4},{1,5},{4,8},{9,13},{14,2},{7,3},{10,6},{3,7},{6... | collective-permute-start | bytes 393224 | tf_op jit(solution)/shard_map/ppermute | solution.py:607
  43.5 0.0 collective-permute-done.7.refs_0_
  43.5 3.7 %collective-permute-start.12 = (bf16[4,128,128]{2,1,0:T(8,128)(2,1)S(1)}, bf16[4,128,128]{2,1,0:T(8,128)(2,1)S(1)}, u32[]{:S(2)}, u32[]{:S(2)}) collective-permute-start(bf16[4,128,128]{2,1,0:T(8,128)(2,1)S(1)} %get-tuple-element.49), channel_id=1, source_target_pairs={{4,0},{9,5},{12,8},{5,9},{8,12},{1,13},{6,2},{11,7},{14,10},{7,11}... | collective-permute-start | bytes 393224 | tf_op jit(solution)/shard_map/ppermute | solution.py:607
  47.3 0.0 collective-permute-done.8.refs_1_
  47.3 2.4 %collective-permute-start.13 = (bf16[4,128,128]{2,1,0:T(8,128)(2,1)S(1)}, bf16[4,128,128]{2,1,0:T(8,128)(2,1)S(1)}, u32[]{:S(2)}, u32[]{:S(2)}) collective-permute-start(bf16[4,128,128]{2,1,0:T(8,128)(2,1)S(1)} %get-tuple-element.50), channel_id=1, source_target_pairs={{3,1},{6,4},{7,5},{10,8},{11,9},{14,12},{1,3},{4,6},{5,7},{8,10},{... | collective-permute-start | bytes 393224 | tf_op jit(solution)/shard_map/ppermute | solution.py:607
  49.7 0.0 collective-permute-done.9.refs_2_
  49.8 0.0 collective-permute-done.10.refs_3_
  49.8 0.0 collective-permute-done.11.refs_4_
  49.8 0.6 %collective-permute-done.12.refs_5_ = bf16[4,128,128]{2,1,0:T(8,128)(2,1)S(1)} collective-permute-done((bf16[4,128,128]{2,1,0:T(8,128)(2,1)S(1)}, bf16[4,128,128]{2,1,0:T(8,128)(2,1)S(1)}, u32[]{:S(2)}, u32[]{:S(2)}) %collective-permute-start.12) | collective-permute-done | bytes 131104 | tf_op jit(solution)/shard_map/ppermute | solution.py:607
  50.4 3.7 %collective-permute-done.13.refs_6_ = bf16[4,128,128]{2,1,0:T(8,128)(2,1)S(1)} collective-permute-done((bf16[4,128,128]{2,1,0:T(8,128)(2,1)S(1)}, bf16[4,128,128]{2,1,0:T(8,128)(2,1)S(1)}, u32[]{:S(2)}, u32[]{:S(2)}) %collective-permute-start.13) | collective-permute-done | bytes 131104 | tf_op jit(solution)/shard_map/ppermute | solution.py:607
  54.2 1.0 %unpack.1 = (bf16[1,1,128,768]{3,2,1,0:T(8,128)(2,1)}, bf16[1,1,128,768]{3,2,1,0:T(8,128)(2,1)}, bf16[1,1,128,768]{3,2,1,0:T(8,128)(2,1)}, bf16[1,1,128,768]{3,2,1,0:T(8,128)(2,1)}) custom-call(bf16[4,128,128]{2,1,0:T(8,128)(2,1)S(1)} %collective-permute-done.7.refs_0_, bf16[4,128,128]{2,1,0:T(8,128)(2,1)S(1)} %collective-permute-done.8.refs_1_, ...), custom_call_target="tpu_custom_call" | custom-call | tf_op jit(solution)/shard_map/unpack/pallas_call | solution.py:676
Async XLA Ops:
  1.9 14.4 %collective-permute-start = (bf16[4,128,128]{2,1,0:T(8,128)(2,1)S(1)}, bf16[4,128,128]{2,1,0:T(8,128)(2,1)S(1)}, u32[]{:S(2)}, u32[]{:S(2)}) collective-permute-start(bf16[4,128,128]{2,1,0:T(8,128)(2,1)S(1)} %get-tuple-element.28), channel_id=1, source_target_pairs={{0,10},{1,11},{4,14},{9,3},{12,6},{13,7},{2,8},{3,9},{6,12},{11,1}... | collective-permute-start | bytes 393224 | tf_op jit(solution)/shard_map/ppermute | solution.py:607
  3.2 16.8 %collective-permute-start.1 = (bf16[4,128,128]{2,1,0:T(8,128)(2,1)S(1)}, bf16[4,128,128]{2,1,0:T(8,128)(2,1)S(1)}, u32[]{:S(2)}, u32[]{:S(2)}) collective-permute-start(bf16[4,128,128]{2,1,0:T(8,128)(2,1)S(1)} %get-tuple-element.29), channel_id=1, source_target_pairs={{0,8},{1,9},{4,12},{9,1},{12,4},{13,5},{2,10},{3,11},{6,14},{11,3}... | collective-permute-start | bytes 393224 | tf_op jit(solution)/shard_map/ppermute | solution.py:607
  4.5 18.0 %collective-permute-start.2 = (bf16[4,128,128]{2,1,0:T(8,128)(2,1)S(1)}, bf16[4,128,128]{2,1,0:T(8,128)(2,1)S(1)}, u32[]{:S(2)}, u32[]{:S(2)}) collective-permute-start(bf16[4,128,128]{2,1,0:T(8,128)(2,1)S(1)} %get-tuple-element.30), channel_id=1, source_target_pairs={{0,14},{1,7},{4,10},{5,3},{8,6},{13,11},{2,12},{3,5},{6,8},{7,1},{... | collective-permute-start | bytes 393224 | tf_op jit(solution)/shard_map/ppermute | solution.py:607
  12.0 10.6 %collective-permute-start.3 = (bf16[4,128,128]{2,1,0:T(8,128)(2,1)S(1)}, bf16[4,128,128]{2,1,0:T(8,128)(2,1)S(1)}, u32[]{:S(2)}, u32[]{:S(2)}) collective-permute-start(bf16[4,128,128]{2,1,0:T(8,128)(2,1)S(1)} %get-tuple-element.31), channel_id=1, source_target_pairs={{0,6},{5,11},{8,14},{9,7},{12,10},{13,3},{2,4},{7,9},{10,12},{11,5... | collective-permute-start | bytes 393224 | tf_op jit(solution)/shard_map/ppermute | solution.py:607
  14.4 10.6 %collective-permute-start.4 = (bf16[4,128,128]{2,1,0:T(8,128)(2,1)S(1)}, bf16[4,128,128]{2,1,0:T(8,128)(2,1)S(1)}, u32[]{:S(2)}, u32[]{:S(2)}) collective-permute-start(bf16[4,128,128]{2,1,0:T(8,128)(2,1)S(1)} %get-tuple-element.32), channel_id=1, source_target_pairs={{0,12},{1,5},{4,8},{5,1},{8,4},{13,9},{2,14},{3,7},{6,10},{7,3},{1... | collective-permute-start | bytes 393224 | tf_op jit(solution)/shard_map/ppermute | solution.py:607
  16.3 10.2 %collective-permute-start.5 = (bf16[4,128,128]{2,1,0:T(8,128)(2,1)S(1)}, bf16[4,128,128]{2,1,0:T(8,128)(2,1)S(1)}, u32[]{:S(2)}, u32[]{:S(2)}) collective-permute-start(bf16[4,128,128]{2,1,0:T(8,128)(2,1)S(1)} %get-tuple-element.34), channel_id=1, source_target_pairs={{0,4},{5,9},{8,12},{9,5},{12,8},{13,1},{2,6},{7,11},{10,14},{11,7}... | collective-permute-start | bytes 393224 | tf_op jit(solution)/shard_map/ppermute | solution.py:607
  20.1 6.9 %collective-permute-start.6 = (bf16[4,128,128]{2,1,0:T(8,128)(2,1)S(1)}, bf16[4,128,128]{2,1,0:T(8,128)(2,1)S(1)}, u32[]{:S(2)}, u32[]{:S(2)}) collective-permute-start(bf16[4,128,128]{2,1,0:T(8,128)(2,1)S(1)} %get-tuple-element.35), channel_id=1, source_target_pairs={{1,3},{4,6},{5,7},{8,10},{9,11},{12,14},{3,1},{6,4},{7,5},{10,8},{... | collective-permute-start | bytes 393224 | tf_op jit(solution)/shard_map/ppermute | solution.py:607
  30.0 13.5 %collective-permute-start.7 = (bf16[4,128,128]{2,1,0:T(8,128)(2,1)S(1)}, bf16[4,128,128]{2,1,0:T(8,128)(2,1)S(1)}, u32[]{:S(2)}, u32[]{:S(2)}) collective-permute-start(bf16[4,128,128]{2,1,0:T(8,128)(2,1)S(1)} %get-tuple-element.44), channel_id=1, source_target_pairs={{10,0},{11,1},{14,4},{3,9},{6,12},{7,13},{8,2},{9,3},{12,6},{1,11}... | collective-permute-start | bytes 393224 | tf_op jit(solution)/shard_map/ppermute | solution.py:607
  31.3 16.0 %collective-permute-start.8 = (bf16[4,128,128]{2,1,0:T(8,128)(2,1)S(1)}, bf16[4,128,128]{2,1,0:T(8,128)(2,1)S(1)}, u32[]{:S(2)}, u32[]{:S(2)}) collective-permute-start(bf16[4,128,128]{2,1,0:T(8,128)(2,1)S(1)} %get-tuple-element.45), channel_id=1, source_target_pairs={{8,0},{9,1},{12,4},{1,9},{4,12},{5,13},{10,2},{11,3},{14,6},{3,11}... | collective-permute-start | bytes 393224 | tf_op jit(solution)/shard_map/ppermute | solution.py:607
  32.6 17.1 %collective-permute-start.9 = (bf16[4,128,128]{2,1,0:T(8,128)(2,1)S(1)}, bf16[4,128,128]{2,1,0:T(8,128)(2,1)S(1)}, u32[]{:S(2)}, u32[]{:S(2)}) collective-permute-start(bf16[4,128,128]{2,1,0:T(8,128)(2,1)S(1)} %get-tuple-element.46), channel_id=1, source_target_pairs={{14,0},{7,1},{10,4},{3,5},{6,8},{11,13},{12,2},{5,3},{8,6},{1,7},{... | collective-permute-start | bytes 393224 | tf_op jit(solution)/shard_map/ppermute | solution.py:607
  39.2 10.6 %collective-permute-start.10 = (bf16[4,128,128]{2,1,0:T(8,128)(2,1)S(1)}, bf16[4,128,128]{2,1,0:T(8,128)(2,1)S(1)}, u32[]{:S(2)}, u32[]{:S(2)}) collective-permute-start(bf16[4,128,128]{2,1,0:T(8,128)(2,1)S(1)} %get-tuple-element.47), channel_id=1, source_target_pairs={{6,0},{11,5},{14,8},{7,9},{10,12},{3,13},{4,2},{9,7},{12,10},{5,11... | collective-permute-start | bytes 393224 | tf_op jit(solution)/shard_map/ppermute | solution.py:607
  41.6 8.2 %collective-permute-start.11 = (bf16[4,128,128]{2,1,0:T(8,128)(2,1)S(1)}, bf16[4,128,128]{2,1,0:T(8,128)(2,1)S(1)}, u32[]{:S(2)}, u32[]{:S(2)}) collective-permute-start(bf16[4,128,128]{2,1,0:T(8,128)(2,1)S(1)} %get-tuple-element.48), channel_id=1, source_target_pairs={{12,0},{5,1},{8,4},{1,5},{4,8},{9,13},{14,2},{7,3},{10,6},{3,7},{6... | collective-permute-start | bytes 393224 | tf_op jit(solution)/shard_map/ppermute | solution.py:607
  43.5 6.9 %collective-permute-start.12 = (bf16[4,128,128]{2,1,0:T(8,128)(2,1)S(1)}, bf16[4,128,128]{2,1,0:T(8,128)(2,1)S(1)}, u32[]{:S(2)}, u32[]{:S(2)}) collective-permute-start(bf16[4,128,128]{2,1,0:T(8,128)(2,1)S(1)} %get-tuple-element.49), channel_id=1, source_target_pairs={{4,0},{9,5},{12,8},{5,9},{8,12},{1,13},{6,2},{11,7},{14,10},{7,11}... | collective-permute-start | bytes 393224 | tf_op jit(solution)/shard_map/ppermute | solution.py:607
  47.3 6.9 %collective-permute-start.13 = (bf16[4,128,128]{2,1,0:T(8,128)(2,1)S(1)}, bf16[4,128,128]{2,1,0:T(8,128)(2,1)S(1)}, u32[]{:S(2)}, u32[]{:S(2)}) collective-permute-start(bf16[4,128,128]{2,1,0:T(8,128)(2,1)S(1)} %get-tuple-element.50), channel_id=1, source_target_pairs={{3,1},{6,4},{7,5},{10,8},{11,9},{14,12},{1,3},{4,6},{5,7},{8,10},{... | collective-permute-start | bytes 393224 | tf_op jit(solution)/shard_map/ppermute | solution.py:607

commit v5 on v3

--- a/solution.py
+++ b/solution.py
@@ -310,28 +310,18 @@
 def unpack_kernel(lat, lon, heads, *refs):
     blocks, tensors, whole, sems = refs[:-6], refs[-6:-2], refs[-2], refs[-1]
     row, col, core = (lax.axis_index(a) for a in ("lat", "lon", "head"))
-    parts = sems.shape[1]
-    size = whole.shape[1] // parts
     copies = []
-    for n in range(parts):
-        rows = slice(n * size, (n + 1) * size)
+    for t, tensor in enumerate(tensors):
         for m, block in enumerate(blocks):
             head, used = head_of(*partner(row, col, core, m, lat, lon), core, lat, lon, heads)
 
             @pl.when(used)
             def _():
                 features = pl.ds(pl.multiple_of(head * HD, HD), HD)
-                for t in range(4):
-                    whole[t, rows, features] = block[t, rows, :]
-
-        rows = pl.ds(n * size, size)
-        for t, tensor in enumerate(tensors):
-            copies.append(
-                pltpu.make_async_copy(
-                    whole.at[t, rows, :], tensor.at[0, 0, rows, :], sems.at[t, n]
-                )
-            )
-            copies[-1].start()
+                whole[t, :, features] = block[t]
+
+        copies.append(pltpu.make_async_copy(whole.at[t], tensor.at[0, 0], sems.at[t]))
+        copies[-1].start()
     for copy in copies:
         copy.wait()
 
@@ -680,7 +670,7 @@
             out_specs=[in_hbm] * 4,
             scratch_shapes=[
                 pltpu.VMEM((4, tile_len, width), low),
-                pltpu.SemaphoreType.DMA((4, 4)),
+                pltpu.SemaphoreType.DMA((4,)),
             ],
             compiler_params=small,
             name="unpack",

time: 55.7 us -> 55.6 us (level)
  no operation moved by 1% of the time
where the time goes in v5:
time: 55.6 us; the launch traced here: 55.1 us
  starting transfers between devices  40.2 us (72%)
  waiting for transfers between devices  7.23 us (13%)
  Pallas kernels  6.87 us (12%)
  between operations  0.84 us (2%)
    ppermute x14, starting transfers between devices, sent(): lax.ppermute(found[n], axes, routes(n, lat, lon, cores, heads, back))  40.2 us
    ppermute x14, waiting for transfers between devices, sent(): lax.ppermute(found[n], axes, routes(n, lat, lon, cores, heads, back))  7.23 us
    pallas_call x1, Pallas kernels, by_heads(): pl.pallas_call(functools.partial(finish_kernel, lat, lon, times), out_sha...  3.08 us
    pallas_call x1, Pallas kernels, by_heads(): pl.pallas_call(functools.partial(begin_kernel, lat, lon, times), out_shap...  1.54 us
    pallas_call x1, Pallas kernels, by_heads(): pl.pallas_call(functools.partial(pack_kernel, lat, lon, heads), out_shape...  1.3 us
  transfers between devices with their start and end apart: 14, of which 4 were waited for; matrix products, arithmetic and copies ran while one was open for 0% of the time, Pallas kernels for 3%

profile of v5, /device:TPU:20, one launch (start us, length us, event | category | flops | bytes accessed | tf_op | source)
XLA Modules:
  0.0 55.1 jit_solution(13553637264212266301)
XLA Ops:
  0.6 1.3 %pack.1 = (bf16[4,128,128]{2,1,0:T(8,128)(2,1)S(1)}, bf16[4,128,128]{2,1,0:T(8,128)(2,1)S(1)}, bf16[4,128,128]{2,1,0:T(8,128)(2,1)S(1)}, bf16[4,128,128]{2,1,0:T...) custom-call(bf16[1,1,128,768]{3,2,1,0:T(8,128)(2,1)} %refs_0_.2, ...), custom_call_target="tpu_custom_call" | custom-call | tf_op jit(solution)/shard_map/pack/pallas_call | solution.py:603
  1.9 1.3 %collective-permute-start = (bf16[4,128,128]{2,1,0:T(8,128)(2,1)S(1)}, bf16[4,128,128]{2,1,0:T(8,128)(2,1)S(1)}, u32[]{:S(2)}, u32[]{:S(2)}) collective-permute-start(bf16[4,128,128]{2,1,0:T(8,128)(2,1)S(1)} %get-tuple-element.28), channel_id=1, source_target_pairs={{0,10},{1,11},{4,14},{9,3},{12,6},{13,7},{2,8},{3,9},{6,12},{11,1}... | collective-permute-start | bytes 393224 | tf_op jit(solution)/shard_map/ppermute | solution.py:597
  3.2 1.3 %collective-permute-start.1 = (bf16[4,128,128]{2,1,0:T(8,128)(2,1)S(1)}, bf16[4,128,128]{2,1,0:T(8,128)(2,1)S(1)}, u32[]{:S(2)}, u32[]{:S(2)}) collective-permute-start(bf16[4,128,128]{2,1,0:T(8,128)(2,1)S(1)} %get-tuple-element.29), channel_id=1, source_target_pairs={{0,8},{1,9},{4,12},{9,1},{12,4},{13,5},{2,10},{3,11},{6,14},{11,3}... | collective-permute-start | bytes 393224 | tf_op jit(solution)/shard_map/ppermute | solution.py:597
  4.5 7.4 %collective-permute-start.2 = (bf16[4,128,128]{2,1,0:T(8,128)(2,1)S(1)}, bf16[4,128,128]{2,1,0:T(8,128)(2,1)S(1)}, u32[]{:S(2)}, u32[]{:S(2)}) collective-permute-start(bf16[4,128,128]{2,1,0:T(8,128)(2,1)S(1)} %get-tuple-element.30), channel_id=1, source_target_pairs={{0,14},{1,7},{4,10},{5,3},{8,6},{13,11},{2,12},{3,5},{6,8},{7,1},{... | collective-permute-start | bytes 393224 | tf_op jit(solution)/shard_map/ppermute | solution.py:597
  12.0 2.4 %collective-permute-start.3 = (bf16[4,128,128]{2,1,0:T(8,128)(2,1)S(1)}, bf16[4,128,128]{2,1,0:T(8,128)(2,1)S(1)}, u32[]{:S(2)}, u32[]{:S(2)}) collective-permute-start(bf16[4,128,128]{2,1,0:T(8,128)(2,1)S(1)} %get-tuple-element.31), channel_id=1, source_target_pairs={{0,6},{5,11},{8,14},{9,7},{12,10},{13,3},{2,4},{7,9},{10,12},{11,5... | collective-permute-start | bytes 393224 | tf_op jit(solution)/shard_map/ppermute | solution.py:597
  14.4 1.9 %collective-permute-start.4 = (bf16[4,128,128]{2,1,0:T(8,128)(2,1)S(1)}, bf16[4,128,128]{2,1,0:T(8,128)(2,1)S(1)}, u32[]{:S(2)}, u32[]{:S(2)}) collective-permute-start(bf16[4,128,128]{2,1,0:T(8,128)(2,1)S(1)} %get-tuple-element.32), channel_id=1, source_target_pairs={{0,12},{1,5},{4,8},{5,1},{8,4},{13,9},{2,14},{3,7},{6,10},{7,3},{1... | collective-permute-start | bytes 393224 | tf_op jit(solution)/shard_map/ppermute | solution.py:597
  16.3 0.0 collective-permute-done.refs_1_.refs_0_
  16.3 3.7 %collective-permute-start.5 = (bf16[4,128,128]{2,1,0:T(8,128)(2,1)S(1)}, bf16[4,128,128]{2,1,0:T(8,128)(2,1)S(1)}, u32[]{:S(2)}, u32[]{:S(2)}) collective-permute-start(bf16[4,128,128]{2,1,0:T(8,128)(2,1)S(1)} %get-tuple-element.34), channel_id=1, source_target_pairs={{0,4},{5,9},{8,12},{9,5},{12,8},{13,1},{2,6},{7,11},{10,14},{11,7}... | collective-permute-start | bytes 393224 | tf_op jit(solution)/shard_map/ppermute | solution.py:597
  20.1 0.0 collective-permute-done.1.refs_2_.refs_1_
  20.1 2.4 %collective-permute-start.6 = (bf16[4,128,128]{2,1,0:T(8,128)(2,1)S(1)}, bf16[4,128,128]{2,1,0:T(8,128)(2,1)S(1)}, u32[]{:S(2)}, u32[]{:S(2)}) collective-permute-start(bf16[4,128,128]{2,1,0:T(8,128)(2,1)S(1)} %get-tuple-element.35), channel_id=1, source_target_pairs={{1,3},{4,6},{5,7},{8,10},{9,11},{12,14},{3,1},{6,4},{7,5},{10,8},{... | collective-permute-start | bytes 393224 | tf_op jit(solution)/shard_map/ppermute | solution.py:597
  22.5 0.0 collective-permute-done.2.refs_3_.refs_2_
  22.5 0.0 collective-permute-done.3.refs_4_.refs_3_
  22.6 2.4 %collective-permute-done.4.refs_5_.refs_4_ = bf16[4,128,128]{2,1,0:T(8,128)(2,1)S(1)} collective-permute-done((bf16[4,128,128]{2,1,0:T(8,128)(2,1)S(1)}, bf16[4,128,128]{2,1,0:T(8,128)(2,1)S(1)}, u32[]{:S(2)}, u32[]{:S(2)}) %collective-permute-start.4) | collective-permute-done | bytes 131104 | tf_op jit(solution)/shard_map/ppermute | solution.py:597
  25.0 1.5 %begin.1 = (bf16[8,128,128]{2,1,0:T(8,128)(2,1)S(1)}, bf16[8,128,128]{2,1,0:T(8,128)(2,1)S(1)}, bf16[128,768]{1,0:T(8,128)(2,1)S(1)}, bf16[128,768]{1,0:T(8,128)...) custom-call(s32[2,4]{1,0:T(2,128)} %refs_0_.3, ...), custom_call_target="tpu_custom_call" | custom-call | flops 452984832 | bytes 786432 | tf_op jit(solution)/shard_map/begin/pallas_call | solution.py:629
  26.5 0.0 collective-permute-done.5.refs_6_
  26.5 0.4 collective-permute-done.6.refs_7_
  26.9 3.1 %finish.1 = (bf16[4,128,128]{2,1,0:T(8,128)(2,1)S(1)}, bf16[4,128,128]{2,1,0:T(8,128)(2,1)S(1)}, bf16[4,128,128]{2,1,0:T(8,128)(2,1)S(1)}, bf16[4,128,128]{2,1,0...) custom-call(bf16[4,128,128]{2,1,0:T(8,128)(2,1)S(1)} %collective-per, ...), custom_call_target="tpu_custom_call" | custom-call | flops 1426063360 | bytes 2097152 | tf_op jit(solution)/shard_map/finish/pallas_call | solution.py:643
  30.0 1.3 %collective-permute-start.7 = (bf16[4,128,128]{2,1,0:T(8,128)(2,1)S(1)}, bf16[4,128,128]{2,1,0:T(8,128)(2,1)S(1)}, u32[]{:S(2)}, u32[]{:S(2)}) collective-permute-start(bf16[4,128,128]{2,1,0:T(8,128)(2,1)S(1)} %get-tuple-element.44), channel_id=1, source_target_pairs={{10,0},{11,1},{14,4},{3,9},{6,12},{7,13},{8,2},{9,3},{12,6},{1,11}... | collective-permute-start | bytes 393224 | tf_op jit(solution)/shard_map/ppermute | solution.py:597
  31.3 1.3 %collective-permute-start.8 = (bf16[4,128,128]{2,1,0:T(8,128)(2,1)S(1)}, bf16[4,128,128]{2,1,0:T(8,128)(2,1)S(1)}, u32[]{:S(2)}, u32[]{:S(2)}) collective-permute-start(bf16[4,128,128]{2,1,0:T(8,128)(2,1)S(1)} %get-tuple-element.45), channel_id=1, source_target_pairs={{8,0},{9,1},{12,4},{1,9},{4,12},{5,13},{10,2},{11,3},{14,6},{3,11}... | collective-permute-start | bytes 393224 | tf_op jit(solution)/shard_map/ppermute | solution.py:597
  32.6 6.5 %collective-permute-start.9 = (bf16[4,128,128]{2,1,0:T(8,128)(2,1)S(1)}, bf16[4,128,128]{2,1,0:T(8,128)(2,1)S(1)}, u32[]{:S(2)}, u32[]{:S(2)}) collective-permute-start(bf16[4,128,128]{2,1,0:T(8,128)(2,1)S(1)} %get-tuple-element.46), channel_id=1, source_target_pairs={{14,0},{7,1},{10,4},{3,5},{6,8},{11,13},{12,2},{5,3},{8,6},{1,7},{... | collective-permute-start | bytes 393224 | tf_op jit(solution)/shard_map/ppermute | solution.py:597
  39.2 2.4 %collective-permute-start.10 = (bf16[4,128,128]{2,1,0:T(8,128)(2,1)S(1)}, bf16[4,128,128]{2,1,0:T(8,128)(2,1)S(1)}, u32[]{:S(2)}, u32[]{:S(2)}) collective-permute-start(bf16[4,128,128]{2,1,0:T(8,128)(2,1)S(1)} %get-tuple-element.47), channel_id=1, source_target_pairs={{6,0},{11,5},{14,8},{7,9},{10,12},{3,13},{4,2},{9,7},{12,10},{5,11... | collective-permute-start | bytes 393224 | tf_op jit(solution)/shard_map/ppermute | solution.py:597
  41.6 1.9 %collective-permute-start.11 = (bf16[4,128,128]{2,1,0:T(8,128)(2,1)S(1)}, bf16[4,128,128]{2,1,0:T(8,128)(2,1)S(1)}, u32[]{:S(2)}, u32[]{:S(2)}) collective-permute-start(bf16[4,128,128]{2,1,0:T(8,128)(2,1)S(1)} %get-tuple-element.48), channel_id=1, source_target_pairs={{12,0},{5,1},{8,4},{1,5},{4,8},{9,13},{14,2},{7,3},{10,6},{3,7},{6... | collective-permute-start | bytes 393224 | tf_op jit(solution)/shard_map/ppermute | solution.py:597
  43.5 0.0 collective-permute-done.7.refs_0_
  43.5 3.7 %collective-permute-start.12 = (bf16[4,128,128]{2,1,0:T(8,128)(2,1)S(1)}, bf16[4,128,128]{2,1,0:T(8,128)(2,1)S(1)}, u32[]{:S(2)}, u32[]{:S(2)}) collective-permute-start(bf16[4,128,128]{2,1,0:T(8,128)(2,1)S(1)} %get-tuple-element.49), channel_id=1, source_target_pairs={{4,0},{9,5},{12,8},{5,9},{8,12},{1,13},{6,2},{11,7},{14,10},{7,11}... | collective-permute-start | bytes 393224 | tf_op jit(solution)/shard_map/ppermute | solution.py:597
  47.3 0.0 collective-permute-done.8.refs_1_
  47.3 2.4 %collective-permute-start.13 = (bf16[4,128,128]{2,1,0:T(8,128)(2,1)S(1)}, bf16[4,128,128]{2,1,0:T(8,128)(2,1)S(1)}, u32[]{:S(2)}, u32[]{:S(2)}) collective-permute-start(bf16[4,128,128]{2,1,0:T(8,128)(2,1)S(1)} %get-tuple-element.50), channel_id=1, source_target_pairs={{3,1},{6,4},{7,5},{10,8},{11,9},{14,12},{1,3},{4,6},{5,7},{8,10},{... | collective-permute-start | bytes 393224 | tf_op jit(solution)/shard_map/ppermute | solution.py:597
  49.7 0.0 collective-permute-done.9.refs_2_
  49.8 0.0 collective-permute-done.10.refs_3_
  49.8 0.0 collective-permute-done.11.refs_4_
  49.8 0.6 %collective-permute-done.12.refs_5_ = bf16[4,128,128]{2,1,0:T(8,128)(2,1)S(1)} collective-permute-done((bf16[4,128,128]{2,1,0:T(8,128)(2,1)S(1)}, bf16[4,128,128]{2,1,0:T(8,128)(2,1)S(1)}, u32[]{:S(2)}, u32[]{:S(2)}) %collective-permute-start.12) | collective-permute-done | bytes 131104 | tf_op jit(solution)/shard_map/ppermute | solution.py:597
  50.4 3.7 %collective-permute-done.13.refs_6_ = bf16[4,128,128]{2,1,0:T(8,128)(2,1)S(1)} collective-permute-done((bf16[4,128,128]{2,1,0:T(8,128)(2,1)S(1)}, bf16[4,128,128]{2,1,0:T(8,128)(2,1)S(1)}, u32[]{:S(2)}, u32[]{:S(2)}) %collective-permute-start.13) | collective-permute-done | bytes 131104 | tf_op jit(solution)/shard_map/ppermute | solution.py:597
  54.2 0.9 %unpack.1 = (bf16[1,1,128,768]{3,2,1,0:T(8,128)(2,1)}, bf16[1,1,128,768]{3,2,1,0:T(8,128)(2,1)}, bf16[1,1,128,768]{3,2,1,0:T(8,128)(2,1)}, bf16[1,1,128,768]{3,2,1,0:T(8,128)(2,1)}) custom-call(bf16[4,128,128]{2,1,0:T(8,128)(2,1)S(1)} %collective-permute-done.7.refs_0_, bf16[4,128,128]{2,1,0:T(8,128)(2,1)S(1)} %collective-permute-done.8.refs_1_, ...), custom_call_target="tpu_custom_call" | custom-call | tf_op jit(solution)/shard_map/unpack/pallas_call | solution.py:666
Async XLA Ops:
  1.9 14.4 %collective-permute-start = (bf16[4,128,128]{2,1,0:T(8,128)(2,1)S(1)}, bf16[4,128,128]{2,1,0:T(8,128)(2,1)S(1)}, u32[]{:S(2)}, u32[]{:S(2)}) collective-permute-start(bf16[4,128,128]{2,1,0:T(8,128)(2,1)S(1)} %get-tuple-element.28), channel_id=1, source_target_pairs={{0,10},{1,11},{4,14},{9,3},{12,6},{13,7},{2,8},{3,9},{6,12},{11,1}... | collective-permute-start | bytes 393224 | tf_op jit(solution)/shard_map/ppermute | solution.py:597
  3.2 16.8 %collective-permute-start.1 = (bf16[4,128,128]{2,1,0:T(8,128)(2,1)S(1)}, bf16[4,128,128]{2,1,0:T(8,128)(2,1)S(1)}, u32[]{:S(2)}, u32[]{:S(2)}) collective-permute-start(bf16[4,128,128]{2,1,0:T(8,128)(2,1)S(1)} %get-tuple-element.29), channel_id=1, source_target_pairs={{0,8},{1,9},{4,12},{9,1},{12,4},{13,5},{2,10},{3,11},{6,14},{11,3}... | collective-permute-start | bytes 393224 | tf_op jit(solution)/shard_map/ppermute | solution.py:597
  4.5 18.0 %collective-permute-start.2 = (bf16[4,128,128]{2,1,0:T(8,128)(2,1)S(1)}, bf16[4,128,128]{2,1,0:T(8,128)(2,1)S(1)}, u32[]{:S(2)}, u32[]{:S(2)}) collective-permute-start(bf16[4,128,128]{2,1,0:T(8,128)(2,1)S(1)} %get-tuple-element.30), channel_id=1, source_target_pairs={{0,14},{1,7},{4,10},{5,3},{8,6},{13,11},{2,12},{3,5},{6,8},{7,1},{... | collective-permute-start | bytes 393224 | tf_op jit(solution)/shard_map/ppermute | solution.py:597
  12.0 10.6 %collective-permute-start.3 = (bf16[4,128,128]{2,1,0:T(8,128)(2,1)S(1)}, bf16[4,128,128]{2,1,0:T(8,128)(2,1)S(1)}, u32[]{:S(2)}, u32[]{:S(2)}) collective-permute-start(bf16[4,128,128]{2,1,0:T(8,128)(2,1)S(1)} %get-tuple-element.31), channel_id=1, source_target_pairs={{0,6},{5,11},{8,14},{9,7},{12,10},{13,3},{2,4},{7,9},{10,12},{11,5... | collective-permute-start | bytes 393224 | tf_op jit(solution)/shard_map/ppermute | solution.py:597
  14.4 10.6 %collective-permute-start.4 = (bf16[4,128,128]{2,1,0:T(8,128)(2,1)S(1)}, bf16[4,128,128]{2,1,0:T(8,128)(2,1)S(1)}, u32[]{:S(2)}, u32[]{:S(2)}) collective-permute-start(bf16[4,128,128]{2,1,0:T(8,128)(2,1)S(1)} %get-tuple-element.32), channel_id=1, source_target_pairs={{0,12},{1,5},{4,8},{5,1},{8,4},{13,9},{2,14},{3,7},{6,10},{7,3},{1... | collective-permute-start | bytes 393224 | tf_op jit(solution)/shard_map/ppermute | solution.py:597
  16.3 10.2 %collective-permute-start.5 = (bf16[4,128,128]{2,1,0:T(8,128)(2,1)S(1)}, bf16[4,128,128]{2,1,0:T(8,128)(2,1)S(1)}, u32[]{:S(2)}, u32[]{:S(2)}) collective-permute-start(bf16[4,128,128]{2,1,0:T(8,128)(2,1)S(1)} %get-tuple-element.34), channel_id=1, source_target_pairs={{0,4},{5,9},{8,12},{9,5},{12,8},{13,1},{2,6},{7,11},{10,14},{11,7}... | collective-permute-start | bytes 393224 | tf_op jit(solution)/shard_map/ppermute | solution.py:597
  20.1 6.9 %collective-permute-start.6 = (bf16[4,128,128]{2,1,0:T(8,128)(2,1)S(1)}, bf16[4,128,128]{2,1,0:T(8,128)(2,1)S(1)}, u32[]{:S(2)}, u32[]{:S(2)}) collective-permute-start(bf16[4,128,128]{2,1,0:T(8,128)(2,1)S(1)} %get-tuple-element.35), channel_id=1, source_target_pairs={{1,3},{4,6},{5,7},{8,10},{9,11},{12,14},{3,1},{6,4},{7,5},{10,8},{... | collective-permute-start | bytes 393224 | tf_op jit(solution)/shard_map/ppermute | solution.py:597
  30.0 13.5 %collective-permute-start.7 = (bf16[4,128,128]{2,1,0:T(8,128)(2,1)S(1)}, bf16[4,128,128]{2,1,0:T(8,128)(2,1)S(1)}, u32[]{:S(2)}, u32[]{:S(2)}) collective-permute-start(bf16[4,128,128]{2,1,0:T(8,128)(2,1)S(1)} %get-tuple-element.44), channel_id=1, source_target_pairs={{10,0},{11,1},{14,4},{3,9},{6,12},{7,13},{8,2},{9,3},{12,6},{1,11}... | collective-permute-start | bytes 393224 | tf_op jit(solution)/shard_map/ppermute | solution.py:597
  31.3 16.0 %collective-permute-start.8 = (bf16[4,128,128]{2,1,0:T(8,128)(2,1)S(1)}, bf16[4,128,128]{2,1,0:T(8,128)(2,1)S(1)}, u32[]{:S(2)}, u32[]{:S(2)}) collective-permute-start(bf16[4,128,128]{2,1,0:T(8,128)(2,1)S(1)} %get-tuple-element.45), channel_id=1, source_target_pairs={{8,0},{9,1},{12,4},{1,9},{4,12},{5,13},{10,2},{11,3},{14,6},{3,11}... | collective-permute-start | bytes 393224 | tf_op jit(solution)/shard_map/ppermute | solution.py:597
  32.6 17.1 %collective-permute-start.9 = (bf16[4,128,128]{2,1,0:T(8,128)(2,1)S(1)}, bf16[4,128,128]{2,1,0:T(8,128)(2,1)S(1)}, u32[]{:S(2)}, u32[]{:S(2)}) collective-permute-start(bf16[4,128,128]{2,1,0:T(8,128)(2,1)S(1)} %get-tuple-element.46), channel_id=1, source_target_pairs={{14,0},{7,1},{10,4},{3,5},{6,8},{11,13},{12,2},{5,3},{8,6},{1,7},{... | collective-permute-start | bytes 393224 | tf_op jit(solution)/shard_map/ppermute | solution.py:597
  39.2 10.6 %collective-permute-start.10 = (bf16[4,128,128]{2,1,0:T(8,128)(2,1)S(1)}, bf16[4,128,128]{2,1,0:T(8,128)(2,1)S(1)}, u32[]{:S(2)}, u32[]{:S(2)}) collective-permute-start(bf16[4,128,128]{2,1,0:T(8,128)(2,1)S(1)} %get-tuple-element.47), channel_id=1, source_target_pairs={{6,0},{11,5},{14,8},{7,9},{10,12},{3,13},{4,2},{9,7},{12,10},{5,11... | collective-permute-start | bytes 393224 | tf_op jit(solution)/shard_map/ppermute | solution.py:597
  41.6 8.2 %collective-permute-start.11 = (bf16[4,128,128]{2,1,0:T(8,128)(2,1)S(1)}, bf16[4,128,128]{2,1,0:T(8,128)(2,1)S(1)}, u32[]{:S(2)}, u32[]{:S(2)}) collective-permute-start(bf16[4,128,128]{2,1,0:T(8,128)(2,1)S(1)} %get-tuple-element.48), channel_id=1, source_target_pairs={{12,0},{5,1},{8,4},{1,5},{4,8},{9,13},{14,2},{7,3},{10,6},{3,7},{6... | collective-permute-start | bytes 393224 | tf_op jit(solution)/shard_map/ppermute | solution.py:597
  43.5 6.9 %collective-permute-start.12 = (bf16[4,128,128]{2,1,0:T(8,128)(2,1)S(1)}, bf16[4,128,128]{2,1,0:T(8,128)(2,1)S(1)}, u32[]{:S(2)}, u32[]{:S(2)}) collective-permute-start(bf16[4,128,128]{2,1,0:T(8,128)(2,1)S(1)} %get-tuple-element.49), channel_id=1, source_target_pairs={{4,0},{9,5},{12,8},{5,9},{8,12},{1,13},{6,2},{11,7},{14,10},{7,11}... | collective-permute-start | bytes 393224 | tf_op jit(solution)/shard_map/ppermute | solution.py:597
  47.3 6.9 %collective-permute-start.13 = (bf16[4,128,128]{2,1,0:T(8,128)(2,1)S(1)}, bf16[4,128,128]{2,1,0:T(8,128)(2,1)S(1)}, u32[]{:S(2)}, u32[]{:S(2)}) collective-permute-start(bf16[4,128,128]{2,1,0:T(8,128)(2,1)S(1)} %get-tuple-element.50), channel_id=1, source_target_pairs={{3,1},{6,4},{7,5},{10,8},{11,9},{14,12},{1,3},{4,6},{5,7},{8,10},{... | collective-permute-start | bytes 393224 | tf_op jit(solution)/shard_map/ppermute | solution.py:597

commit v6 on v5

--- a/solution.py
+++ b/solution.py
@@ -607,7 +607,7 @@
         out_specs=[in_vmem] * tiles,
         scratch_shapes=[
             pltpu.VMEM((4, tile_len, width), low),
-            pltpu.SemaphoreType.DMA((4, 4)),
+            pltpu.SemaphoreType.DMA((4, 8)),
         ],
         compiler_params=small,
         name="pack",

time: 55.6 us -> 55.7 us (level)
  no operation moved by 1% of the time
where the time goes in v6:
time: 55.7 us; the launch traced here: 55.2 us
  starting transfers between devices  40.1 us (72%)
  waiting for transfers between devices  7.24 us (13%)
  Pallas kernels  6.99 us (13%)
  between operations  0.84 us (2%)
    ppermute x14, starting transfers between devices, sent(): lax.ppermute(found[n], axes, routes(n, lat, lon, cores, heads, back))  40.1 us
    ppermute x14, waiting for transfers between devices, sent(): lax.ppermute(found[n], axes, routes(n, lat, lon, cores, heads, back))  7.24 us
    pallas_call x1, Pallas kernels, by_heads(): pl.pallas_call(functools.partial(finish_kernel, lat, lon, times), out_sha...  3.08 us
    pallas_call x1, Pallas kernels, by_heads(): pl.pallas_call(functools.partial(begin_kernel, lat, lon, times), out_shap...  1.54 us
    pallas_call x1, Pallas kernels, by_heads(): pl.pallas_call(functools.partial(pack_kernel, lat, lon, heads), out_shape...  1.42 us
  transfers between devices with their start and end apart: 14, of which 4 were waited for; matrix products, arithmetic and copies ran while one was open for 0% of the time, Pallas kernels for 3%

profile of v6, /device:TPU:20, one launch (start us, length us, event | category | flops | bytes accessed | tf_op | source)
XLA Modules:
  0.0 55.2 jit_solution(1729280715513437000)
XLA Ops:
  0.6 1.4 %pack.1 = (bf16[4,128,128]{2,1,0:T(8,128)(2,1)S(1)}, bf16[4,128,128]{2,1,0:T(8,128)(2,1)S(1)}, bf16[4,128,128]{2,1,0:T(8,128)(2,1)S(1)}, bf16[4,128,128]{2,1,0:T...) custom-call(bf16[1,1,128,768]{3,2,1,0:T(8,128)(2,1)} %refs_0_.2, ...), custom_call_target="tpu_custom_call" | custom-call | tf_op jit(solution)/shard_map/pack/pallas_call | solution.py:603
  2.1 1.3 %collective-permute-start = (bf16[4,128,128]{2,1,0:T(8,128)(2,1)S(1)}, bf16[4,128,128]{2,1,0:T(8,128)(2,1)S(1)}, u32[]{:S(2)}, u32[]{:S(2)}) collective-permute-start(bf16[4,128,128]{2,1,0:T(8,128)(2,1)S(1)} %get-tuple-element.28), channel_id=1, source_target_pairs={{0,10},{1,11},{4,14},{9,3},{12,6},{13,7},{2,8},{3,9},{6,12},{11,1}... | collective-permute-start | bytes 393224 | tf_op jit(solution)/shard_map/ppermute | solution.py:597
  3.4 1.3 %collective-permute-start.1 = (bf16[4,128,128]{2,1,0:T(8,128)(2,1)S(1)}, bf16[4,128,128]{2,1,0:T(8,128)(2,1)S(1)}, u32[]{:S(2)}, u32[]{:S(2)}) collective-permute-start(bf16[4,128,128]{2,1,0:T(8,128)(2,1)S(1)} %get-tuple-element.29), channel_id=1, source_target_pairs={{0,8},{1,9},{4,12},{9,1},{12,4},{13,5},{2,10},{3,11},{6,14},{11,3}... | collective-permute-start | bytes 393224 | tf_op jit(solution)/shard_map/ppermute | solution.py:597
  4.7 7.4 %collective-permute-start.2 = (bf16[4,128,128]{2,1,0:T(8,128)(2,1)S(1)}, bf16[4,128,128]{2,1,0:T(8,128)(2,1)S(1)}, u32[]{:S(2)}, u32[]{:S(2)}) collective-permute-start(bf16[4,128,128]{2,1,0:T(8,128)(2,1)S(1)} %get-tuple-element.30), channel_id=1, source_target_pairs={{0,14},{1,7},{4,10},{5,3},{8,6},{13,11},{2,12},{3,5},{6,8},{7,1},{... | collective-permute-start | bytes 393224 | tf_op jit(solution)/shard_map/ppermute | solution.py:597
  12.1 2.4 %collective-permute-start.3 = (bf16[4,128,128]{2,1,0:T(8,128)(2,1)S(1)}, bf16[4,128,128]{2,1,0:T(8,128)(2,1)S(1)}, u32[]{:S(2)}, u32[]{:S(2)}) collective-permute-start(bf16[4,128,128]{2,1,0:T(8,128)(2,1)S(1)} %get-tuple-element.31), channel_id=1, source_target_pairs={{0,6},{5,11},{8,14},{9,7},{12,10},{13,3},{2,4},{7,9},{10,12},{11,5... | collective-permute-start | bytes 393224 | tf_op jit(solution)/shard_map/ppermute | solution.py:597
  14.5 1.9 %collective-permute-start.4 = (bf16[4,128,128]{2,1,0:T(8,128)(2,1)S(1)}, bf16[4,128,128]{2,1,0:T(8,128)(2,1)S(1)}, u32[]{:S(2)}, u32[]{:S(2)}) collective-permute-start(bf16[4,128,128]{2,1,0:T(8,128)(2,1)S(1)} %get-tuple-element.32), channel_id=1, source_target_pairs={{0,12},{1,5},{4,8},{5,1},{8,4},{13,9},{2,14},{3,7},{6,10},{7,3},{1... | collective-permute-start | bytes 393224 | tf_op jit(solution)/shard_map/ppermute | solution.py:597
  16.4 0.0 collective-permute-done.refs_1_.refs_0_
  16.4 3.7 %collective-permute-start.5 = (bf16[4,128,128]{2,1,0:T(8,128)(2,1)S(1)}, bf16[4,128,128]{2,1,0:T(8,128)(2,1)S(1)}, u32[]{:S(2)}, u32[]{:S(2)}) collective-permute-start(bf16[4,128,128]{2,1,0:T(8,128)(2,1)S(1)} %get-tuple-element.34), channel_id=1, source_target_pairs={{0,4},{5,9},{8,12},{9,5},{12,8},{13,1},{2,6},{7,11},{10,14},{11,7}... | collective-permute-start | bytes 393224 | tf_op jit(solution)/shard_map/ppermute | solution.py:597
  20.2 0.0 collective-permute-done.1.refs_2_.refs_1_
  20.2 2.4 %collective-permute-start.6 = (bf16[4,128,128]{2,1,0:T(8,128)(2,1)S(1)}, bf16[4,128,128]{2,1,0:T(8,128)(2,1)S(1)}, u32[]{:S(2)}, u32[]{:S(2)}) collective-permute-start(bf16[4,128,128]{2,1,0:T(8,128)(2,1)S(1)} %get-tuple-element.35), channel_id=1, source_target_pairs={{1,3},{4,6},{5,7},{8,10},{9,11},{12,14},{3,1},{6,4},{7,5},{10,8},{... | collective-permute-start | bytes 393224 | tf_op jit(solution)/shard_map/ppermute | solution.py:597
  22.7 0.0 collective-permute-done.2.refs_3_.refs_2_
  22.7 0.0 collective-permute-done.3.refs_4_.refs_3_
  22.7 2.4 %collective-permute-done.4.refs_5_.refs_4_ = bf16[4,128,128]{2,1,0:T(8,128)(2,1)S(1)} collective-permute-done((bf16[4,128,128]{2,1,0:T(8,128)(2,1)S(1)}, bf16[4,128,128]{2,1,0:T(8,128)(2,1)S(1)}, u32[]{:S(2)}, u32[]{:S(2)}) %collective-permute-start.4) | collective-permute-done | bytes 131104 | tf_op jit(solution)/shard_map/ppermute | solution.py:597
  25.1 1.5 %begin.1 = (bf16[8,128,128]{2,1,0:T(8,128)(2,1)S(1)}, bf16[8,128,128]{2,1,0:T(8,128)(2,1)S(1)}, bf16[128,768]{1,0:T(8,128)(2,1)S(1)}, bf16[128,768]{1,0:T(8,128)...) custom-call(s32[2,4]{1,0:T(2,128)} %refs_0_.3, ...), custom_call_target="tpu_custom_call" | custom-call | flops 452984832 | bytes 786432 | tf_op jit(solution)/shard_map/begin/pallas_call | solution.py:629
  26.6 0.0 collective-permute-done.5.refs_6_
  26.6 0.5 collective-permute-done.6.refs_7_
  27.1 3.1 %finish.1 = (bf16[4,128,128]{2,1,0:T(8,128)(2,1)S(1)}, bf16[4,128,128]{2,1,0:T(8,128)(2,1)S(1)}, bf16[4,128,128]{2,1,0:T(8,128)(2,1)S(1)}, bf16[4,128,128]{2,1,0...) custom-call(bf16[4,128,128]{2,1,0:T(8,128)(2,1)S(1)} %collective-per, ...), custom_call_target="tpu_custom_call" | custom-call | flops 1426063360 | bytes 2097152 | tf_op jit(solution)/shard_map/finish/pallas_call | solution.py:643
  30.1 1.3 %collective-permute-start.7 = (bf16[4,128,128]{2,1,0:T(8,128)(2,1)S(1)}, bf16[4,128,128]{2,1,0:T(8,128)(2,1)S(1)}, u32[]{:S(2)}, u32[]{:S(2)}) collective-permute-start(bf16[4,128,128]{2,1,0:T(8,128)(2,1)S(1)} %get-tuple-element.44), channel_id=1, source_target_pairs={{10,0},{11,1},{14,4},{3,9},{6,12},{7,13},{8,2},{9,3},{12,6},{1,11}... | collective-permute-start | bytes 393224 | tf_op jit(solution)/shard_map/ppermute | solution.py:597
  31.5 1.3 %collective-permute-start.8 = (bf16[4,128,128]{2,1,0:T(8,128)(2,1)S(1)}, bf16[4,128,128]{2,1,0:T(8,128)(2,1)S(1)}, u32[]{:S(2)}, u32[]{:S(2)}) collective-permute-start(bf16[4,128,128]{2,1,0:T(8,128)(2,1)S(1)} %get-tuple-element.45), channel_id=1, source_target_pairs={{8,0},{9,1},{12,4},{1,9},{4,12},{5,13},{10,2},{11,3},{14,6},{3,11}... | collective-permute-start | bytes 393224 | tf_op jit(solution)/shard_map/ppermute | solution.py:597
  32.8 6.5 %collective-permute-start.9 = (bf16[4,128,128]{2,1,0:T(8,128)(2,1)S(1)}, bf16[4,128,128]{2,1,0:T(8,128)(2,1)S(1)}, u32[]{:S(2)}, u32[]{:S(2)}) collective-permute-start(bf16[4,128,128]{2,1,0:T(8,128)(2,1)S(1)} %get-tuple-element.46), channel_id=1, source_target_pairs={{14,0},{7,1},{10,4},{3,5},{6,8},{11,13},{12,2},{5,3},{8,6},{1,7},{... | collective-permute-start | bytes 393224 | tf_op jit(solution)/shard_map/ppermute | solution.py:597
  39.3 2.4 %collective-permute-start.10 = (bf16[4,128,128]{2,1,0:T(8,128)(2,1)S(1)}, bf16[4,128,128]{2,1,0:T(8,128)(2,1)S(1)}, u32[]{:S(2)}, u32[]{:S(2)}) collective-permute-start(bf16[4,128,128]{2,1,0:T(8,128)(2,1)S(1)} %get-tuple-element.47), channel_id=1, source_target_pairs={{6,0},{11,5},{14,8},{7,9},{10,12},{3,13},{4,2},{9,7},{12,10},{5,11... | collective-permute-start | bytes 393224 | tf_op jit(solution)/shard_map/ppermute | solution.py:597
  41.7 1.9 %collective-permute-start.11 = (bf16[4,128,128]{2,1,0:T(8,128)(2,1)S(1)}, bf16[4,128,128]{2,1,0:T(8,128)(2,1)S(1)}, u32[]{:S(2)}, u32[]{:S(2)}) collective-permute-start(bf16[4,128,128]{2,1,0:T(8,128)(2,1)S(1)} %get-tuple-element.48), channel_id=1, source_target_pairs={{12,0},{5,1},{8,4},{1,5},{4,8},{9,13},{14,2},{7,3},{10,6},{3,7},{6... | collective-permute-start | bytes 393224 | tf_op jit(solution)/shard_map/ppermute | solution.py:597
  43.6 0.0 collective-permute-done.7.refs_0_
  43.7 3.7 %collective-permute-start.12 = (bf16[4,128,128]{2,1,0:T(8,128)(2,1)S(1)}, bf16[4,128,128]{2,1,0:T(8,128)(2,1)S(1)}, u32[]{:S(2)}, u32[]{:S(2)}) collective-permute-start(bf16[4,128,128]{2,1,0:T(8,128)(2,1)S(1)} %get-tuple-element.49), channel_id=1, source_target_pairs={{4,0},{9,5},{12,8},{5,9},{8,12},{1,13},{6,2},{11,7},{14,10},{7,11}... | collective-permute-start | bytes 393224 | tf_op jit(solution)/shard_map/ppermute | solution.py:597
  47.4 0.0 collective-permute-done.8.refs_1_
  47.4 2.4 %collective-permute-start.13 = (bf16[4,128,128]{2,1,0:T(8,128)(2,1)S(1)}, bf16[4,128,128]{2,1,0:T(8,128)(2,1)S(1)}, u32[]{:S(2)}, u32[]{:S(2)}) collective-permute-start(bf16[4,128,128]{2,1,0:T(8,128)(2,1)S(1)} %get-tuple-element.50), channel_id=1, source_target_pairs={{3,1},{6,4},{7,5},{10,8},{11,9},{14,12},{1,3},{4,6},{5,7},{8,10},{... | collective-permute-start | bytes 393224 | tf_op jit(solution)/shard_map/ppermute | solution.py:597
  49.8 0.0 collective-permute-done.9.refs_2_
  49.9 0.0 collective-permute-done.10.refs_3_
  49.9 0.0 collective-permute-done.11.refs_4_
  49.9 0.6 %collective-permute-done.12.refs_5_ = bf16[4,128,128]{2,1,0:T(8,128)(2,1)S(1)} collective-permute-done((bf16[4,128,128]{2,1,0:T(8,128)(2,1)S(1)}, bf16[4,128,128]{2,1,0:T(8,128)(2,1)S(1)}, u32[]{:S(2)}, u32[]{:S(2)}) %collective-permute-start.12) | collective-permute-done | bytes 131104 | tf_op jit(solution)/shard_map/ppermute | solution.py:597
  50.5 3.7 %collective-permute-done.13.refs_6_ = bf16[4,128,128]{2,1,0:T(8,128)(2,1)S(1)} collective-permute-done((bf16[4,128,128]{2,1,0:T(8,128)(2,1)S(1)}, bf16[4,128,128]{2,1,0:T(8,128)(2,1)S(1)}, u32[]{:S(2)}, u32[]{:S(2)}) %collective-permute-start.13) | collective-permute-done | bytes 131104 | tf_op jit(solution)/shard_map/ppermute | solution.py:597
  54.3 0.9 %unpack.1 = (bf16[1,1,128,768]{3,2,1,0:T(8,128)(2,1)}, bf16[1,1,128,768]{3,2,1,0:T(8,128)(2,1)}, bf16[1,1,128,768]{3,2,1,0:T(8,128)(2,1)}, bf16[1,1,128,768]{3,2,1,0:T(8,128)(2,1)}) custom-call(bf16[4,128,128]{2,1,0:T(8,128)(2,1)S(1)} %collective-permute-done.7.refs_0_, bf16[4,128,128]{2,1,0:T(8,128)(2,1)S(1)} %collective-permute-done.8.refs_1_, ...), custom_call_target="tpu_custom_call" | custom-call | tf_op jit(solution)/shard_map/unpack/pallas_call | solution.py:666
Async XLA Ops:
  2.1 14.4 %collective-permute-start = (bf16[4,128,128]{2,1,0:T(8,128)(2,1)S(1)}, bf16[4,128,128]{2,1,0:T(8,128)(2,1)S(1)}, u32[]{:S(2)}, u32[]{:S(2)}) collective-permute-start(bf16[4,128,128]{2,1,0:T(8,128)(2,1)S(1)} %get-tuple-element.28), channel_id=1, source_target_pairs={{0,10},{1,11},{4,14},{9,3},{12,6},{13,7},{2,8},{3,9},{6,12},{11,1}... | collective-permute-start | bytes 393224 | tf_op jit(solution)/shard_map/ppermute | solution.py:597
  3.4 16.8 %collective-permute-start.1 = (bf16[4,128,128]{2,1,0:T(8,128)(2,1)S(1)}, bf16[4,128,128]{2,1,0:T(8,128)(2,1)S(1)}, u32[]{:S(2)}, u32[]{:S(2)}) collective-permute-start(bf16[4,128,128]{2,1,0:T(8,128)(2,1)S(1)} %get-tuple-element.29), channel_id=1, source_target_pairs={{0,8},{1,9},{4,12},{9,1},{12,4},{13,5},{2,10},{3,11},{6,14},{11,3}... | collective-permute-start | bytes 393224 | tf_op jit(solution)/shard_map/ppermute | solution.py:597
  4.7 18.0 %collective-permute-start.2 = (bf16[4,128,128]{2,1,0:T(8,128)(2,1)S(1)}, bf16[4,128,128]{2,1,0:T(8,128)(2,1)S(1)}, u32[]{:S(2)}, u32[]{:S(2)}) collective-permute-start(bf16[4,128,128]{2,1,0:T(8,128)(2,1)S(1)} %get-tuple-element.30), channel_id=1, source_target_pairs={{0,14},{1,7},{4,10},{5,3},{8,6},{13,11},{2,12},{3,5},{6,8},{7,1},{... | collective-permute-start | bytes 393224 | tf_op jit(solution)/shard_map/ppermute | solution.py:597
  12.1 10.6 %collective-permute-start.3 = (bf16[4,128,128]{2,1,0:T(8,128)(2,1)S(1)}, bf16[4,128,128]{2,1,0:T(8,128)(2,1)S(1)}, u32[]{:S(2)}, u32[]{:S(2)}) collective-permute-start(bf16[4,128,128]{2,1,0:T(8,128)(2,1)S(1)} %get-tuple-element.31), channel_id=1, source_target_pairs={{0,6},{5,11},{8,14},{9,7},{12,10},{13,3},{2,4},{7,9},{10,12},{11,5... | collective-permute-start | bytes 393224 | tf_op jit(solution)/shard_map/ppermute | solution.py:597
  14.5 10.6 %collective-permute-start.4 = (bf16[4,128,128]{2,1,0:T(8,128)(2,1)S(1)}, bf16[4,128,128]{2,1,0:T(8,128)(2,1)S(1)}, u32[]{:S(2)}, u32[]{:S(2)}) collective-permute-start(bf16[4,128,128]{2,1,0:T(8,128)(2,1)S(1)} %get-tuple-element.32), channel_id=1, source_target_pairs={{0,12},{1,5},{4,8},{5,1},{8,4},{13,9},{2,14},{3,7},{6,10},{7,3},{1... | collective-permute-start | bytes 393224 | tf_op jit(solution)/shard_map/ppermute | solution.py:597
  16.4 10.2 %collective-permute-start.5 = (bf16[4,128,128]{2,1,0:T(8,128)(2,1)S(1)}, bf16[4,128,128]{2,1,0:T(8,128)(2,1)S(1)}, u32[]{:S(2)}, u32[]{:S(2)}) collective-permute-start(bf16[4,128,128]{2,1,0:T(8,128)(2,1)S(1)} %get-tuple-element.34), channel_id=1, source_target_pairs={{0,4},{5,9},{8,12},{9,5},{12,8},{13,1},{2,6},{7,11},{10,14},{11,7}... | collective-permute-start | bytes 393224 | tf_op jit(solution)/shard_map/ppermute | solution.py:597
  20.2 6.9 %collective-permute-start.6 = (bf16[4,128,128]{2,1,0:T(8,128)(2,1)S(1)}, bf16[4,128,128]{2,1,0:T(8,128)(2,1)S(1)}, u32[]{:S(2)}, u32[]{:S(2)}) collective-permute-start(bf16[4,128,128]{2,1,0:T(8,128)(2,1)S(1)} %get-tuple-element.35), channel_id=1, source_target_pairs={{1,3},{4,6},{5,7},{8,10},{9,11},{12,14},{3,1},{6,4},{7,5},{10,8},{... | collective-permute-start | bytes 393224 | tf_op jit(solution)/shard_map/ppermute | solution.py:597
  30.1 13.5 %collective-permute-start.7 = (bf16[4,128,128]{2,1,0:T(8,128)(2,1)S(1)}, bf16[4,128,128]{2,1,0:T(8,128)(2,1)S(1)}, u32[]{:S(2)}, u32[]{:S(2)}) collective-permute-start(bf16[4,128,128]{2,1,0:T(8,128)(2,1)S(1)} %get-tuple-element.44), channel_id=1, source_target_pairs={{10,0},{11,1},{14,4},{3,9},{6,12},{7,13},{8,2},{9,3},{12,6},{1,11}... | collective-permute-start | bytes 393224 | tf_op jit(solution)/shard_map/ppermute | solution.py:597
  31.5 15.9 %collective-permute-start.8 = (bf16[4,128,128]{2,1,0:T(8,128)(2,1)S(1)}, bf16[4,128,128]{2,1,0:T(8,128)(2,1)S(1)}, u32[]{:S(2)}, u32[]{:S(2)}) collective-permute-start(bf16[4,128,128]{2,1,0:T(8,128)(2,1)S(1)} %get-tuple-element.45), channel_id=1, source_target_pairs={{8,0},{9,1},{12,4},{1,9},{4,12},{5,13},{10,2},{11,3},{14,6},{3,11}... | collective-permute-start | bytes 393224 | tf_op jit(solution)/shard_map/ppermute | solution.py:597
  32.8 17.1 %collective-permute-start.9 = (bf16[4,128,128]{2,1,0:T(8,128)(2,1)S(1)}, bf16[4,128,128]{2,1,0:T(8,128)(2,1)S(1)}, u32[]{:S(2)}, u32[]{:S(2)}) collective-permute-start(bf16[4,128,128]{2,1,0:T(8,128)(2,1)S(1)} %get-tuple-element.46), channel_id=1, source_target_pairs={{14,0},{7,1},{10,4},{3,5},{6,8},{11,13},{12,2},{5,3},{8,6},{1,7},{... | collective-permute-start | bytes 393224 | tf_op jit(solution)/shard_map/ppermute | solution.py:597
  39.3 10.6 %collective-permute-start.10 = (bf16[4,128,128]{2,1,0:T(8,128)(2,1)S(1)}, bf16[4,128,128]{2,1,0:T(8,128)(2,1)S(1)}, u32[]{:S(2)}, u32[]{:S(2)}) collective-permute-start(bf16[4,128,128]{2,1,0:T(8,128)(2,1)S(1)} %get-tuple-element.47), channel_id=1, source_target_pairs={{6,0},{11,5},{14,8},{7,9},{10,12},{3,13},{4,2},{9,7},{12,10},{5,11... | collective-permute-start | bytes 393224 | tf_op jit(solution)/shard_map/ppermute | solution.py:597
  41.7 8.2 %collective-permute-start.11 = (bf16[4,128,128]{2,1,0:T(8,128)(2,1)S(1)}, bf16[4,128,128]{2,1,0:T(8,128)(2,1)S(1)}, u32[]{:S(2)}, u32[]{:S(2)}) collective-permute-start(bf16[4,128,128]{2,1,0:T(8,128)(2,1)S(1)} %get-tuple-element.48), channel_id=1, source_target_pairs={{12,0},{5,1},{8,4},{1,5},{4,8},{9,13},{14,2},{7,3},{10,6},{3,7},{6... | collective-permute-start | bytes 393224 | tf_op jit(solution)/shard_map/ppermute | solution.py:597
  43.7 6.9 %collective-permute-start.12 = (bf16[4,128,128]{2,1,0:T(8,128)(2,1)S(1)}, bf16[4,128,128]{2,1,0:T(8,128)(2,1)S(1)}, u32[]{:S(2)}, u32[]{:S(2)}) collective-permute-start(bf16[4,128,128]{2,1,0:T(8,128)(2,1)S(1)} %get-tuple-element.49), channel_id=1, source_target_pairs={{4,0},{9,5},{12,8},{5,9},{8,12},{1,13},{6,2},{11,7},{14,10},{7,11}... | collective-permute-start | bytes 393224 | tf_op jit(solution)/shard_map/ppermute | solution.py:597
  47.4 6.9 %collective-permute-start.13 = (bf16[4,128,128]{2,1,0:T(8,128)(2,1)S(1)}, bf16[4,128,128]{2,1,0:T(8,128)(2,1)S(1)}, u32[]{:S(2)}, u32[]{:S(2)}) collective-permute-start(bf16[4,128,128]{2,1,0:T(8,128)(2,1)S(1)} %get-tuple-element.50), channel_id=1, source_target_pairs={{3,1},{6,4},{7,5},{10,8},{11,9},{14,12},{1,3},{4,6},{5,7},{8,10},{... | collective-permute-start | bytes 393224 | tf_op jit(solution)/shard_map/ppermute | solution.py:597
